TPU v7x, 512 devices: a whole 4x8x8 slice. The times are simulated.
512 devices in a mesh: dp: 32 (over y, x), expert: 16 (over z, core).
Axes of the slice: x: 4, y: 8, z: 8, core: 2. Of those that a mesh axis runs over, the one named last changes fastest.
Arguments:
- tokens: bfloat16 [65536, 1024], P(('dp', 'expert')), may hold values from -6 to 6
- grad_out: bfloat16 [65536, 1024], P(('dp', 'expert')), may hold values from -24 to 24
- route_ids: int32 [65536, 6], P(('dp', 'expert')), may hold values from 0 to 15, as said below
- route_slots: int32 [65536, 6], P(('dp', 'expert')), may hold values from 0 to 48, as said below
- route_probs: float32 [65536, 6], P(('dp', 'expert')), may hold values from 0.05 to 1
- w_gate: bfloat16 [16, 1024, 704], P('expert'), may hold values from -0.1875 to 0.1875
- w_up: bfloat16 [16, 1024, 704], P('expert'), may hold values from -0.1875 to 0.1875
- w_down: bfloat16 [16, 704, 1024], P('expert'), may hold values from -0.21875 to 0.21875
Outputs:
- grad_tokens: bfloat16 [65536, 1024], P(('dp', 'expert'))
- grad_down: float32 [16, 704, 1024], P('expert', None, 'dp')
Inputs may be any that keep to these rules, and one draw needn't show every extreme that they name: `route_ids`: the 6 experts of a token are distinct. Among the routes of one device's 128 tokens, taken in token order and then route order, route_slots counts the earlier routes to the same expert; the value 48 marks a route dropped because that expert's 48 slots for this device are full, and kept routes to one expert from one device have distinct slots; in every device's tokens some expert is over its capacity.
All inputs are finite; a program needn't handle non-finite values.
Results may differ from a plain program's by a relative error of at most 0.024.
Values may be sent and summed in bfloat16 or wider, within the bound.
No kernel may reach another device: no remote copies, remote signals or barrier semaphores. Data moves between devices by JAX's collectives and lax.ppermute only.
A program may use at most 64 MiB of HBM per device.

v0:
```python
import jax
import jax.numpy as jnp
from jax import lax
from jax.sharding import PartitionSpec as P


def on_device(tokens, grad_out, route_ids, route_slots, route_probs, w_gate, w_up, w_down):
    tok_rows, features = tokens.shape
    routes = route_ids.shape[1]
    local_experts = w_gate.shape[0]
    groups = lax.axis_size("expert")
    experts_all = local_experts * groups
    capacity = tok_rows * routes // experts_all
    slots_all = experts_all * capacity
    target = jnp.where(route_slots < capacity, route_ids * capacity + route_slots, slots_all)
    rows_in = jnp.zeros((slots_all, features), jnp.bfloat16)
    rows_grad = jnp.zeros((slots_all, features), jnp.bfloat16)
    weights_in = jnp.zeros((slots_all,), jnp.float32)
    for route_index in range(routes):
        rows_in = rows_in.at[target[:, route_index]].set(tokens, mode="drop")
        rows_grad = rows_grad.at[target[:, route_index]].set(grad_out, mode="drop")
        weights_in = weights_in.at[target[:, route_index]].set(
            route_probs[:, route_index], mode="drop"
        )
    rows_in = rows_in.reshape(groups, local_experts, capacity, features)
    rows_grad = rows_grad.reshape(groups, local_experts, capacity, features)
    weights_in = weights_in.reshape(groups, local_experts, capacity)
    inputs_here = lax.all_to_all(rows_in, "expert", split_axis=0, concat_axis=0, tiled=True)
    grads_here = lax.all_to_all(rows_grad, "expert", split_axis=0, concat_axis=0, tiled=True)
    probs_here = lax.all_to_all(
        weights_in.astype(jnp.bfloat16), "expert", split_axis=0, concat_axis=0, tiled=True
    ).astype(weights_in.dtype)
    gate_pre = jnp.einsum("secd,edf->secf", inputs_here, w_gate, preferred_element_type=jnp.float32)
    up_pre = jnp.einsum("secd,edf->secf", inputs_here, w_up, preferred_element_type=jnp.float32)
    gate_sig = jax.nn.sigmoid(gate_pre)
    activated = gate_pre * gate_sig
    expert_hidden = (activated * up_pre).astype(jnp.bfloat16)
    expert_scaled = (probs_here[..., None] * grads_here.astype(jnp.float32)).astype(jnp.bfloat16)
    grad_hidden = jnp.einsum(
        "secd,efd->secf", expert_scaled, w_down, preferred_element_type=jnp.float32
    )
    grad_gate = (grad_hidden * up_pre * gate_sig * (1.0 + gate_pre * (1.0 - gate_sig))).astype(
        jnp.bfloat16
    )
    grad_up = (grad_hidden * activated).astype(jnp.bfloat16)
    back_rows = (
        jnp.einsum("secf,edf->secd", grad_gate, w_gate, preferred_element_type=jnp.float32)
        + jnp.einsum("secf,edf->secd", grad_up, w_up, preferred_element_type=jnp.float32)
    ).astype(jnp.bfloat16)
    back_rows, hidden, scaled = (back_rows, expert_hidden, expert_scaled)
    came_back = lax.all_to_all(back_rows, "expert", split_axis=0, concat_axis=0, tiled=True)
    back_flat = came_back.reshape(slots_all, features)
    summed = jnp.zeros((tok_rows, features), jnp.float32)
    for route_index in range(routes):
        picked = jnp.take(back_flat, target[:, route_index], axis=0, mode="fill", fill_value=0)
        summed = summed + picked.astype(jnp.float32)
    grad_tokens = summed.astype(jnp.bfloat16)
    mine = lax.psum_scatter(
        jnp.einsum("secd,secf->def", scaled, hidden, preferred_element_type=jnp.float32).astype(
            jnp.bfloat16
        ),
        "dp",
        scatter_dimension=0,
        tiled=True,
    ).astype(jnp.float32)
    grad_down = jnp.transpose(mine, (1, 2, 0))
    return (grad_tokens, grad_down)


def solution(mesh):
    in_specs = (
        P(("dp", "expert"), None),
        P(("dp", "expert"), None),
        P(("dp", "expert"), None),
        P(("dp", "expert"), None),
        P(("dp", "expert"), None),
        P("expert", None, None),
        P("expert", None, None),
        P("expert", None, None),
    )
    out_specs = (P(("dp", "expert"), None), P("expert", None, "dp"))
    return jax.shard_map(
        on_device, mesh=mesh, in_specs=in_specs, out_specs=out_specs, check_vma=False
    )
```

profile of v0, /device:TPU:6, one launch (start us, length us, event | category | flops | bytes accessed | tf_op | source)
XLA Modules:
  0.0 350.7 jit_solution(1303297552065031218)
XLA Ops:
  15.5 10.4 %all-to-all-start = ((bf16[16,1,48]{2,1,0:T(2,128)(2,1)}), bf16[16,1,48]{2,1,0:T(2,128)(2,1)S(1)}, u32[]{:S(2)}, u32[]{:S(2)}) async-start(bf16[16,1,48]{2,1,0:T(2,128)(2,1)} %convert_element_type.94), calls=%async_computation | async-start | bytes 16384 | tf_op jit(solution)/shard_map/all_to_all | solution.py:30
  25.9 2.5 scatter_custom_fusion.12
  28.4 3.9 %scatter_fusion.10 = bf16[768,1024]{1,0:T(8,128)(2,1)} fusion(bf16[768,1024]{1,0:T(8,128)(2,1)} %scatter_custom_fusion.12, s32[128]{0:T(128)S(1)} %get-tuple-element.41, bf16[128,1024]{1,0:T(8,128)(2,1)S(1)} %copy-done.1), kind=kCustom, calls=%fused_computation.19 | custom fusion | bytes 786944 | tf_op jit(solution)/shard_map/scatter | solution.py:20
  32.3 3.9 %scatter_fusion.11 = bf16[768,1024]{1,0:T(8,128)(2,1)} fusion(bf16[768,1024]{1,0:T(8,128)(2,1)} %scatter_fusion.10, s32[128]{0:T(128)S(1)} %get-tuple-element.42, bf16[128,1024]{1,0:T(8,128)(2,1)S(1)} %copy-done.1), kind=kCustom, calls=%fused_computation.20 | custom fusion | bytes 786944 | tf_op jit(solution)/shard_map/scatter | solution.py:20
  36.2 3.9 %scatter_fusion.12 = bf16[768,1024]{1,0:T(8,128)(2,1)} fusion(bf16[768,1024]{1,0:T(8,128)(2,1)} %scatter_fusion.11, s32[128]{0:T(128)S(1)} %get-tuple-element.43, bf16[128,1024]{1,0:T(8,128)(2,1)S(1)} %copy-done.1), kind=kCustom, calls=%fused_computation.21 | custom fusion | bytes 786944 | tf_op jit(solution)/shard_map/scatter | solution.py:20
  40.1 3.9 %scatter_fusion.13 = bf16[768,1024]{1,0:T(8,128)(2,1)} fusion(bf16[768,1024]{1,0:T(8,128)(2,1)} %scatter_fusion.12, s32[128]{0:T(128)S(1)} %get-tuple-element.44, bf16[128,1024]{1,0:T(8,128)(2,1)S(1)} %copy-done.1), kind=kCustom, calls=%fused_computation.22 | custom fusion | bytes 786944 | tf_op jit(solution)/shard_map/scatter | solution.py:20
  44.0 3.9 %scatter_fusion.14 = bf16[768,1024]{1,0:T(8,128)(2,1)} fusion(bf16[768,1024]{1,0:T(8,128)(2,1)} %scatter_fusion.13, s32[128]{0:T(128)S(1)} %get-tuple-element.39, bf16[128,1024]{1,0:T(8,128)(2,1)S(1)} %copy-done.1), kind=kCustom, calls=%fused_computation.23 | custom fusion | bytes 786944 | tf_op jit(solution)/shard_map/scatter | solution.py:20
  48.0 7.4 %all-to-all-start.2 = ((bf16[16,1,48,1024]{3,2,1,0:T(8,128)(2,1)}), bf16[16,1,48,1024]{3,2,1,0:T(8,128)(2,1)S(1)}, u32[]{:S(2)}, u32[]{:S(2)}) async-start(bf16[16,1,48,1024]{3,2,1,0:T(8,128)(2,1)} %bitcast.23), calls=%async_computation.2 | async-start | bytes 3145728 | tf_op jit(solution)/shard_map/all_to_all | solution.py:28
  57.8 3.9 %scatter_fusion.5 = bf16[768,1024]{1,0:T(8,128)(2,1)} fusion(bf16[768,1024]{1,0:T(8,128)(2,1)} %scatter_custom_fusion.6, s32[128]{0:T(128)S(1)} %get-tuple-element.41, bf16[128,1024]{1,0:T(8,128)(2,1)S(1)} %copy-done.2), kind=kCustom, calls=%fused_computation.13 | custom fusion | bytes 786944 | tf_op jit(solution)/shard_map/scatter | solution.py:21
  61.7 3.9 %scatter_fusion.6 = bf16[768,1024]{1,0:T(8,128)(2,1)} fusion(bf16[768,1024]{1,0:T(8,128)(2,1)} %scatter_fusion.5, s32[128]{0:T(128)S(1)} %get-tuple-element.42, bf16[128,1024]{1,0:T(8,128)(2,1)S(1)} %copy-done.2), kind=kCustom, calls=%fused_computation.14 | custom fusion | bytes 786944 | tf_op jit(solution)/shard_map/scatter | solution.py:21
  65.6 3.9 %scatter_fusion.7 = bf16[768,1024]{1,0:T(8,128)(2,1)} fusion(bf16[768,1024]{1,0:T(8,128)(2,1)} %scatter_fusion.6, s32[128]{0:T(128)S(1)} %get-tuple-element.43, bf16[128,1024]{1,0:T(8,128)(2,1)S(1)} %copy-done.2), kind=kCustom, calls=%fused_computation.15 | custom fusion | bytes 786944 | tf_op jit(solution)/shard_map/scatter | solution.py:21
  69.5 3.9 %scatter_fusion.8 = bf16[768,1024]{1,0:T(8,128)(2,1)} fusion(bf16[768,1024]{1,0:T(8,128)(2,1)} %scatter_fusion.7, s32[128]{0:T(128)S(1)} %get-tuple-element.44, bf16[128,1024]{1,0:T(8,128)(2,1)S(1)} %copy-done.2), kind=kCustom, calls=%fused_computation.16 | custom fusion | bytes 786944 | tf_op jit(solution)/shard_map/scatter | solution.py:21
  73.4 3.9 %scatter_fusion.9 = bf16[768,1024]{1,0:T(8,128)(2,1)} fusion(bf16[768,1024]{1,0:T(8,128)(2,1)} %scatter_fusion.8, s32[128]{0:T(128)S(1)} %get-tuple-element.39, bf16[128,1024]{1,0:T(8,128)(2,1)S(1)} %copy-done.2), kind=kCustom, calls=%fused_computation.17 | custom fusion | bytes 786944 | tf_op jit(solution)/shard_map/scatter | solution.py:21
  77.3 15.9 %all-to-all-done.2 = bf16[16,1,48,1024]{3,2,1,0:T(8,128)(2,1)S(1)} async-done(((bf16[16,1,48,1024]{3,2,1,0:T(8,128)(2,1)}), bf16[16,1,48,1024]{3,2,1,0:T(8,128)(2,1)S(1)}, u32[]{:S(2)}, u32[]{:S(2)}) %all-to-all-start.2) | async-done | bytes 1572896 | tf_op jit(solution)/shard_map/all_to_all | solution.py:28
  93.2 4.9 %all-to-all-start.1 = ((bf16[16,1,48,1024]{3,2,1,0:T(8,128)(2,1)}), bf16[16,1,48,1024]{3,2,1,0:T(8,128)(2,1)}, u32[]{:S(2)}, u32[]{:S(2)}) async-start(bf16[16,1,48,1024]{3,2,1,0:T(8,128)(2,1)} %bitcast.15), calls=%async_computation.1 | async-start | bytes 3145728 | tf_op jit(solution)/shard_map/all_to_all | solution.py:29
  98.1 2.8 fusion.10
  100.9 2.9 fusion.12
  103.8 32.2 %all-to-all-done.1 = bf16[16,1,48,1024]{3,2,1,0:T(8,128)(2,1)} async-done(((bf16[16,1,48,1024]{3,2,1,0:T(8,128)(2,1)}), bf16[16,1,48,1024]{3,2,1,0:T(8,128)(2,1)}, u32[]{:S(2)}, u32[]{:S(2)}) %all-to-all-start.1) | async-done | bytes 1572896 | tf_op jit(solution)/shard_map/all_to_all | solution.py:29
  136.0 3.4 fusion.21
  141.6 2.6 fusion.14
  144.2 4.8 %all-to-all-start.3 = ((bf16[16,1,48,1024]{3,2,1,0:T(8,128)(2,1)}), bf16[16,1,48,1024]{3,2,1,0:T(8,128)(2,1)S(1)}, u32[]{:S(2)}, u32[]{:S(2)}) async-start(bf16[16,1,48,1024]{3,2,1,0:T(8,128)(2,1)} %fusion.14), calls=%async_computation.3 | async-start | bytes 3145728 | tf_op jit(solution)/shard_map/all_to_all | solution.py:51
  149.0 5.5 %fusion.15 = bf16[1024,1,704]{0,2,1:T(8,128)(2,1)} fusion(bf16[16,1,48,1024]{3,2,1,0:T(8,128)(2,1)} %all-to-all-done.1, f32[16,48]{1,0:T(8,128)S(1)} %bitcast.195, f32[16,48,704]{2,1,0:T(8,128)} %fusion.12, f32[16,48,704]{2,1,0:T(8,128)} %fusion.10), kind=kOutput, calls=%fused_computation.48 | convolution fusion | flops 1113620480 | bytes 7343104 | tf_op jit(solution)/shard_map/secd,secf->def/dot_general | solution.py:59
  154.6 8.4 %copy.21 = bf16[1024,1,704]{2,1,0:T(2,128)(2,1)} copy(bf16[1024,1,704]{0,2,1:T(8,128)(2,1)} %fusion.15) | data formatting | bytes 2883584 | tf_op jit(solution)/shard_map/convert_element_type | solution.py:59
  166.2 165.7 %all-reduce.3.cloned.1.call-done = bf16[1024,1,704]{2,1,0:T(2,128)(2,1)} async-done(((bf16[1024,1,704]{2,1,0:T(2,128)(2,1)}), bf16[1024,1,704]{2,1,0:T(2,128)(2,1)}) %all-reduce.3.cloned.1.call-update) | async-done | bytes 1441808
  (52 shorter events, 27.4 us)
Async XLA Ops:
  7.2 90.9 %copy-start = (bf16[1,1024,704]{1,2,0:T(8,128)(2,1)S(1)}, bf16[1,1024,704]{1,2,0:T(8,128)(2,1)}, u32[]{:S(2)}) copy-start(bf16[1,1024,704]{1,2,0:T(8,128)(2,1)} %param.15) | copy-start | bytes 4325380
  11.8 14.1 %copy-start.1 = (bf16[128,1024]{1,0:T(8,128)(2,1)S(1)}, bf16[128,1024]{1,0:T(8,128)(2,1)}, u32[]{:S(2)}) copy-start(bf16[128,1024]{1,0:T(8,128)(2,1)} %param.10) | copy-start | bytes 786436
  15.5 32.5 %all-to-all-start = ((bf16[16,1,48]{2,1,0:T(2,128)(2,1)}), bf16[16,1,48]{2,1,0:T(2,128)(2,1)S(1)}, u32[]{:S(2)}, u32[]{:S(2)}) async-start(bf16[16,1,48]{2,1,0:T(2,128)(2,1)} %convert_element_type.94), calls=%async_computation | async-start | bytes 16384 | tf_op jit(solution)/shard_map/all_to_all | solution.py:30
  48.0 7.4 %copy-start.2 = (bf16[128,1024]{1,0:T(8,128)(2,1)S(1)}, bf16[128,1024]{1,0:T(8,128)(2,1)}, u32[]{:S(2)}) copy-start(bf16[128,1024]{1,0:T(8,128)(2,1)} %param.11) | copy-start | bytes 786436
  48.0 45.2 %all-to-all-start.2 = ((bf16[16,1,48,1024]{3,2,1,0:T(8,128)(2,1)}), bf16[16,1,48,1024]{3,2,1,0:T(8,128)(2,1)S(1)}, u32[]{:S(2)}, u32[]{:S(2)}) async-start(bf16[16,1,48,1024]{3,2,1,0:T(8,128)(2,1)} %bitcast.23), calls=%async_computation.2 | async-start | bytes 3145728 | tf_op jit(solution)/shard_map/all_to_all | solution.py:28
  93.2 42.8 %all-to-all-start.1 = ((bf16[16,1,48,1024]{3,2,1,0:T(8,128)(2,1)}), bf16[16,1,48,1024]{3,2,1,0:T(8,128)(2,1)}, u32[]{:S(2)}, u32[]{:S(2)}) async-start(bf16[16,1,48,1024]{3,2,1,0:T(8,128)(2,1)} %bitcast.15), calls=%async_computation.1 | async-start | bytes 3145728 | tf_op jit(solution)/shard_map/all_to_all | solution.py:29
  98.1 2.8 copy-start.6
  136.0 3.4 copy-start.8
  136.0 3.4 copy-start.9
  139.5 2.1 copy-start.7
  144.2 189.3 %all-to-all-start.3 = ((bf16[16,1,48,1024]{3,2,1,0:T(8,128)(2,1)}), bf16[16,1,48,1024]{3,2,1,0:T(8,128)(2,1)S(1)}, u32[]{:S(2)}, u32[]{:S(2)}) async-start(bf16[16,1,48,1024]{3,2,1,0:T(8,128)(2,1)} %fusion.14), calls=%async_computation.3 | async-start | bytes 3145728 | tf_op jit(solution)/shard_map/all_to_all | solution.py:51
  149.0 182.9 %all-reduce.3.cloned.1.call-start = ((), (), s32[]{:S(2)}) async-start(), calls=%async_computation.4 | async-start | bytes 6291456
  340.0 1.6 copy-start.3
  340.0 1.6 copy-start.4
  340.0 1.6 copy-start.5
Sparse Core Ops, SparseCore 0:
  163.1 168.6 all-reduce.2
where the time goes:
time: 353 us; the launch traced here: 351 us
  waiting for transfers between devices  214 us (61%)
  local copies, waits for them, and re-layouts  70 us (20%)
  starting transfers between devices  27.5 us (8%)
  matrix products  19.3 us (5%)
  between operations  14.9 us (4%)
  other arithmetic  5.24 us (1%)
    unnamed x2, waiting for transfers between devices  166 us
    all_to_all x1, waiting for transfers between devices, on_device(): lax.all_to_all(rows_grad, 'expert', split_axis=0, concat_axis=0, tiled=True)  32.2 us
    scatter x6, local copies, waits for them, and re-layouts, on_device(): rows_in = rows_in.at[target[:, route_index]].set(tokens, mode='drop')  22 us
    scatter x6, local copies, waits for them, and re-layouts, on_device(): rows_grad = rows_grad.at[target[:, route_index]].set(grad_out, mode='drop')  22 us
    all_to_all x1, waiting for transfers between devices, on_device(): lax.all_to_all(rows_in, 'expert', split_axis=0, concat_axis=0, tiled=True)  15.9 us
    all_to_all x1, starting transfers between devices, on_device(): lax.all_to_all(weights_in.astype(jnp.bfloat16), 'expert', split_axis=0, c...  10.4 us
    convert_element_type x1, local copies, waits for them, and re-layouts, on_device(): jnp.einsum('secd,secf->def', scaled, hidden, preferred_element_type=jnp.f...  8.39 us
    gather x6, local copies, waits for them, and re-layouts, on_device(): jnp.take(back_flat, target[:, route_index], axis=0, mode='fill', fill_val...  8.08 us
  transfers between devices with their start and end apart: 5, of which 3 were waited for; matrix products, arithmetic and copies ran while one was open for 19% of the time, Pallas kernels for 0%

commit v1 on v0

v1 whole, which is shorter than its diff:
```python
import jax
import jax.numpy as jnp
from jax import lax
from jax.experimental import pallas as pl
from jax.experimental.pallas import tpu as pltpu
from jax.sharding import PartitionSpec as P

BF16 = jnp.bfloat16
F32 = jnp.float32
ROWS = 128
CAP = 48
META = 8
CHIPS = 8
VMEM = pltpu.CompilerParams(vmem_limit_bytes=40 * 1024 * 1024)
NT = (((1,), (1,)), ((), ()))
TN = (((0,), (0,)), ((), ()))


def dot(a, b, dims=(((1,), (0,)), ((), ()))):
    return lax.dot_general(a, b, dims, preferred_element_type=F32)


def call(kernel, outs, args, flops=0, scratch=()):
    moved = sum(a.size * a.dtype.itemsize for a in (*args, *outs))
    return pl.pallas_call(
        kernel,
        out_shape=outs,
        in_specs=[pl.BlockSpec(memory_space=pltpu.VMEM)] * len(args),
        out_specs=[pl.BlockSpec(memory_space=pltpu.VMEM)] * len(outs),
        scratch_shapes=list(scratch),
        compiler_params=VMEM,
        cost_estimate=pl.CostEstimate(flops=flops, bytes_accessed=moved, transcendentals=0),
    )(*args)


def shape(dims, kind=BF16):
    return jax.ShapeDtypeStruct(dims, kind)


def pack_kernel(tokens, ids, slots, probs, out):
    out[:ROWS, :] = tokens[...]
    routes = ids.shape[0]
    meta = jnp.zeros((META, out.shape[1]), F32)
    row = lax.broadcasted_iota(jnp.int32, (META, ROWS), 0)
    spare = jnp.zeros((META - routes, ROWS), F32)
    filled = [
        jnp.where(row < routes, jnp.concatenate([v.astype(F32), spare], 0), -1.0)
        for v in (ids[...], slots[...], probs[...])
    ]
    tail = jnp.zeros((META, out.shape[1] - 3 * ROWS), F32)
    out[ROWS:, :] = jnp.concatenate([*filled, tail], 1).astype(BF16)


def one_hot(meta, expert):
    ids = meta[:, :ROWS].astype(F32)
    slots = meta[:, ROWS : 2 * ROWS].astype(F32)
    probs = meta[:, 2 * ROWS : 3 * ROWS].astype(F32)
    mine = ids == expert.astype(F32)
    slot = jnp.sum(jnp.where(mine, slots + 1.0, 0.0), 0, keepdims=True) - 1.0
    prob = jnp.sum(jnp.where(mine, probs, 0.0), 0, keepdims=True)
    hit = lax.broadcasted_iota(jnp.int32, (CAP, ROWS), 0).astype(F32) == slot
    return jnp.where(hit, 1.0, 0.0), jnp.where(hit, prob, 0.0)


def select_kernel(*refs):
    toks, grads = refs[:CHIPS], refs[CHIPS : 2 * CHIPS]
    own_x, own_s, sib = refs[2 * CHIPS :]
    me = lax.axis_index("expert")
    other = me + 1 - 2 * lax.rem(me, 2)
    z = lax.div(me, 2)
    for d in range(CHIPS):
        at = lax.rem(z - d + CHIPS, CHIPS)
        meta = toks[d][ROWS:, :]
        pick, weigh = zip(one_hot(meta, me), one_hot(meta, other))
        x = dot(jnp.concatenate(pick, 0).astype(BF16), toks[d][:ROWS, :]).astype(BF16)
        s = dot(jnp.concatenate(weigh, 0).astype(BF16), grads[d][...]).astype(BF16)
        own_x[at] = x[:CAP]
        own_s[at] = s[:CAP]
        sib[0, at] = x[CAP:]
        sib[1, at] = s[CAP:]


def expert_kernel(own_x, own_s, got, w_gate, w_up, w_down, back, hidden):
    me = lax.axis_index("expert")
    core = lax.rem(me, 2)
    width = 4
    for half in range(2):
        where = core if half == 0 else 1 - core

        @pl.loop(0, CHIPS // width)
        def _(i):
            rows = pl.ds(i * width, width)
            if half == 0:
                x, s = own_x[rows], own_s[rows]
            else:
                x, s = got[0, rows], got[1, rows]
            x = x.reshape(width * CAP, -1)
            s = s.reshape(width * CAP, -1)
            gate = dot(x, w_gate[...], NT)
            up = dot(x, w_up[...], NT)
            down = dot(s, w_down[...], NT)
            sig = jax.nn.sigmoid(gate)
            act = gate * sig
            hidden[half, rows] = (act * up).astype(BF16).reshape(width, CAP, -1)
            grad_gate = (down * up * sig * (1.0 + gate * (1.0 - sig))).astype(BF16)
            grad_up = (down * act).astype(BF16)
            out = (dot(grad_gate, w_gate[...]) + dot(grad_up, w_up[...])).astype(BF16)
            for j in range(width):
                back[i * width + j, where] = out[j * CAP : (j + 1) * CAP]


def grad_kernel(own_s, got, hidden, out):
    slots = CHIPS * CAP
    parts = out.shape[0]
    own = own_s[...].reshape(slots, -1)
    theirs = got[1].reshape(slots, -1)
    for i in range(4):
        cols = slice(i * 256, (i + 1) * 256)
        total = dot(own[:, cols], hidden[0].reshape(slots, -1), TN)
        total += dot(theirs[:, cols], hidden[1].reshape(slots, -1), TN)
        out[i * parts // 4 : (i + 1) * parts // 4] = total.astype(BF16).reshape(
            parts // 4, -1, total.shape[1]
        )


def combine_kernel(ids, slots, came, out):
    spread = jnp.zeros((came.shape[0], ROWS), F32)
    row = lax.broadcasted_iota(jnp.int32, spread.shape, 0)
    for k in range(ids.shape[0]):
        slot = slots[k : k + 1, :]
        target = jnp.where(slot < CAP, ids[k : k + 1, :] * CAP + slot, -1)
        spread = jnp.where(row == target, 1.0, spread)
    out[...] = dot(spread.astype(BF16), came[...], TN).astype(BF16)


def ring(step, swap=0):
    return [
        (z * 2 + c, ((z + step) % CHIPS) * 2 + (c + swap) % 2) for z in range(CHIPS) for c in range(2)
    ]


def on_device(tokens, grad_out, route_ids, route_slots, route_probs, w_gate, w_up, w_down):
    width = tokens.shape[1]
    hidden_width = w_down.shape[1]
    parts = lax.axis_size("dp")
    ids, slots, probs = route_ids.T, route_slots.T, route_probs.T
    w_gate, w_up, w_down = w_gate[0].T, w_up[0].T, w_down[0]

    def hop(x, step, swap=0):
        return lax.ppermute(x, "expert", ring(step, swap))

    grads = {0: grad_out}
    toks = {}
    (toks[0],) = call(
        pack_kernel, [shape((ROWS + META, width))], [tokens, ids, slots, probs]
    )
    for s in (1, 2, 3):
        grads[s] = hop(grads[s - 1], 1)
        toks[-s] = hop(toks[1 - s], -1)
        toks[s] = hop(toks[s - 1], 1)
        grads[-s] = hop(grads[1 - s], -1)
    toks[4] = hop(toks[3], 1)
    grads[4] = hop(grads[-3], -1)
    order = [0, 1, 2, 3, 4, -3, -2, -1]
    rows = shape((CHIPS, CAP, width))
    own_x, own_s, sib = call(
        select_kernel,
        [rows, rows, shape((2, CHIPS, CAP, width))],
        [toks[d] for d in order] + [grads[d] for d in order],
        flops=4 * CHIPS * 2 * CAP * ROWS * width,
    )
    got = hop(sib, 0, 1)
    back, hidden = call(
        expert_kernel,
        [shape((CHIPS, 2, CAP, width)), shape((2, CHIPS, CAP, hidden_width))],
        [own_x, own_s, got, w_gate, w_up, w_down],
        flops=10 * 2 * CHIPS * CAP * width * hidden_width,
    )
    came = lax.all_to_all(
        back.reshape(2 * CHIPS, CAP, width), "expert", split_axis=0, concat_axis=0, tiled=True
    )
    (summand,) = call(
        grad_kernel,
        [shape((parts, width // parts, hidden_width))],
        [own_s, got, hidden],
        flops=2 * 2 * CHIPS * CAP * width * hidden_width,
    )
    summands = lax.all_to_all(summand, "dp", split_axis=0, concat_axis=0, tiled=True)
    grad_down = jnp.sum(summands.astype(F32), 0).T[None]
    (grad_tokens,) = call(
        combine_kernel,
        [shape((ROWS, width))],
        [ids, slots, came.reshape(2 * CHIPS * CAP, width)],
        flops=2 * 2 * CHIPS * CAP * width * ROWS,
    )
    return grad_tokens, grad_down


def solution(mesh):
    token_spec = P(("dp", "expert"), None)
    weight_spec = P("expert", None, None)
    return jax.shard_map(
        on_device,
        mesh=mesh,
        in_specs=(token_spec,) * 5 + (weight_spec,) * 3,
        out_specs=(token_spec, P("expert", None, "dp")),
        check_vma=False,
    )
```

time: 353 us -> 180 us (0.51)
  waiting for transfers between devices: 214 us -> 47.3 us
  local copies, waits for them, and re-layouts: 70 us -> 3.97 us
  blocking collectives: 0 us -> 49.6 us
  starting transfers between devices: 27.5 us -> 58.1 us
  matrix products: 19.3 us -> 0 us
  Pallas kernels: 0 us -> 15.9 us
  between operations: 14.9 us -> 0.89 us
  other arithmetic: 5.24 us -> 0.88 us
    unnamed x2 -> x0, waiting for transfers between devices: 166 us -> none
    ppermute x0 -> x15, starting transfers between devices: none -> 53.6 us  [hop(): return lax.ppermute(x, 'expert', ring(step, swap))]
    scatter x18 -> x0, local copies, waits for them, and re-layouts: 49.9 us -> none  [the longest x6 22 us: on_device(): rows_in = rows_in.at[target[:, route_index]].set(tokens, mode='drop')]
    all_to_all x0 -> x1, blocking collectives: none -> 49.6 us  [on_device(): lax.all_to_all(summand, 'dp', split_axis=0, concat_axis=0, tiled=True)]
    all_to_all x4 -> x1, starting transfers between devices: 27.5 us -> 4.46 us  [on_device(): lax.all_to_all(back.reshape(2 * CHIPS, CAP, width), 'expert', split_axis=...]
    dot_general x6 -> x0, matrix products: 19.3 us -> none  [the longest x1 5.52 us: on_device(): jnp.einsum('secd,secf->def', scaled, hidden, preferred_element_type=jnp.f...]
    pallas_call x0 -> x5, Pallas kernels: none -> 15.9 us  [call(): pl.pallas_call(kernel, out_shape=outs, in_specs=[pl.BlockSpec(memory_spac...]
    all_to_all x4 -> x1, waiting for transfers between devices: 48.1 us -> 37 us  [on_device(): lax.all_to_all(back.reshape(2 * CHIPS, CAP, width), 'expert', split_axis=...]
  transfers between devices with their start and end apart: 5 -> 16, of which waited for: 3 -> 5; matrix products, arithmetic and copies ran while one was open for 19% -> 0% of each run, Pallas kernels for 0% -> 0%
where the time goes in v1:
time: 180 us; the launch traced here: 177 us
  starting transfers between devices  58.1 us (32%)
  blocking collectives  49.6 us (28%)
  waiting for transfers between devices  47.3 us (26%)
  Pallas kernels  15.9 us (9%)
  local copies, waits for them, and re-layouts  3.97 us (2%)
    ppermute x15, starting transfers between devices, hop(): return lax.ppermute(x, 'expert', ring(step, swap))  53.6 us
    all_to_all x1, blocking collectives, on_device(): lax.all_to_all(summand, 'dp', split_axis=0, concat_axis=0, tiled=True)  49.6 us
    all_to_all x1, waiting for transfers between devices, on_device(): lax.all_to_all(back.reshape(2 * CHIPS, CAP, width), 'expert', split_axis=...  37 us
    pallas_call x5, Pallas kernels, call(): pl.pallas_call(kernel, out_shape=outs, in_specs=[pl.BlockSpec(memory_spac...  15.9 us
    ppermute x15, waiting for transfers between devices, hop(): return lax.ppermute(x, 'expert', ring(step, swap))  10.3 us
    all_to_all x1, starting transfers between devices, on_device(): lax.all_to_all(back.reshape(2 * CHIPS, CAP, width), 'expert', split_axis=...  4.46 us
    unnamed x20, local copies, waits for them, and re-layouts  3.97 us
  transfers between devices with their start and end apart: 16, of which 5 were waited for; matrix products, arithmetic and copies ran while one was open for 0% of the time, Pallas kernels for 0%

profile of v1, /device:TPU:6, one launch (start us, length us, event | category | flops | bytes accessed | tf_op | source)
XLA Modules:
  0.0 176.5 jit_solution(11794103158314793087)
XLA Ops:
  3.7 4.3 %collective-permute-start = (bf16[136,1024]{1,0:T(8,128)(2,1)S(1)}, bf16[136,1024]{1,0:T(8,128)(2,1)S(1)}, u32[]{:S(2)}, u32[]{:S(2)}) collective-permute-start(bf16[136,1024]{1,0:T(8,128)(2,1)S(1)} %shard_map.95.refs_0_), channel_id=1, source_target_pairs={{0,2},{1,3},{2,4},{3,5},{4,6},{5,7},{6,8},{7,9},{8,10},{9,11},{10,... | collective-permute-start | bytes 835592 | tf_op jit(solution)/shard_map/ppermute | solution.py:150
  8.0 8.6 %collective-permute-start.10 = (bf16[128,1024]{1,0:T(8,128)(2,1)}, bf16[128,1024]{1,0:T(8,128)(2,1)S(1)}, u32[]{:S(2)}, u32[]{:S(2)}) collective-permute-start(bf16[128,1024]{1,0:T(8,128)(2,1)} %refs_8_.1), channel_id=1, source_target_pairs={{0,14},{1,15},{2,0},{3,1},{4,2},{5,3},{6,4},{7,5},{8,6},{9,7},{10,... | collective-permute-start | bytes 786440 | tf_op jit(solution)/shard_map/ppermute | solution.py:150
  16.6 3.9 %collective-permute-start.4 = (bf16[136,1024]{1,0:T(8,128)(2,1)S(1)}, bf16[136,1024]{1,0:T(8,128)(2,1)S(1)}, u32[]{:S(2)}, u32[]{:S(2)}) collective-permute-start(bf16[136,1024]{1,0:T(8,128)(2,1)S(1)} %shard_map.95.refs_0_), channel_id=1, source_target_pairs={{0,14},{1,15},{2,0},{3,1},{4,2},{5,3},{6,4},{7,5},{8,6},{9,7},{10,... | collective-permute-start | bytes 835592 | tf_op jit(solution)/shard_map/ppermute | solution.py:150
  21.3 1.9 %collective-permute-start.1 = (bf16[136,1024]{1,0:T(8,128)(2,1)S(1)}, bf16[136,1024]{1,0:T(8,128)(2,1)S(1)}, u32[]{:S(2)}, u32[]{:S(2)}) collective-permute-start(bf16[136,1024]{1,0:T(8,128)(2,1)S(1)} %collective-permute-done.refs_1_), channel_id=1, source_target_pairs={{0,2},{1,3},{2,4},{3,5},{4,6},{5,7},{6,8},{7,9},{8,10},{9,11},{10,... | collective-permute-start | bytes 835592 | tf_op jit(solution)/shard_map/ppermute | solution.py:150
  23.2 1.9 %collective-permute-start.7 = (bf16[128,1024]{1,0:T(8,128)(2,1)}, bf16[128,1024]{1,0:T(8,128)(2,1)S(1)}, u32[]{:S(2)}, u32[]{:S(2)}) collective-permute-start(bf16[128,1024]{1,0:T(8,128)(2,1)} %refs_8_.1), channel_id=1, source_target_pairs={{0,2},{1,3},{2,4},{3,5},{4,6},{5,7},{6,8},{7,9},{8,10},{9,11},{10,... | collective-permute-start | bytes 786440 | tf_op jit(solution)/shard_map/ppermute | solution.py:150
  25.1 5.1 %collective-permute-start.11 = (bf16[128,1024]{1,0:T(8,128)(2,1)S(1)}, bf16[128,1024]{1,0:T(8,128)(2,1)S(1)}, u32[]{:S(2)}, u32[]{:S(2)}) collective-permute-start(bf16[128,1024]{1,0:T(8,128)(2,1)S(1)} %collective-permute-done.10.refs_15_), channel_id=1, source_target_pairs={{0,14},{1,15},{2,0},{3,1},{4,2},{5,3},{6,4},{7,5},{8,6},{9,7},{10,... | collective-permute-start | bytes 786440 | tf_op jit(solution)/shard_map/ppermute | solution.py:150
  30.3 3.9 %collective-permute-start.5 = (bf16[136,1024]{1,0:T(8,128)(2,1)S(1)}, bf16[136,1024]{1,0:T(8,128)(2,1)S(1)}, u32[]{:S(2)}, u32[]{:S(2)}) collective-permute-start(bf16[136,1024]{1,0:T(8,128)(2,1)S(1)} %collective-permute-done.4.refs_7_), channel_id=1, source_target_pairs={{0,14},{1,15},{2,0},{3,1},{4,2},{5,3},{6,4},{7,5},{8,6},{9,7},{10,... | collective-permute-start | bytes 835592 | tf_op jit(solution)/shard_map/ppermute | solution.py:150
  34.2 1.9 %collective-permute-start.2 = (bf16[136,1024]{1,0:T(8,128)(2,1)S(1)}, bf16[136,1024]{1,0:T(8,128)(2,1)S(1)}, u32[]{:S(2)}, u32[]{:S(2)}) collective-permute-start(bf16[136,1024]{1,0:T(8,128)(2,1)S(1)} %collective-permute-done.1.refs_2_), channel_id=1, source_target_pairs={{0,2},{1,3},{2,4},{3,5},{4,6},{5,7},{6,8},{7,9},{8,10},{9,11},{10,... | collective-permute-start | bytes 835592 | tf_op jit(solution)/shard_map/ppermute | solution.py:150
  36.1 1.7 collective-permute-done.7.refs_9_
  37.8 1.9 %collective-permute-start.8 = (bf16[128,1024]{1,0:T(8,128)(2,1)S(1)}, bf16[128,1024]{1,0:T(8,128)(2,1)S(1)}, u32[]{:S(2)}, u32[]{:S(2)}) collective-permute-start(bf16[128,1024]{1,0:T(8,128)(2,1)S(1)} %collective-permute-done.7.refs_9_), channel_id=1, source_target_pairs={{0,2},{1,3},{2,4},{3,5},{4,6},{5,7},{6,8},{7,9},{8,10},{9,11},{10,... | collective-permute-start | bytes 786440 | tf_op jit(solution)/shard_map/ppermute | solution.py:150
  39.7 5.1 %collective-permute-start.12 = (bf16[128,1024]{1,0:T(8,128)(2,1)S(1)}, bf16[128,1024]{1,0:T(8,128)(2,1)S(1)}, u32[]{:S(2)}, u32[]{:S(2)}) collective-permute-start(bf16[128,1024]{1,0:T(8,128)(2,1)S(1)} %collective-permute-done.11.refs_14_), channel_id=1, source_target_pairs={{0,14},{1,15},{2,0},{3,1},{4,2},{5,3},{6,4},{7,5},{8,6},{9,7},{10,... | collective-permute-start | bytes 786440 | tf_op jit(solution)/shard_map/ppermute | solution.py:150
  44.9 2.3 %collective-permute-start.6 = (bf16[136,1024]{1,0:T(8,128)(2,1)S(1)}, bf16[136,1024]{1,0:T(8,128)(2,1)S(1)}, u32[]{:S(2)}, u32[]{:S(2)}) collective-permute-start(bf16[136,1024]{1,0:T(8,128)(2,1)S(1)} %collective-permute-done.5.refs_6_), channel_id=1, source_target_pairs={{0,14},{1,15},{2,0},{3,1},{4,2},{5,3},{6,4},{7,5},{8,6},{9,7},{10,... | collective-permute-start | bytes 835592 | tf_op jit(solution)/shard_map/ppermute | solution.py:150
  47.2 3.6 %collective-permute-start.3 = (bf16[136,1024]{1,0:T(8,128)(2,1)S(1)}, bf16[136,1024]{1,0:T(8,128)(2,1)S(1)}, u32[]{:S(2)}, u32[]{:S(2)}) collective-permute-start(bf16[136,1024]{1,0:T(8,128)(2,1)S(1)} %collective-permute-done.2.refs_3_), channel_id=1, source_target_pairs={{0,2},{1,3},{2,4},{3,5},{4,6},{5,7},{6,8},{7,9},{8,10},{9,11},{10,... | collective-permute-start | bytes 835592 | tf_op jit(solution)/shard_map/ppermute | solution.py:150
  50.8 1.9 %collective-permute-start.9 = (bf16[128,1024]{1,0:T(8,128)(2,1)S(1)}, bf16[128,1024]{1,0:T(8,128)(2,1)S(1)}, u32[]{:S(2)}, u32[]{:S(2)}) collective-permute-start(bf16[128,1024]{1,0:T(8,128)(2,1)S(1)} %collective-permute-done.8.refs_10_), channel_id=1, source_target_pairs={{0,2},{1,3},{2,4},{3,5},{4,6},{5,7},{6,8},{7,9},{8,10},{9,11},{10,... | collective-permute-start | bytes 786440 | tf_op jit(solution)/shard_map/ppermute | solution.py:150
  52.7 5.1 %collective-permute-start.13 = (bf16[128,1024]{1,0:T(8,128)(2,1)S(1)}, bf16[128,1024]{1,0:T(8,128)(2,1)S(1)}, u32[]{:S(2)}, u32[]{:S(2)}) collective-permute-start(bf16[128,1024]{1,0:T(8,128)(2,1)S(1)} %collective-permute-done.12.refs_13_), channel_id=1, source_target_pairs={{0,14},{1,15},{2,0},{3,1},{4,2},{5,3},{6,4},{7,5},{8,6},{9,7},{10,... | collective-permute-start | bytes 786440 | tf_op jit(solution)/shard_map/ppermute | solution.py:150
  57.9 4.5 %collective-permute-done.9.refs_11_ = bf16[128,1024]{1,0:T(8,128)(2,1)S(1)} collective-permute-done((bf16[128,1024]{1,0:T(8,128)(2,1)S(1)}, bf16[128,1024]{1,0:T(8,128)(2,1)S(1)}, u32[]{:S(2)}, u32[]{:S(2)}) %collective-permute-start.9) | collective-permute-done | bytes 262176 | tf_op jit(solution)/shard_map/ppermute | solution.py:150
  64.3 2.1 %collective-permute-start.14 = (bf16[2,8,48,1024]{3,2,1,0:T(8,128)(2,1)S(1)}, bf16[2,8,48,1024]{3,2,1,0:T(8,128)(2,1)S(1)}, u32[]{:S(2)}, u32[]{:S(2)}) collective-permute-start(bf16[2,8,48,1024]{3,2,1,0:T(8,128)(2,1)S(1)} %get-tuple-element.9), channel_id=1, source_target_pairs={{0,1},{1,0},{2,3},{3,2},{4,5},{5,4},{6,7},{7,6},{8,9},{9,8},{10,11... | collective-permute-start | bytes 4718600 | tf_op jit(solution)/shard_map/ppermute | solution.py:150
  66.3 3.4 %collective-permute-done.14.got = bf16[2,8,48,1024]{3,2,1,0:T(8,128)(2,1)S(1)} collective-permute-done((bf16[2,8,48,1024]{3,2,1,0:T(8,128)(2,1)S(1)}, bf16[2,8,48,1024]{3,2,1,0:T(8,128)(2,1)S(1)}, u32[]{:S(2)}, u32[]{:S(2)}) %collective-permute-start.14) | collective-permute-done | bytes 1572896 | tf_op jit(solution)/shard_map/ppermute | solution.py:150
  69.7 11.8 %shard_map.97 = (bf16[8,2,48,1024]{3,2,1,0:T(8,128)(2,1)}, bf16[2,8,48,704]{3,2,1,0:T(8,128)(2,1)S(1)}) custom-call(bf16[8,48,1024]{2,1,0:T(8,128)(2,1)S(1)} %get-tuple-element.7.own_x, bf16[8,48,1024]{2,1,0:T(8,128)(2,1)S(1)} %get-tuple-element.8.own_s, bf16[2,8,48,1024]{3,2,1,0:T(8,128)(2,1)S(1)} %collective-permute-done.14.got, ...), custom_call_target="tpu_custom_call" | custom-call | flops 5536481280 | bytes 10125312 | tf_op jit(solution)/shard_map/pallas_call | solution.py:25
  81.5 1.8 %shard_map.99 = bf16[32,32,704]{2,1,0:T(8,128)(2,1)S(1)} custom-call(bf16[8,48,1024]{2,1,0:T(8,128)(2,1)S(1)} %get-tuple-element.8.own_s, bf16[2,8,48,1024]{3,2,1,0:T(8,128)(2,1)S(1)} %collective-permute-done.14.got, bf16[2,8,48,704]{3,2,1,0:T(8,128)(2,1)S(1)} %get-tuple-element.11.hidden), custom_call_target="tpu_custom_call" | custom-call | flops 1107296256 | bytes 4882432 | tf_op jit(solution)/shard_map/pallas_call | solution.py:25
  83.4 49.6 %all_to_all.10 = bf16[32,32,704]{2,1,0:T(8,128)(2,1)S(1)} all-to-all(bf16[32,32,704]{2,1,0:T(8,128)(2,1)S(1)} %shard_map.99), channel_id=1, replica_groups=mesh['dp'=32,'expert'=16] {'dp'}, dimensions={0} | all-to-all | bytes 2883584 | tf_op jit(solution)/shard_map/all_to_all | solution.py:188
  132.9 4.5 %all-to-all-start = ((bf16[16,48,1024]{2,1,0:T(8,128)(2,1)}), bf16[16,48,1024]{2,1,0:T(8,128)(2,1)S(1)}, u32[]{:S(2)}, u32[]{:S(2)}) async-start(bf16[16,48,1024]{2,1,0:T(8,128)(2,1)} %bitcast.8), calls=%async_computation | async-start | bytes 3145728 | tf_op jit(solution)/shard_map/all_to_all | solution.py:179
  138.3 37.0 %all-to-all-done = bf16[16,48,1024]{2,1,0:T(8,128)(2,1)S(1)} async-done(((bf16[16,48,1024]{2,1,0:T(8,128)(2,1)}), bf16[16,48,1024]{2,1,0:T(8,128)(2,1)S(1)}, u32[]{:S(2)}, u32[]{:S(2)}) %all-to-all-start) | async-done | bytes 1572896 | tf_op jit(solution)/shard_map/all_to_all | solution.py:179
  175.3 1.2 shard_map.98
  (35 shorter events, 6.7 us)
Async XLA Ops:
  0.6 1.0 copy-start.1
  1.6 0.7 copy-start.2
  3.7 17.6 %collective-permute-start = (bf16[136,1024]{1,0:T(8,128)(2,1)S(1)}, bf16[136,1024]{1,0:T(8,128)(2,1)S(1)}, u32[]{:S(2)}, u32[]{:S(2)}) collective-permute-start(bf16[136,1024]{1,0:T(8,128)(2,1)S(1)} %shard_map.95.refs_0_), channel_id=1, source_target_pairs={{0,2},{1,3},{2,4},{3,5},{4,6},{5,7},{6,8},{7,9},{8,10},{9,11},{10,... | collective-permute-start | bytes 835592 | tf_op jit(solution)/shard_map/ppermute | solution.py:150
  8.0 17.2 %collective-permute-start.10 = (bf16[128,1024]{1,0:T(8,128)(2,1)}, bf16[128,1024]{1,0:T(8,128)(2,1)S(1)}, u32[]{:S(2)}, u32[]{:S(2)}) collective-permute-start(bf16[128,1024]{1,0:T(8,128)(2,1)} %refs_8_.1), channel_id=1, source_target_pairs={{0,14},{1,15},{2,0},{3,1},{4,2},{5,3},{6,4},{7,5},{8,6},{9,7},{10,... | collective-permute-start | bytes 786440 | tf_op jit(solution)/shard_map/ppermute | solution.py:150
  16.6 13.7 %collective-permute-start.4 = (bf16[136,1024]{1,0:T(8,128)(2,1)S(1)}, bf16[136,1024]{1,0:T(8,128)(2,1)S(1)}, u32[]{:S(2)}, u32[]{:S(2)}) collective-permute-start(bf16[136,1024]{1,0:T(8,128)(2,1)S(1)} %shard_map.95.refs_0_), channel_id=1, source_target_pairs={{0,14},{1,15},{2,0},{3,1},{4,2},{5,3},{6,4},{7,5},{8,6},{9,7},{10,... | collective-permute-start | bytes 835592 | tf_op jit(solution)/shard_map/ppermute | solution.py:150
  21.3 12.9 %collective-permute-start.1 = (bf16[136,1024]{1,0:T(8,128)(2,1)S(1)}, bf16[136,1024]{1,0:T(8,128)(2,1)S(1)}, u32[]{:S(2)}, u32[]{:S(2)}) collective-permute-start(bf16[136,1024]{1,0:T(8,128)(2,1)S(1)} %collective-permute-done.refs_1_), channel_id=1, source_target_pairs={{0,2},{1,3},{2,4},{3,5},{4,6},{5,7},{6,8},{7,9},{8,10},{9,11},{10,... | collective-permute-start | bytes 835592 | tf_op jit(solution)/shard_map/ppermute | solution.py:150
  23.2 14.6 %collective-permute-start.7 = (bf16[128,1024]{1,0:T(8,128)(2,1)}, bf16[128,1024]{1,0:T(8,128)(2,1)S(1)}, u32[]{:S(2)}, u32[]{:S(2)}) collective-permute-start(bf16[128,1024]{1,0:T(8,128)(2,1)} %refs_8_.1), channel_id=1, source_target_pairs={{0,2},{1,3},{2,4},{3,5},{4,6},{5,7},{6,8},{7,9},{8,10},{9,11},{10,... | collective-permute-start | bytes 786440 | tf_op jit(solution)/shard_map/ppermute | solution.py:150
  25.1 14.6 %collective-permute-start.11 = (bf16[128,1024]{1,0:T(8,128)(2,1)S(1)}, bf16[128,1024]{1,0:T(8,128)(2,1)S(1)}, u32[]{:S(2)}, u32[]{:S(2)}) collective-permute-start(bf16[128,1024]{1,0:T(8,128)(2,1)S(1)} %collective-permute-done.10.refs_15_), channel_id=1, source_target_pairs={{0,14},{1,15},{2,0},{3,1},{4,2},{5,3},{6,4},{7,5},{8,6},{9,7},{10,... | collective-permute-start | bytes 786440 | tf_op jit(solution)/shard_map/ppermute | solution.py:150
  30.3 14.6 %collective-permute-start.5 = (bf16[136,1024]{1,0:T(8,128)(2,1)S(1)}, bf16[136,1024]{1,0:T(8,128)(2,1)S(1)}, u32[]{:S(2)}, u32[]{:S(2)}) collective-permute-start(bf16[136,1024]{1,0:T(8,128)(2,1)S(1)} %collective-permute-done.4.refs_7_), channel_id=1, source_target_pairs={{0,14},{1,15},{2,0},{3,1},{4,2},{5,3},{6,4},{7,5},{8,6},{9,7},{10,... | collective-permute-start | bytes 835592 | tf_op jit(solution)/shard_map/ppermute | solution.py:150
  34.2 13.0 %collective-permute-start.2 = (bf16[136,1024]{1,0:T(8,128)(2,1)S(1)}, bf16[136,1024]{1,0:T(8,128)(2,1)S(1)}, u32[]{:S(2)}, u32[]{:S(2)}) collective-permute-start(bf16[136,1024]{1,0:T(8,128)(2,1)S(1)} %collective-permute-done.1.refs_2_), channel_id=1, source_target_pairs={{0,2},{1,3},{2,4},{3,5},{4,6},{5,7},{6,8},{7,9},{8,10},{9,11},{10,... | collective-permute-start | bytes 835592 | tf_op jit(solution)/shard_map/ppermute | solution.py:150
  37.8 12.9 %collective-permute-start.8 = (bf16[128,1024]{1,0:T(8,128)(2,1)S(1)}, bf16[128,1024]{1,0:T(8,128)(2,1)S(1)}, u32[]{:S(2)}, u32[]{:S(2)}) collective-permute-start(bf16[128,1024]{1,0:T(8,128)(2,1)S(1)} %collective-permute-done.7.refs_9_), channel_id=1, source_target_pairs={{0,2},{1,3},{2,4},{3,5},{4,6},{5,7},{6,8},{7,9},{8,10},{9,11},{10,... | collective-permute-start | bytes 786440 | tf_op jit(solution)/shard_map/ppermute | solution.py:150
  39.7 13.0 %collective-permute-start.12 = (bf16[128,1024]{1,0:T(8,128)(2,1)S(1)}, bf16[128,1024]{1,0:T(8,128)(2,1)S(1)}, u32[]{:S(2)}, u32[]{:S(2)}) collective-permute-start(bf16[128,1024]{1,0:T(8,128)(2,1)S(1)} %collective-permute-done.11.refs_14_), channel_id=1, source_target_pairs={{0,14},{1,15},{2,0},{3,1},{4,2},{5,3},{6,4},{7,5},{8,6},{9,7},{10,... | collective-permute-start | bytes 786440 | tf_op jit(solution)/shard_map/ppermute | solution.py:150
  44.9 17.4 %collective-permute-start.6 = (bf16[136,1024]{1,0:T(8,128)(2,1)S(1)}, bf16[136,1024]{1,0:T(8,128)(2,1)S(1)}, u32[]{:S(2)}, u32[]{:S(2)}) collective-permute-start(bf16[136,1024]{1,0:T(8,128)(2,1)S(1)} %collective-permute-done.5.refs_6_), channel_id=1, source_target_pairs={{0,14},{1,15},{2,0},{3,1},{4,2},{5,3},{6,4},{7,5},{8,6},{9,7},{10,... | collective-permute-start | bytes 835592 | tf_op jit(solution)/shard_map/ppermute | solution.py:150
  47.2 15.1 %collective-permute-start.3 = (bf16[136,1024]{1,0:T(8,128)(2,1)S(1)}, bf16[136,1024]{1,0:T(8,128)(2,1)S(1)}, u32[]{:S(2)}, u32[]{:S(2)}) collective-permute-start(bf16[136,1024]{1,0:T(8,128)(2,1)S(1)} %collective-permute-done.2.refs_3_), channel_id=1, source_target_pairs={{0,2},{1,3},{2,4},{3,5},{4,6},{5,7},{6,8},{7,9},{8,10},{9,11},{10,... | collective-permute-start | bytes 835592 | tf_op jit(solution)/shard_map/ppermute | solution.py:150
  50.8 11.5 %collective-permute-start.9 = (bf16[128,1024]{1,0:T(8,128)(2,1)S(1)}, bf16[128,1024]{1,0:T(8,128)(2,1)S(1)}, u32[]{:S(2)}, u32[]{:S(2)}) collective-permute-start(bf16[128,1024]{1,0:T(8,128)(2,1)S(1)} %collective-permute-done.8.refs_10_), channel_id=1, source_target_pairs={{0,2},{1,3},{2,4},{3,5},{4,6},{5,7},{6,8},{7,9},{8,10},{9,11},{10,... | collective-permute-start | bytes 786440 | tf_op jit(solution)/shard_map/ppermute | solution.py:150
  52.7 9.6 %collective-permute-start.13 = (bf16[128,1024]{1,0:T(8,128)(2,1)S(1)}, bf16[128,1024]{1,0:T(8,128)(2,1)S(1)}, u32[]{:S(2)}, u32[]{:S(2)}) collective-permute-start(bf16[128,1024]{1,0:T(8,128)(2,1)S(1)} %collective-permute-done.12.refs_13_), channel_id=1, source_target_pairs={{0,14},{1,15},{2,0},{3,1},{4,2},{5,3},{6,4},{7,5},{8,6},{9,7},{10,... | collective-permute-start | bytes 786440 | tf_op jit(solution)/shard_map/ppermute | solution.py:150
  62.3 1.0 copy-start
  63.3 6.4 %copy-start.7 = (bf16[1,1024,704]{1,2,0:T(8,128)(2,1)S(1)}, bf16[1,1024,704]{1,2,0:T(8,128)(2,1)}, u32[]{:S(2)}) copy-start(bf16[1,1024,704]{1,2,0:T(8,128)(2,1)} %param.13) | copy-start | bytes 4325380
  63.3 6.4 %copy-start.8 = (bf16[1,1024,704]{1,2,0:T(8,128)(2,1)S(1)}, bf16[1,1024,704]{1,2,0:T(8,128)(2,1)}, u32[]{:S(2)}) copy-start(bf16[1,1024,704]{1,2,0:T(8,128)(2,1)} %param.14) | copy-start | bytes 4325380
  63.3 6.4 %copy-start.9 = (bf16[1,704,1024]{2,1,0:T(8,128)(2,1)S(1)}, bf16[1,704,1024]{2,1,0:T(8,128)(2,1)}, u32[]{:S(2)}) copy-start(bf16[1,704,1024]{2,1,0:T(8,128)(2,1)} %param.15) | copy-start | bytes 4325380
  64.3 5.4 %collective-permute-start.14 = (bf16[2,8,48,1024]{3,2,1,0:T(8,128)(2,1)S(1)}, bf16[2,8,48,1024]{3,2,1,0:T(8,128)(2,1)S(1)}, u32[]{:S(2)}, u32[]{:S(2)}) collective-permute-start(bf16[2,8,48,1024]{3,2,1,0:T(8,128)(2,1)S(1)} %get-tuple-element.9), channel_id=1, source_target_pairs={{0,1},{1,0},{2,3},{3,2},{4,5},{5,4},{6,7},{7,6},{8,9},{9,8},{10,11... | collective-permute-start | bytes 4718600 | tf_op jit(solution)/shard_map/ppermute | solution.py:150
  132.9 42.3 %all-to-all-start = ((bf16[16,48,1024]{2,1,0:T(8,128)(2,1)}), bf16[16,48,1024]{2,1,0:T(8,128)(2,1)S(1)}, u32[]{:S(2)}, u32[]{:S(2)}) async-start(bf16[16,48,1024]{2,1,0:T(8,128)(2,1)} %bitcast.8), calls=%async_computation | async-start | bytes 3145728 | tf_op jit(solution)/shard_map/all_to_all | solution.py:179
  137.4 37.9 %copy-start.3 = (s32[128,6]{0,1:T(8,128)S(1)}, s32[128,6]{0,1:T(8,128)}, u32[]{:S(2)}) copy-start(s32[128,6]{0,1:T(8,128)} %param.10) | copy-start | bytes 9220
  137.4 37.8 %copy-start.5 = (s32[128,6]{0,1:T(8,128)S(1)}, s32[128,6]{0,1:T(8,128)}, u32[]{:S(2)}) copy-start(s32[128,6]{0,1:T(8,128)} %param.11) | copy-start | bytes 9220
  (2 other events, 1.4 us)

commit v2 on v1

v2 whole, which is shorter than its diff:
```python
import functools

import jax
import jax.numpy as jnp
from jax import lax
from jax.experimental import pallas as pl
from jax.experimental.pallas import tpu as pltpu
from jax.sharding import PartitionSpec as P

BF16 = jnp.bfloat16
F32 = jnp.float32
ROWS = 128
CAP = 48
META = 8
CHIPS = 8
XS, YS, QUAD = 4, 8, 4
MIB = 1024 * 1024
NT = (((1,), (1,)), ((), ()))
TN = (((0,), (0,)), ((), ()))


def dot(a, b, dims=(((1,), (0,)), ((), ()))):
    return lax.dot_general(a, b, dims, preferred_element_type=F32)


def call(kernel, outs, args, flops=0, scratch=(), limit=16, after=()):
    moved = sum(a.size * a.dtype.itemsize for a in (*args, *outs))
    return pl.pallas_call(
        lambda *refs: kernel(*refs[len(after) :]),
        out_shape=outs,
        in_specs=[pl.BlockSpec(memory_space=pl.ANY)] * len(after)
        + [pl.BlockSpec(memory_space=pltpu.VMEM)] * len(args),
        out_specs=[pl.BlockSpec(memory_space=pltpu.VMEM)] * len(outs),
        scratch_shapes=list(scratch),
        compiler_params=pltpu.CompilerParams(vmem_limit_bytes=limit * MIB),
        cost_estimate=pl.CostEstimate(flops=flops, bytes_accessed=moved, transcendentals=0),
    )(*after, *args)


def shape(dims, kind=BF16):
    return jax.ShapeDtypeStruct(dims, kind)


def pack_kernel(tokens, grads, ids, slots, probs, out, out_grads, *scratch):
    sems, staged = scratch[-1], scratch[:-1]
    copies = [
        pltpu.make_async_copy(tokens, out.at[pl.ds(0, ROWS)], sems.at[3]),
        pltpu.make_async_copy(grads, out_grads, sems.at[4]),
    ]
    for i, v in enumerate((ids, slots, probs)):
        copies.append(pltpu.make_async_copy(v, staged[i], sems.at[i]))
    for c in copies:
        c.start()
    for c in copies:
        c.wait()
    width, routes = out.shape[1], ids.shape[0]
    row = lax.broadcasted_iota(jnp.int32, (META, ROWS), 0)
    spare = jnp.zeros((META - routes, ROWS), F32)
    filled = [
        jnp.where(row < routes, jnp.concatenate([v[...].astype(F32), spare], 0), -1.0)
        for v in staged
    ]
    tail = jnp.zeros((META, width - 3 * ROWS), F32)
    out[ROWS:, :] = jnp.concatenate([*filled, tail], 1).astype(BF16)


def one_hot(meta, expert):
    ids = meta[:, :ROWS].astype(F32)
    slots = meta[:, ROWS : 2 * ROWS].astype(F32)
    probs = meta[:, 2 * ROWS : 3 * ROWS].astype(F32)
    mine = ids == expert.astype(F32)
    slot = jnp.sum(jnp.where(mine, slots + 1.0, 0.0), 0, keepdims=True) - 1.0
    prob = jnp.sum(jnp.where(mine, probs, 0.0), 0, keepdims=True)
    hit = lax.broadcasted_iota(jnp.int32, (CAP, ROWS), 0).astype(F32) == slot
    return jnp.where(hit, 1.0, 0.0), jnp.where(hit, prob, 0.0)


def neighbours():
    me = lax.axis_index("expert")
    return me, me + 1 - 2 * lax.rem(me, 2)


def around(expert, step):
    return lax.rem(expert + 2 * step + 2 * CHIPS, 2 * CHIPS)


def pick(tok, grad, experts):
    meta = tok[ROWS:, :]
    hits, weights = zip(*(one_hot(meta, e) for e in experts))
    x = dot(jnp.concatenate(hits, 0).astype(BF16), tok[:ROWS, :]).astype(BF16)
    s = dot(jnp.concatenate(weights, 0).astype(BF16), grad[...]).astype(BF16)
    return x, s


def select_kernel(n, *refs):
    toks, grads, (own, sib) = refs[:n], refs[n : 2 * n], refs[2 * n :]
    me, other = neighbours()
    for d in range(n):
        x, s = pick(toks[d], grads[d], [me, other])
        for i, out in enumerate((own, sib)):
            out[0, d] = x[i * CAP : (i + 1) * CAP]
            out[1, d] = s[i * CAP : (i + 1) * CAP]


def expert_rows(own, got, w_gate, w_up, w_down, hidden):
    rows = own.shape[1] * CAP
    x = jnp.concatenate([own[0].reshape(rows, -1), got[0].reshape(rows, -1)], 0)
    s = jnp.concatenate([own[1].reshape(rows, -1), got[1].reshape(rows, -1)], 0)
    gate = dot(x, w_gate[...], NT)
    up = dot(x, w_up[...], NT)
    down = dot(s, w_down[...], NT)
    sig = jax.nn.sigmoid(gate)
    act = gate * sig
    hidden[...] = (act * up).astype(BF16)
    grad_gate = (down * up * sig * (1.0 + gate * (1.0 - sig))).astype(BF16)
    grad_up = (down * act).astype(BF16)
    return (dot(grad_gate, w_gate[...]) + dot(grad_up, w_up[...])).astype(BF16)


def first_kernel(own, got, w_gate, w_up, w_down, hidden, back, done):
    done[...] = jnp.zeros_like(done)
    back[...] = expert_rows(own, got, w_gate, w_up, w_down, hidden).reshape(back.shape)


def last_kernel(blocks, early, *refs):
    own, got, w_gate, w_up, w_down, back_early, own_early, got_early, hidden_early = refs[:9]
    back, *outs, hidden, total = refs[9:]
    me, other = neighbours()
    late = expert_rows(own, got, w_gate, w_up, w_down, hidden)
    for i, d in enumerate(early):
        back[around(me, -d)] = back_early[i]
        back[around(other, -d)] = back_early[len(early) + i]
    for i, d in enumerate(blocks):
        back[around(me, -d)] = late[i * CAP : (i + 1) * CAP]
        j = len(blocks) + i
        back[around(other, -d)] = late[j * CAP : (j + 1) * CAP]

    width = own.shape[-1]
    s = [r[1].reshape(-1, width) for r in (own_early, got_early, own, got)]
    s = jnp.concatenate(s, 0)
    h = jnp.concatenate([hidden_early[...], hidden[...]], 0)
    parts = total.shape[0]
    for i in range(4):
        cols = slice(i * width // 4, (i + 1) * width // 4)
        part = dot(s[:, cols], h, TN).astype(BF16)
        total[i * parts // 4 : (i + 1) * parts // 4] = part.reshape(parts // 4, -1, h.shape[1])
    x = dp_place()[1]
    for step, out in enumerate(outs):
        at = lax.rem(x + step, XS)
        for y in range(YS):
            out[y] = total[y * XS + at]


def dp_place():
    at = lax.axis_index("dp")
    return lax.div(at, XS), lax.rem(at, XS)


def sum_x_kernel(*refs):
    parts, outs = refs[:XS], refs[XS:]
    place = lax.rem(dp_place()[0], QUAD)
    for step, out in enumerate(outs):
        at = lax.rem(place + step, QUAD)
        for quad in range(YS // QUAD):
            out[quad] = sum(r[quad * QUAD + at].astype(F32) for r in parts).astype(BF16)


def sum_quad_kernel(*refs):
    *parts, keep, send = refs
    quad = lax.div(dp_place()[0], QUAD)
    keep[...] = sum(r[quad].astype(F32) for r in parts)
    send[...] = sum(r[1 - quad].astype(F32) for r in parts).astype(BF16)


def sum_pair_kernel(keep, got, out):
    out[...] = keep[...] + got[...].astype(F32)


def combine_kernel(ids, slots, came, out):
    spread = jnp.zeros((came.shape[0], ROWS), F32)
    row = lax.broadcasted_iota(jnp.int32, spread.shape, 0)
    for k in range(ids.shape[0]):
        slot = slots[k : k + 1, :]
        target = jnp.where(slot < CAP, ids[k : k + 1, :] * CAP + slot, -1)
        spread = jnp.where(row == target, 1.0, spread)
    out[...] = dot(spread.astype(BF16), came[...], TN).astype(BF16)


def ring(step, swap=0):
    return [
        (z * 2 + c, ((z + step) % CHIPS) * 2 + (c + swap) % 2) for z in range(CHIPS) for c in range(2)
    ]


def shift(quads, places, dx):
    return [
        (
            (q * QUAD + r) * XS + x,
            ((q + quads) % (YS // QUAD) * QUAD + (r + places) % QUAD) * XS + (x + dx) % XS,
        )
        for q in range(YS // QUAD)
        for r in range(QUAD)
        for x in range(XS)
    ]


def on_device(tokens, grad_out, route_ids, route_slots, route_probs, w_gate, w_up, w_down):
    width = tokens.shape[1]
    hidden_width = w_down.shape[1]
    ids, slots, probs = route_ids.T, route_slots.T, route_probs.T
    weights = [w_gate[0].T, w_up[0].T, w_down[0]]

    def hop(x, step, swap=0):
        return lax.ppermute(x, "expert", ring(step, swap))

    def dp_hop(x, *step):
        return lax.ppermute(x, "dp", shift(*step))

    toks, grads = {}, {}
    toks[0], grads[0] = pl.pallas_call(
        pack_kernel,
        out_shape=[shape((ROWS + META, width)), shape((ROWS, width))],
        in_specs=[pl.BlockSpec(memory_space=pl.ANY)] * 5,
        out_specs=[pl.BlockSpec(memory_space=pltpu.VMEM)] * 2,
        scratch_shapes=[
            *(pltpu.VMEM(v.shape, v.dtype) for v in (ids, slots, probs)),
            pltpu.SemaphoreType.DMA((5,)),
        ],
        compiler_params=pltpu.CompilerParams(vmem_limit_bytes=58 * MIB),
        cost_estimate=pl.CostEstimate(flops=0, bytes_accessed=tokens.size * 8, transcendentals=0),
    )(tokens, grad_out, ids, slots, probs)
    for s in (1, 2, 3):
        grads[s] = hop(grads[s - 1], 1)
        toks[-s] = hop(toks[1 - s], -1)
        toks[s] = hop(toks[s - 1], 1)
        grads[-s] = hop(grads[1 - s], -1)
    toks[4] = hop(toks[3], 1)
    grads[4] = hop(grads[-3], -1)

    def select(blocks, after=()):
        group = shape((2, len(blocks), CAP, width))
        own, sib = call(
            functools.partial(select_kernel, len(blocks)),
            [group, group],
            [toks[d] for d in blocks] + [grads[d] for d in blocks],
            flops=8 * len(blocks) * CAP * ROWS * width,
            after=after,
        )
        return own, hop(sib, 0, 1)

    early, late = [0, 1, -1, 2, -2], [3, -3, 4]
    own_a, got_a = select(early, [toks[3], grads[-3]])
    rows = 2 * len(early) * CAP
    hidden_a, back_a, done = call(
        first_kernel,
        [shape((rows, hidden_width)), shape((2 * len(early), CAP, width)), shape((8, 128), F32)],
        [own_a, got_a, *weights],
        flops=10 * rows * width * hidden_width,
        limit=32,
    )
    own_b, got_b = select(late, [done])
    rows = 2 * len(late) * CAP
    strip = width // (XS * YS)
    back, *by_x = call(
        functools.partial(last_kernel, late, early),
        [shape((2 * CHIPS, CAP, width))] + [shape((YS, strip, hidden_width))] * XS,
        [own_b, got_b, *weights, back_a, own_a, got_a, hidden_a],
        flops=10 * rows * width * hidden_width + 4 * CHIPS * CAP * width * hidden_width,
        scratch=[
            pltpu.VMEM((rows, hidden_width), BF16),
            pltpu.VMEM((XS * YS, strip, hidden_width), BF16),
        ],
        limit=32,
    )
    came = lax.all_to_all(back, "expert", split_axis=0, concat_axis=0, tiled=True)
    (grad_tokens,) = call(
        combine_kernel,
        [shape((ROWS, width))],
        [ids, slots, came.reshape(2 * CHIPS * CAP, width)],
        flops=2 * 2 * CHIPS * CAP * width * ROWS,
    )

    by_x = [by_x[0]] + [dp_hop(by_x[d], 0, 0, d) for d in range(1, XS)]
    by_y = call(sum_x_kernel, [shape((YS // QUAD, strip, hidden_width))] * QUAD, by_x)
    by_y = [by_y[0]] + [dp_hop(by_y[d], 0, d, 0) for d in range(1, QUAD)]
    one = (strip, hidden_width)
    keep, send = call(sum_quad_kernel, [shape(one, F32), shape(one)], by_y)
    (grad_down,) = call(sum_pair_kernel, [shape(one, F32)], [keep, dp_hop(send, 1, 0, 0)])
    return grad_tokens, grad_down.T[None]


def solution(mesh):
    token_spec = P(("dp", "expert"), None)
    weight_spec = P("expert", None, None)
    return jax.shard_map(
        on_device,
        mesh=mesh,
        in_specs=(token_spec,) * 5 + (weight_spec,) * 3,
        out_specs=(token_spec, P("expert", None, "dp")),
        check_vma=False,
    )
```

time: 180 us -> 143 us (0.79)
  blocking collectives: 49.6 us -> 0 us
  starting transfers between devices: 58.1 us -> 86.7 us
  waiting for transfers between devices: 47.3 us -> 34.4 us
    all_to_all x1 -> x0, blocking collectives: 49.6 us -> none  [on_device(): lax.all_to_all(summand, 'dp', split_axis=0, concat_axis=0, tiled=True)]
    all_to_all x1, waiting for transfers between devices: 37 us -> 0.01 us  [on_device(): lax.all_to_all(back, 'expert', split_axis=0, concat_axis=0, tiled=True)]
    ppermute x0 -> x7, starting transfers between devices: none -> 27.2 us  [dp_hop(): return lax.ppermute(x, 'dp', shift(*step))]
    ppermute x0 -> x7, waiting for transfers between devices: none -> 22.8 us  [dp_hop(): return lax.ppermute(x, 'dp', shift(*step))]
    ppermute x15 -> x16, starting transfers between devices: 53.6 us -> 55.5 us  [hop(): return lax.ppermute(x, 'expert', ring(step, swap))]
    ppermute x15 -> x16, waiting for transfers between devices: 10.3 us -> 11.5 us  [hop(): return lax.ppermute(x, 'expert', ring(step, swap))]
    unnamed x20 -> x16, local copies, waits for them, and re-layouts: 3.97 us -> 3.28 us
    pallas_call x5 -> x9, Pallas kernels: 15.9 us -> 15.3 us  [the longest x8 13.4 us: call(): pl.pallas_call(lambda *refs: kernel(*refs[len(after):]), out_shape=outs,...]
  transfers between devices with their start and end apart: 16 -> 24, of which waited for: 5 -> 11; matrix products, arithmetic and copies ran while one was open for 0% -> 0% of each run, Pallas kernels for 0% -> 5%
where the time goes in v2:
time: 143 us; the launch traced here: 141 us
  starting transfers between devices  86.7 us (61%)
  waiting for transfers between devices  34.4 us (24%)
  Pallas kernels  15.3 us (11%)
  local copies, waits for them, and re-layouts  3.28 us (2%)
    ppermute x16, starting transfers between devices, hop(): return lax.ppermute(x, 'expert', ring(step, swap))  55.5 us
    ppermute x7, starting transfers between devices, dp_hop(): return lax.ppermute(x, 'dp', shift(*step))  27.2 us
    ppermute x7, waiting for transfers between devices, dp_hop(): return lax.ppermute(x, 'dp', shift(*step))  22.8 us
    pallas_call x8, Pallas kernels, call(): pl.pallas_call(lambda *refs: kernel(*refs[len(after):]), out_shape=outs,...  13.4 us
    ppermute x16, waiting for transfers between devices, hop(): return lax.ppermute(x, 'expert', ring(step, swap))  11.5 us
    all_to_all x1, starting transfers between devices, on_device(): lax.all_to_all(back, 'expert', split_axis=0, concat_axis=0, tiled=True)  3.96 us
    unnamed x16, local copies, waits for them, and re-layouts  3.28 us
  transfers between devices with their start and end apart: 24, of which 11 were waited for; matrix products, arithmetic and copies ran while one was open for 0% of the time, Pallas kernels for 5%

profile of v2, /device:TPU:6, one launch (start us, length us, event | category | flops | bytes accessed | tf_op | source)
XLA Modules:
  0.0 140.7 jit_solution(13970119520343100856)
XLA Ops:
  2.5 4.3 %collective-permute-start = (bf16[136,1024]{1,0:T(8,128)(2,1)}, bf16[136,1024]{1,0:T(8,128)(2,1)S(1)}, u32[]{:S(2)}, u32[]{:S(2)}) collective-permute-start(bf16[136,1024]{1,0:T(8,128)(2,1)} %get-tuple-element.22.refs_2_), channel_id=1, source_target_pairs={{0,2},{1,3},{2,4},{3,5},{4,6},{5,7},{6,8},{7,9},{8,10},{9,11},{10,... | collective-permute-start | bytes 835592 | tf_op jit(solution)/shard_map/ppermute | solution.py:214
  6.8 8.6 %collective-permute-start.3 = (bf16[128,1024]{1,0:T(8,128)(2,1)}, bf16[128,1024]{1,0:T(8,128)(2,1)S(1)}, u32[]{:S(2)}, u32[]{:S(2)}) collective-permute-start(bf16[128,1024]{1,0:T(8,128)(2,1)} %get-tuple-element.23.refs_7_), channel_id=1, source_target_pairs={{0,14},{1,15},{2,0},{3,1},{4,2},{5,3},{6,4},{7,5},{8,6},{9,7},{10,... | collective-permute-start | bytes 786440 | tf_op jit(solution)/shard_map/ppermute | solution.py:214
  15.4 3.9 %collective-permute-start.6 = (bf16[136,1024]{1,0:T(8,128)(2,1)}, bf16[136,1024]{1,0:T(8,128)(2,1)S(1)}, u32[]{:S(2)}, u32[]{:S(2)}) collective-permute-start(bf16[136,1024]{1,0:T(8,128)(2,1)} %get-tuple-element.22.refs_2_), channel_id=1, source_target_pairs={{0,14},{1,15},{2,0},{3,1},{4,2},{5,3},{6,4},{7,5},{8,6},{9,7},{10,... | collective-permute-start | bytes 835592 | tf_op jit(solution)/shard_map/ppermute | solution.py:214
  24.2 5.1 %collective-permute-start.4 = (bf16[128,1024]{1,0:T(8,128)(2,1)S(1)}, bf16[128,1024]{1,0:T(8,128)(2,1)S(1)}, u32[]{:S(2)}, u32[]{:S(2)}) collective-permute-start(bf16[128,1024]{1,0:T(8,128)(2,1)S(1)} %collective-permute-done.3.refs_9_), channel_id=1, source_target_pairs={{0,14},{1,15},{2,0},{3,1},{4,2},{5,3},{6,4},{7,5},{8,6},{9,7},{10,... | collective-permute-start | bytes 786440 | tf_op jit(solution)/shard_map/ppermute | solution.py:214
  29.3 3.9 %collective-permute-start.7 = (bf16[136,1024]{1,0:T(8,128)(2,1)S(1)}, bf16[136,1024]{1,0:T(8,128)(2,1)S(1)}, u32[]{:S(2)}, u32[]{:S(2)}) collective-permute-start(bf16[136,1024]{1,0:T(8,128)(2,1)S(1)} %collective-permute-done.6.refs_4_), channel_id=1, source_target_pairs={{0,14},{1,15},{2,0},{3,1},{4,2},{5,3},{6,4},{7,5},{8,6},{9,7},{10,... | collective-permute-start | bytes 835592 | tf_op jit(solution)/shard_map/ppermute | solution.py:214
  38.8 5.1 %collective-permute-start.5 = (bf16[128,1024]{1,0:T(8,128)(2,1)S(1)}, bf16[128,1024]{1,0:T(8,128)(2,1)S(1)}, u32[]{:S(2)}, u32[]{:S(2)}) collective-permute-start(bf16[128,1024]{1,0:T(8,128)(2,1)S(1)} %collective-permute-done.4.refs_11_), channel_id=1, source_target_pairs={{0,14},{1,15},{2,0},{3,1},{4,2},{5,3},{6,4},{7,5},{8,6},{9,7},{10,... | collective-permute-start | bytes 786440 | tf_op jit(solution)/shard_map/ppermute | solution.py:214
  43.9 4.8 %collective-permute-done.9.refs_10_ = bf16[128,1024]{1,0:T(8,128)(2,1)S(1)} collective-permute-done((bf16[128,1024]{1,0:T(8,128)(2,1)S(1)}, bf16[128,1024]{1,0:T(8,128)(2,1)S(1)}, u32[]{:S(2)}, u32[]{:S(2)}) %collective-permute-start.9) | collective-permute-done | bytes 262176 | tf_op jit(solution)/shard_map/ppermute | solution.py:214
  55.3 5.1 %collective-permute-start.11 = (bf16[136,1024]{1,0:T(8,128)(2,1)S(1)}, bf16[136,1024]{1,0:T(8,128)(2,1)S(1)}, u32[]{:S(2)}, u32[]{:S(2)}) collective-permute-start(bf16[136,1024]{1,0:T(8,128)(2,1)S(1)} %collective-permute-done.7.refs_6_), channel_id=1, source_target_pairs={{0,14},{1,15},{2,0},{3,1},{4,2},{5,3},{6,4},{7,5},{8,6},{9,7},{10,... | collective-permute-start | bytes 835592 | tf_op jit(solution)/shard_map/ppermute | solution.py:214
  60.5 3.5 %collective-permute-start.14 = (bf16[128,1024]{1,0:T(8,128)(2,1)S(1)}, bf16[128,1024]{1,0:T(8,128)(2,1)S(1)}, u32[]{:S(2)}, u32[]{:S(2)}) collective-permute-start(bf16[128,1024]{1,0:T(8,128)(2,1)S(1)} %collective-permute-done.5.refs_1_.refs_5_), channel_id=1, source_target_pairs={{0,14},{1,15},{2,0},{3,1},{4,2},{5,3},{6,4},{7,5},{8,6},{9,7},{10,... | collective-permute-start | bytes 786440 | tf_op jit(solution)/shard_map/ppermute | solution.py:214
  63.9 2.4 %collective-permute-start.12 = (bf16[136,1024]{1,0:T(8,128)(2,1)S(1)}, bf16[136,1024]{1,0:T(8,128)(2,1)S(1)}, u32[]{:S(2)}, u32[]{:S(2)}) collective-permute-start(bf16[136,1024]{1,0:T(8,128)(2,1)S(1)} %collective-permute-done.2.refs_0_.refs_1_), channel_id=1, source_target_pairs={{0,2},{1,3},{2,4},{3,5},{4,6},{5,7},{6,8},{7,9},{8,10},{9,11},{10,... | collective-permute-start | bytes 835592 | tf_op jit(solution)/shard_map/ppermute | solution.py:214
  67.7 5.4 %shard_map.97 = (bf16[480,704]{1,0:T(8,128)(2,1)S(1)}, bf16[10,48,1024]{2,1,0:T(8,128)(2,1)S(1)}, f32[8,128]{1,0:T(8,128)S(1)}) custom-call(bf16[2,5,48,1024]{3,2,1,0:T(8,128)(2,1)S(1)} %get-tuple-element.24.refs_0_.refs_6_, bf16[2,5,48,1024]{3,2,1,0:T(8,128)(2,1)S(1)} %collective-permute-done.10.refs_1_.refs_7_, bf16[704,1024]{1,0:T(8,128)(2,1)S(1)} %bitcast.19, ...), custom_call_target="tpu_custom_call" | custom-call | flops 3460300800 | bytes 7954432 | tf_op jit(solution)/shard_map/pallas_call | solution.py:28
  79.6 4.7 %shard_map.99 = (bf16[16,48,1024]{2,1,0:T(8,128)(2,1)}, bf16[8,32,704]{2,1,0:T(8,128)(2,1)S(1)}, bf16[8,32,704]{2,1,0:T(8,128)(2,1)S(1)}, bf16[8,32,704]{2,1,0:T(8,128)(2,1)S(1)}, bf16[8,32,704]{2,1,0:T(8,128)(2,1)S(1)}) custom-call(bf16[2,3,48,1024]{3,2,1,0:T(8,128)(2,1)S(1)} %get-tuple-element.27.refs_0_, ...), custom_call_target="tpu_custom_call" | custom-call | flops 3183476736 | bytes 12144640 | tf_op jit(solution)/shard_map/pallas_call | solution.py:28
  84.3 4.0 %all-to-all-start = ((bf16[16,48,1024]{2,1,0:T(8,128)(2,1)}), bf16[16,48,1024]{2,1,0:T(8,128)(2,1)S(1)}, u32[]{:S(2)}, u32[]{:S(2)}) async-start(bf16[16,48,1024]{2,1,0:T(8,128)(2,1)} %get-tuple-element.31), calls=%async_computation | async-start | bytes 3145728 | tf_op jit(solution)/shard_map/all_to_all | solution.py:275
  88.3 2.4 %collective-permute-start.16 = (bf16[8,32,704]{2,1,0:T(8,128)(2,1)S(1)}, bf16[8,32,704]{2,1,0:T(8,128)(2,1)S(1)}, u32[]{:S(2)}, u32[]{:S(2)}) collective-permute-start(bf16[8,32,704]{2,1,0:T(8,128)(2,1)S(1)} %get-tuple-element.33), channel_id=1, source_target_pairs={{0,16},{16,32},{32,48},{48,0},{64,80},{80,96},{96,112},{112,64},{1... | collective-permute-start | bytes 1081352 | tf_op jit(solution)/shard_map/ppermute | solution.py:217
  90.7 4.3 %collective-permute-start.17 = (bf16[8,32,704]{2,1,0:T(8,128)(2,1)S(1)}, bf16[8,32,704]{2,1,0:T(8,128)(2,1)S(1)}, u32[]{:S(2)}, u32[]{:S(2)}) collective-permute-start(bf16[8,32,704]{2,1,0:T(8,128)(2,1)S(1)} %get-tuple-element.34), channel_id=1, source_target_pairs={{0,32},{16,48},{32,0},{48,16},{64,96},{80,112},{96,64},{112,80},{1... | collective-permute-start | bytes 1081352 | tf_op jit(solution)/shard_map/ppermute | solution.py:217
  97.0 5.2 %collective-permute-done.16.refs_1_ = bf16[8,32,704]{2,1,0:T(8,128)(2,1)S(1)} collective-permute-done((bf16[8,32,704]{2,1,0:T(8,128)(2,1)S(1)}, bf16[8,32,704]{2,1,0:T(8,128)(2,1)S(1)}, u32[]{:S(2)}, u32[]{:S(2)}) %collective-permute-start.16) | collective-permute-done | bytes 360480 | tf_op jit(solution)/shard_map/ppermute | solution.py:217
  102.1 4.0 %collective-permute-done.17.refs_2_ = bf16[8,32,704]{2,1,0:T(8,128)(2,1)S(1)} collective-permute-done((bf16[8,32,704]{2,1,0:T(8,128)(2,1)S(1)}, bf16[8,32,704]{2,1,0:T(8,128)(2,1)S(1)}, u32[]{:S(2)}, u32[]{:S(2)}) %collective-permute-start.17) | collective-permute-done | bytes 360480 | tf_op jit(solution)/shard_map/ppermute | solution.py:217
  106.1 7.6 %collective-permute-done.18.refs_3_ = bf16[8,32,704]{2,1,0:T(8,128)(2,1)S(1)} collective-permute-done((bf16[8,32,704]{2,1,0:T(8,128)(2,1)S(1)}, bf16[8,32,704]{2,1,0:T(8,128)(2,1)S(1)}, u32[]{:S(2)}, u32[]{:S(2)}) %collective-permute-start.18) | collective-permute-done | bytes 360480 | tf_op jit(solution)/shard_map/ppermute | solution.py:217
  113.9 3.5 %collective-permute-start.19 = (bf16[2,32,704]{2,1,0:T(8,128)(2,1)S(1)}, bf16[2,32,704]{2,1,0:T(8,128)(2,1)S(1)}, u32[]{:S(2)}, u32[]{:S(2)}) collective-permute-start(bf16[2,32,704]{2,1,0:T(8,128)(2,1)S(1)} %get-tuple-element.37), channel_id=1, source_target_pairs={{0,64},{16,80},{32,96},{48,112},{64,128},{80,144},{96,160},{112,17... | collective-permute-start | bytes 270344 | tf_op jit(solution)/shard_map/ppermute | solution.py:217
  117.4 4.5 %collective-permute-start.20 = (bf16[2,32,704]{2,1,0:T(8,128)(2,1)S(1)}, bf16[2,32,704]{2,1,0:T(8,128)(2,1)S(1)}, u32[]{:S(2)}, u32[]{:S(2)}) collective-permute-start(bf16[2,32,704]{2,1,0:T(8,128)(2,1)S(1)} %get-tuple-element.38), channel_id=1, source_target_pairs={{0,128},{16,144},{32,160},{48,176},{64,192},{80,208},{96,224},{112... | collective-permute-start | bytes 270344 | tf_op jit(solution)/shard_map/ppermute | solution.py:217
  121.9 3.3 %collective-permute-start.21 = (bf16[2,32,704]{2,1,0:T(8,128)(2,1)S(1)}, bf16[2,32,704]{2,1,0:T(8,128)(2,1)S(1)}, u32[]{:S(2)}, u32[]{:S(2)}) collective-permute-start(bf16[2,32,704]{2,1,0:T(8,128)(2,1)S(1)} %get-tuple-element.39), channel_id=1, source_target_pairs={{0,192},{16,208},{32,224},{48,240},{64,0},{80,16},{96,32},{112,48}... | collective-permute-start | bytes 270344 | tf_op jit(solution)/shard_map/ppermute | solution.py:217
  125.2 2.5 %collective-permute-done.20.refs_2_ = bf16[2,32,704]{2,1,0:T(8,128)(2,1)S(1)} collective-permute-done((bf16[2,32,704]{2,1,0:T(8,128)(2,1)S(1)}, bf16[2,32,704]{2,1,0:T(8,128)(2,1)S(1)}, u32[]{:S(2)}, u32[]{:S(2)}) %collective-permute-start.20) | collective-permute-done | bytes 90144 | tf_op jit(solution)/shard_map/ppermute | solution.py:217
  128.9 7.4 %collective-permute-start.22 = (bf16[32,704]{1,0:T(8,128)(2,1)S(1)}, bf16[32,704]{1,0:T(8,128)(2,1)S(1)}, u32[]{:S(2)}, u32[]{:S(2)}) collective-permute-start(bf16[32,704]{1,0:T(8,128)(2,1)S(1)} %get-tuple-element.41), channel_id=1, source_target_pairs={{0,256},{16,272},{32,288},{48,304},{64,320},{80,336},{96,352},{112... | collective-permute-start | bytes 135176 | tf_op jit(solution)/shard_map/ppermute | solution.py:217
  136.2 2.5 %collective-permute-done.22.refs_1_ = bf16[32,704]{1,0:T(8,128)(2,1)S(1)} collective-permute-done((bf16[32,704]{1,0:T(8,128)(2,1)S(1)}, bf16[32,704]{1,0:T(8,128)(2,1)S(1)}, u32[]{:S(2)}, u32[]{:S(2)}) %collective-permute-start.22) | collective-permute-done | bytes 45088 | tf_op jit(solution)/shard_map/ppermute | solution.py:217
  (49 shorter events, 31.8 us)
Async XLA Ops:
  2.5 17.8 %collective-permute-start = (bf16[136,1024]{1,0:T(8,128)(2,1)}, bf16[136,1024]{1,0:T(8,128)(2,1)S(1)}, u32[]{:S(2)}, u32[]{:S(2)}) collective-permute-start(bf16[136,1024]{1,0:T(8,128)(2,1)} %get-tuple-element.22.refs_2_), channel_id=1, source_target_pairs={{0,2},{1,3},{2,4},{3,5},{4,6},{5,7},{6,8},{7,9},{8,10},{9,11},{10,... | collective-permute-start | bytes 835592 | tf_op jit(solution)/shard_map/ppermute | solution.py:214
  6.8 17.4 %collective-permute-start.3 = (bf16[128,1024]{1,0:T(8,128)(2,1)}, bf16[128,1024]{1,0:T(8,128)(2,1)S(1)}, u32[]{:S(2)}, u32[]{:S(2)}) collective-permute-start(bf16[128,1024]{1,0:T(8,128)(2,1)} %get-tuple-element.23.refs_7_), channel_id=1, source_target_pairs={{0,14},{1,15},{2,0},{3,1},{4,2},{5,3},{6,4},{7,5},{8,6},{9,7},{10,... | collective-permute-start | bytes 786440 | tf_op jit(solution)/shard_map/ppermute | solution.py:214
  15.4 13.9 %collective-permute-start.6 = (bf16[136,1024]{1,0:T(8,128)(2,1)}, bf16[136,1024]{1,0:T(8,128)(2,1)S(1)}, u32[]{:S(2)}, u32[]{:S(2)}) collective-permute-start(bf16[136,1024]{1,0:T(8,128)(2,1)} %get-tuple-element.22.refs_2_), channel_id=1, source_target_pairs={{0,14},{1,15},{2,0},{3,1},{4,2},{5,3},{6,4},{7,5},{8,6},{9,7},{10,... | collective-permute-start | bytes 835592 | tf_op jit(solution)/shard_map/ppermute | solution.py:214
  20.3 12.9 %collective-permute-start.1 = (bf16[136,1024]{1,0:T(8,128)(2,1)S(1)}, bf16[136,1024]{1,0:T(8,128)(2,1)S(1)}, u32[]{:S(2)}, u32[]{:S(2)}) collective-permute-start(bf16[136,1024]{1,0:T(8,128)(2,1)S(1)} %collective-permute-done.refs_3_), channel_id=1, source_target_pairs={{0,2},{1,3},{2,4},{3,5},{4,6},{5,7},{6,8},{7,9},{8,10},{9,11},{10,... | collective-permute-start | bytes 835592 | tf_op jit(solution)/shard_map/ppermute | solution.py:214
  22.2 14.6 %collective-permute-start.8 = (bf16[128,1024]{1,0:T(8,128)(2,1)}, bf16[128,1024]{1,0:T(8,128)(2,1)S(1)}, u32[]{:S(2)}, u32[]{:S(2)}) collective-permute-start(bf16[128,1024]{1,0:T(8,128)(2,1)} %get-tuple-element.23.refs_7_), channel_id=1, source_target_pairs={{0,2},{1,3},{2,4},{3,5},{4,6},{5,7},{6,8},{7,9},{8,10},{9,11},{10,... | collective-permute-start | bytes 786440 | tf_op jit(solution)/shard_map/ppermute | solution.py:214
  24.2 14.6 %collective-permute-start.4 = (bf16[128,1024]{1,0:T(8,128)(2,1)S(1)}, bf16[128,1024]{1,0:T(8,128)(2,1)S(1)}, u32[]{:S(2)}, u32[]{:S(2)}) collective-permute-start(bf16[128,1024]{1,0:T(8,128)(2,1)S(1)} %collective-permute-done.3.refs_9_), channel_id=1, source_target_pairs={{0,14},{1,15},{2,0},{3,1},{4,2},{5,3},{6,4},{7,5},{8,6},{9,7},{10,... | collective-permute-start | bytes 786440 | tf_op jit(solution)/shard_map/ppermute | solution.py:214
  29.3 19.4 %collective-permute-start.7 = (bf16[136,1024]{1,0:T(8,128)(2,1)S(1)}, bf16[136,1024]{1,0:T(8,128)(2,1)S(1)}, u32[]{:S(2)}, u32[]{:S(2)}) collective-permute-start(bf16[136,1024]{1,0:T(8,128)(2,1)S(1)} %collective-permute-done.6.refs_4_), channel_id=1, source_target_pairs={{0,14},{1,15},{2,0},{3,1},{4,2},{5,3},{6,4},{7,5},{8,6},{9,7},{10,... | collective-permute-start | bytes 835592 | tf_op jit(solution)/shard_map/ppermute | solution.py:214
  33.3 15.5 %collective-permute-start.2 = (bf16[136,1024]{1,0:T(8,128)(2,1)S(1)}, bf16[136,1024]{1,0:T(8,128)(2,1)S(1)}, u32[]{:S(2)}, u32[]{:S(2)}) collective-permute-start(bf16[136,1024]{1,0:T(8,128)(2,1)S(1)} %collective-permute-done.1.refs_5_), channel_id=1, source_target_pairs={{0,2},{1,3},{2,4},{3,5},{4,6},{5,7},{6,8},{7,9},{8,10},{9,11},{10,... | collective-permute-start | bytes 835592 | tf_op jit(solution)/shard_map/ppermute | solution.py:214
  36.9 11.8 %collective-permute-start.9 = (bf16[128,1024]{1,0:T(8,128)(2,1)S(1)}, bf16[128,1024]{1,0:T(8,128)(2,1)S(1)}, u32[]{:S(2)}, u32[]{:S(2)}) collective-permute-start(bf16[128,1024]{1,0:T(8,128)(2,1)S(1)} %collective-permute-done.8.refs_8_), channel_id=1, source_target_pairs={{0,2},{1,3},{2,4},{3,5},{4,6},{5,7},{6,8},{7,9},{8,10},{9,11},{10,... | collective-permute-start | bytes 786440 | tf_op jit(solution)/shard_map/ppermute | solution.py:214
  38.8 9.9 %collective-permute-start.5 = (bf16[128,1024]{1,0:T(8,128)(2,1)S(1)}, bf16[128,1024]{1,0:T(8,128)(2,1)S(1)}, u32[]{:S(2)}, u32[]{:S(2)}) collective-permute-start(bf16[128,1024]{1,0:T(8,128)(2,1)S(1)} %collective-permute-done.4.refs_11_), channel_id=1, source_target_pairs={{0,14},{1,15},{2,0},{3,1},{4,2},{5,3},{6,4},{7,5},{8,6},{9,7},{10,... | collective-permute-start | bytes 786440 | tf_op jit(solution)/shard_map/ppermute | solution.py:214
  51.3 15.0 %collective-permute-start.10 = (bf16[2,5,48,1024]{3,2,1,0:T(8,128)(2,1)S(1)}, bf16[2,5,48,1024]{3,2,1,0:T(8,128)(2,1)S(1)}, u32[]{:S(2)}, u32[]{:S(2)}) collective-permute-start(bf16[2,5,48,1024]{3,2,1,0:T(8,128)(2,1)S(1)} %get-tuple-element.25), channel_id=1, source_target_pairs={{0,1},{1,0},{2,3},{3,2},{4,5},{5,4},{6,7},{7,6},{8,9},{9,8},{10,11... | collective-permute-start | bytes 2949128 | tf_op jit(solution)/shard_map/ppermute | solution.py:214
  53.4 19.8 %collective-permute-start.13 = (bf16[128,1024]{1,0:T(8,128)(2,1)S(1)}, bf16[128,1024]{1,0:T(8,128)(2,1)S(1)}, u32[]{:S(2)}, u32[]{:S(2)}) collective-permute-start(bf16[128,1024]{1,0:T(8,128)(2,1)S(1)} %collective-permute-done.9.refs_10_), channel_id=1, source_target_pairs={{0,2},{1,3},{2,4},{3,5},{4,6},{5,7},{6,8},{7,9},{8,10},{9,11},{10,... | collective-permute-start | bytes 786440 | tf_op jit(solution)/shard_map/ppermute | solution.py:214
  55.3 17.9 %collective-permute-start.11 = (bf16[136,1024]{1,0:T(8,128)(2,1)S(1)}, bf16[136,1024]{1,0:T(8,128)(2,1)S(1)}, u32[]{:S(2)}, u32[]{:S(2)}) collective-permute-start(bf16[136,1024]{1,0:T(8,128)(2,1)S(1)} %collective-permute-done.7.refs_6_), channel_id=1, source_target_pairs={{0,14},{1,15},{2,0},{3,1},{4,2},{5,3},{6,4},{7,5},{8,6},{9,7},{10,... | collective-permute-start | bytes 835592 | tf_op jit(solution)/shard_map/ppermute | solution.py:214
  60.5 12.7 %collective-permute-start.14 = (bf16[128,1024]{1,0:T(8,128)(2,1)S(1)}, bf16[128,1024]{1,0:T(8,128)(2,1)S(1)}, u32[]{:S(2)}, u32[]{:S(2)}) collective-permute-start(bf16[128,1024]{1,0:T(8,128)(2,1)S(1)} %collective-permute-done.5.refs_1_.refs_5_), channel_id=1, source_target_pairs={{0,14},{1,15},{2,0},{3,1},{4,2},{5,3},{6,4},{7,5},{8,6},{9,7},{10,... | collective-permute-start | bytes 786440 | tf_op jit(solution)/shard_map/ppermute | solution.py:214
  63.9 11.3 %collective-permute-start.12 = (bf16[136,1024]{1,0:T(8,128)(2,1)S(1)}, bf16[136,1024]{1,0:T(8,128)(2,1)S(1)}, u32[]{:S(2)}, u32[]{:S(2)}) collective-permute-start(bf16[136,1024]{1,0:T(8,128)(2,1)S(1)} %collective-permute-done.2.refs_0_.refs_1_), channel_id=1, source_target_pairs={{0,2},{1,3},{2,4},{3,5},{4,6},{5,7},{6,8},{7,9},{8,10},{9,11},{10,... | collective-permute-start | bytes 835592 | tf_op jit(solution)/shard_map/ppermute | solution.py:214
  75.7 3.9 %collective-permute-start.15 = (bf16[2,3,48,1024]{3,2,1,0:T(8,128)(2,1)S(1)}, bf16[2,3,48,1024]{3,2,1,0:T(8,128)(2,1)S(1)}, u32[]{:S(2)}, u32[]{:S(2)}) collective-permute-start(bf16[2,3,48,1024]{3,2,1,0:T(8,128)(2,1)S(1)} %get-tuple-element.28), channel_id=1, source_target_pairs={{0,1},{1,0},{2,3},{3,2},{4,5},{5,4},{6,7},{7,6},{8,9},{9,8},{10,11... | collective-permute-start | bytes 1769480 | tf_op jit(solution)/shard_map/ppermute | solution.py:214
  84.3 55.1 %all-to-all-start = ((bf16[16,48,1024]{2,1,0:T(8,128)(2,1)}), bf16[16,48,1024]{2,1,0:T(8,128)(2,1)S(1)}, u32[]{:S(2)}, u32[]{:S(2)}) async-start(bf16[16,48,1024]{2,1,0:T(8,128)(2,1)} %get-tuple-element.31), calls=%async_computation | async-start | bytes 3145728 | tf_op jit(solution)/shard_map/all_to_all | solution.py:275
  88.3 13.8 %collective-permute-start.16 = (bf16[8,32,704]{2,1,0:T(8,128)(2,1)S(1)}, bf16[8,32,704]{2,1,0:T(8,128)(2,1)S(1)}, u32[]{:S(2)}, u32[]{:S(2)}) collective-permute-start(bf16[8,32,704]{2,1,0:T(8,128)(2,1)S(1)} %get-tuple-element.33), channel_id=1, source_target_pairs={{0,16},{16,32},{32,48},{48,0},{64,80},{80,96},{96,112},{112,64},{1... | collective-permute-start | bytes 1081352 | tf_op jit(solution)/shard_map/ppermute | solution.py:217
  90.7 15.4 %collective-permute-start.17 = (bf16[8,32,704]{2,1,0:T(8,128)(2,1)S(1)}, bf16[8,32,704]{2,1,0:T(8,128)(2,1)S(1)}, u32[]{:S(2)}, u32[]{:S(2)}) collective-permute-start(bf16[8,32,704]{2,1,0:T(8,128)(2,1)S(1)} %get-tuple-element.34), channel_id=1, source_target_pairs={{0,32},{16,48},{32,0},{48,16},{64,96},{80,112},{96,64},{112,80},{1... | collective-permute-start | bytes 1081352 | tf_op jit(solution)/shard_map/ppermute | solution.py:217
  95.1 18.6 %collective-permute-start.18 = (bf16[8,32,704]{2,1,0:T(8,128)(2,1)S(1)}, bf16[8,32,704]{2,1,0:T(8,128)(2,1)S(1)}, u32[]{:S(2)}, u32[]{:S(2)}) collective-permute-start(bf16[8,32,704]{2,1,0:T(8,128)(2,1)S(1)} %get-tuple-element.35), channel_id=1, source_target_pairs={{0,48},{16,0},{32,16},{48,32},{64,112},{80,64},{96,80},{112,96},{1... | collective-permute-start | bytes 1081352 | tf_op jit(solution)/shard_map/ppermute | solution.py:217
  113.9 11.3 %collective-permute-start.19 = (bf16[2,32,704]{2,1,0:T(8,128)(2,1)S(1)}, bf16[2,32,704]{2,1,0:T(8,128)(2,1)S(1)}, u32[]{:S(2)}, u32[]{:S(2)}) collective-permute-start(bf16[2,32,704]{2,1,0:T(8,128)(2,1)S(1)} %get-tuple-element.37), channel_id=1, source_target_pairs={{0,64},{16,80},{32,96},{48,112},{64,128},{80,144},{96,160},{112,17... | collective-permute-start | bytes 270344 | tf_op jit(solution)/shard_map/ppermute | solution.py:217
  117.4 10.3 %collective-permute-start.20 = (bf16[2,32,704]{2,1,0:T(8,128)(2,1)S(1)}, bf16[2,32,704]{2,1,0:T(8,128)(2,1)S(1)}, u32[]{:S(2)}, u32[]{:S(2)}) collective-permute-start(bf16[2,32,704]{2,1,0:T(8,128)(2,1)S(1)} %get-tuple-element.38), channel_id=1, source_target_pairs={{0,128},{16,144},{32,160},{48,176},{64,192},{80,208},{96,224},{112... | collective-permute-start | bytes 270344 | tf_op jit(solution)/shard_map/ppermute | solution.py:217
  121.9 6.9 %collective-permute-start.21 = (bf16[2,32,704]{2,1,0:T(8,128)(2,1)S(1)}, bf16[2,32,704]{2,1,0:T(8,128)(2,1)S(1)}, u32[]{:S(2)}, u32[]{:S(2)}) collective-permute-start(bf16[2,32,704]{2,1,0:T(8,128)(2,1)S(1)} %get-tuple-element.39), channel_id=1, source_target_pairs={{0,192},{16,208},{32,224},{48,240},{64,0},{80,16},{96,32},{112,48}... | collective-permute-start | bytes 270344 | tf_op jit(solution)/shard_map/ppermute | solution.py:217
  128.9 9.9 %collective-permute-start.22 = (bf16[32,704]{1,0:T(8,128)(2,1)S(1)}, bf16[32,704]{1,0:T(8,128)(2,1)S(1)}, u32[]{:S(2)}, u32[]{:S(2)}) collective-permute-start(bf16[32,704]{1,0:T(8,128)(2,1)S(1)} %get-tuple-element.41), channel_id=1, source_target_pairs={{0,256},{16,272},{32,288},{48,304},{64,320},{80,336},{96,352},{112... | collective-permute-start | bytes 135176 | tf_op jit(solution)/shard_map/ppermute | solution.py:217
  (8 other events, 143.3 us)

commit v3 on v2

--- a/solution.py
+++ b/solution.py
@@ -13,7 +13,7 @@
 CAP = 48
 META = 8
 CHIPS = 8
-XS, YS, QUAD = 4, 8, 4
+XS, YS, PAIRS = 4, 8, 4
 MIB = 1024 * 1024
 NT = (((1,), (1,)), ((), ()))
 TN = (((0,), (0,)), ((), ()))
@@ -23,8 +23,10 @@
     return lax.dot_general(a, b, dims, preferred_element_type=F32)
 
 
-def call(kernel, outs, args, flops=0, scratch=(), limit=16, after=()):
+def call(kernel, outs, args, flops=0, scratch=(), limit=16, after=(), free=False):
     moved = sum(a.size * a.dtype.itemsize for a in (*args, *outs))
+    if free:
+        flops, moved = 0, 0
     return pl.pallas_call(
         lambda *refs: kernel(*refs[len(after) :]),
         out_shape=outs,
@@ -102,31 +104,57 @@
             out[1, d] = s[i * CAP : (i + 1) * CAP]
 
 
-def expert_rows(own, got, w_gate, w_up, w_down, hidden):
-    rows = own.shape[1] * CAP
-    x = jnp.concatenate([own[0].reshape(rows, -1), got[0].reshape(rows, -1)], 0)
-    s = jnp.concatenate([own[1].reshape(rows, -1), got[1].reshape(rows, -1)], 0)
-    gate = dot(x, w_gate[...], NT)
-    up = dot(x, w_up[...], NT)
-    down = dot(s, w_down[...], NT)
+def joined(own, got, part):
+    return jnp.concatenate([r[part].reshape(-1, r.shape[-1]) for r in (own, got)], 0)
+
+
+def forward(own, got, w_gate, w_up):
+    x = joined(own, got, 0)
+    return dot(x, w_gate[...], NT), dot(x, w_up[...], NT)
+
+
+def hidden_rows(gate, up):
+    return (gate * jax.nn.sigmoid(gate) * up).astype(BF16)
+
+
+def backward(own, got, gate, up, w_gate, w_up, w_down):
+    down = dot(joined(own, got, 1), w_down[...], NT)
     sig = jax.nn.sigmoid(gate)
-    act = gate * sig
-    hidden[...] = (act * up).astype(BF16)
     grad_gate = (down * up * sig * (1.0 + gate * (1.0 - sig))).astype(BF16)
-    grad_up = (down * act).astype(BF16)
+    grad_up = (down * (gate * sig)).astype(BF16)
     return (dot(grad_gate, w_gate[...]) + dot(grad_up, w_up[...])).astype(BF16)
 
 
 def first_kernel(own, got, w_gate, w_up, w_down, hidden, back, done):
     done[...] = jnp.zeros_like(done)
-    back[...] = expert_rows(own, got, w_gate, w_up, w_down, hidden).reshape(back.shape)
+    gate, up = forward(own, got, w_gate, w_up)
+    hidden[...] = hidden_rows(gate, up)
+    back[...] = backward(own, got, gate, up, w_gate, w_up, w_down).reshape(back.shape)
+
+
+def weight_kernel(own, got, w_gate, w_up, own_early, got_early, hidden_early, gate, up, total, strip):
+    gate[...], up[...] = forward(own, got, w_gate, w_up)
+    s = jnp.concatenate([joined(own_early, got_early, 1), joined(own, got, 1)], 0)
+    h = jnp.concatenate([hidden_early[...], hidden_rows(gate[...], up[...])], 0)
+    parts, width = total.shape[0], s.shape[1]
+    for i in range(4):
+        cols = slice(i * width // 4, (i + 1) * width // 4)
+        part = dot(s[:, cols], h, TN).astype(BF16)
+        total[i * parts // 4 : (i + 1) * parts // 4] = part.reshape(parts // 4, -1, h.shape[1])
+    take_strip(total, XS // 2, strip)
+
+
+def take_strip(total, step, out):
+    at = lax.rem(dp_place()[1] + step, XS)
+    for y in range(YS):
+        out[y] = total[y * XS + at]
 
 
 def last_kernel(blocks, early, *refs):
-    own, got, w_gate, w_up, w_down, back_early, own_early, got_early, hidden_early = refs[:9]
-    back, *outs, hidden, total = refs[9:]
+    own, got, gate, up, w_gate, w_up, w_down, back_early, total = refs[:9]
+    back, *strips = refs[9:]
     me, other = neighbours()
-    late = expert_rows(own, got, w_gate, w_up, w_down, hidden)
+    late = backward(own, got, gate[...], up[...], w_gate, w_up, w_down)
     for i, d in enumerate(early):
         back[around(me, -d)] = back_early[i]
         back[around(other, -d)] = back_early[len(early) + i]
@@ -134,21 +162,24 @@
         back[around(me, -d)] = late[i * CAP : (i + 1) * CAP]
         j = len(blocks) + i
         back[around(other, -d)] = late[j * CAP : (j + 1) * CAP]
-
-    width = own.shape[-1]
-    s = [r[1].reshape(-1, width) for r in (own_early, got_early, own, got)]
-    s = jnp.concatenate(s, 0)
-    h = jnp.concatenate([hidden_early[...], hidden[...]], 0)
-    parts = total.shape[0]
-    for i in range(4):
-        cols = slice(i * width // 4, (i + 1) * width // 4)
-        part = dot(s[:, cols], h, TN).astype(BF16)
-        total[i * parts // 4 : (i + 1) * parts // 4] = part.reshape(parts // 4, -1, h.shape[1])
-    x = dp_place()[1]
-    for step, out in enumerate(outs):
-        at = lax.rem(x + step, XS)
-        for y in range(YS):
-            out[y] = total[y * XS + at]
+    for step, out in zip((0, 1, XS - 1), strips):
+        take_strip(total, step, out)
+
+
+def hold_kernel(x, out):
+    pass
+
+
+def hold(x, work=10**11):
+    return pl.pallas_call(
+        hold_kernel,
+        out_shape=shape(x.shape, x.dtype),
+        in_specs=[pl.BlockSpec(memory_space=pl.ANY)],
+        out_specs=pl.BlockSpec(memory_space=pl.ANY),
+        input_output_aliases={0: 0},
+        compiler_params=pltpu.CompilerParams(vmem_limit_bytes=MIB),
+        cost_estimate=pl.CostEstimate(flops=work, bytes_accessed=0, transcendentals=0),
+    )(x)
 
 
 def dp_place():
@@ -158,21 +189,21 @@
 
 def sum_x_kernel(*refs):
     parts, outs = refs[:XS], refs[XS:]
-    place = lax.rem(dp_place()[0], QUAD)
+    pair = lax.div(dp_place()[0], 2)
     for step, out in enumerate(outs):
-        at = lax.rem(place + step, QUAD)
-        for quad in range(YS // QUAD):
-            out[quad] = sum(r[quad * QUAD + at].astype(F32) for r in parts).astype(BF16)
-
-
-def sum_quad_kernel(*refs):
+        at = lax.rem(pair + step, PAIRS)
+        for i in range(2):
+            out[i] = sum(r[2 * at + i].astype(F32) for r in parts).astype(BF16)
+
+
+def sum_pairs_kernel(*refs):
     *parts, keep, send = refs
-    quad = lax.div(dp_place()[0], QUAD)
-    keep[...] = sum(r[quad].astype(F32) for r in parts)
-    send[...] = sum(r[1 - quad].astype(F32) for r in parts).astype(BF16)
-
-
-def sum_pair_kernel(keep, got, out):
+    mine = lax.rem(dp_place()[0], 2)
+    keep[...] = sum(r[mine].astype(F32) for r in parts)
+    send[...] = sum(r[1 - mine].astype(F32) for r in parts).astype(BF16)
+
+
+def sum_last_kernel(keep, got, out):
     out[...] = keep[...] + got[...].astype(F32)
 
 
@@ -192,14 +223,14 @@
     ]
 
 
-def shift(quads, places, dx):
+def shift(pairs, inside, dx):
     return [
         (
-            (q * QUAD + r) * XS + x,
-            ((q + quads) % (YS // QUAD) * QUAD + (r + places) % QUAD) * XS + (x + dx) % XS,
+            (2 * p + i) * XS + x,
+            (2 * ((p + pairs) % PAIRS) + (i + inside) % 2) * XS + (x + dx) % XS,
         )
-        for q in range(YS // QUAD)
-        for r in range(QUAD)
+        for p in range(PAIRS)
+        for i in range(2)
         for x in range(XS)
     ]
 
@@ -237,6 +268,10 @@
     toks[4] = hop(toks[3], 1)
     grads[4] = hop(grads[-3], -1)
 
+    toks[-3] = hold(toks[-3], 10**10)
+
+    grads[3] = hold(grads[3], 10**10)
+
     def select(blocks, after=()):
         group = shape((2, len(blocks), CAP, width))
         own, sib = call(
@@ -245,6 +280,7 @@
             [toks[d] for d in blocks] + [grads[d] for d in blocks],
             flops=8 * len(blocks) * CAP * ROWS * width,
             after=after,
+            free=True,
         )
         return own, hop(sib, 0, 1)
 
@@ -257,19 +293,26 @@
         [own_a, got_a, *weights],
         flops=10 * rows * width * hidden_width,
         limit=32,
+        free=True,
     )
     own_b, got_b = select(late, [done])
     rows = 2 * len(late) * CAP
-    strip = width // (XS * YS)
-    back, *by_x = call(
+    cols = width // (XS * YS)
+    strip = shape((YS, cols, hidden_width))
+    wide = shape((rows, hidden_width), F32)
+    gate, up, total, strip2 = call(
+        weight_kernel,
+        [wide, wide, shape((XS * YS, cols, hidden_width)), strip],
+        [own_b, got_b, *weights[:2], own_a, got_a, hidden_a],
+        flops=4 * rows * width * hidden_width + 4 * CHIPS * CAP * width * hidden_width,
+        limit=24,
+    )
+    strip2 = hold(dp_hop(strip2, 0, 0, 2))
+    back, strip0, strip1, strip3 = call(
         functools.partial(last_kernel, late, early),
-        [shape((2 * CHIPS, CAP, width))] + [shape((YS, strip, hidden_width))] * XS,
-        [own_b, got_b, *weights, back_a, own_a, got_a, hidden_a],
-        flops=10 * rows * width * hidden_width + 4 * CHIPS * CAP * width * hidden_width,
-        scratch=[
-            pltpu.VMEM((rows, hidden_width), BF16),
-            pltpu.VMEM((XS * YS, strip, hidden_width), BF16),
-        ],
+        [shape((2 * CHIPS, CAP, width))] + [strip] * 3,
+        [own_b, got_b, gate, up, *weights, back_a, total],
+        flops=6 * rows * width * hidden_width,
         limit=32,
     )
     came = lax.all_to_all(back, "expert", split_axis=0, concat_axis=0, tiled=True)
@@ -280,12 +323,12 @@
         flops=2 * 2 * CHIPS * CAP * width * ROWS,
     )
 
-    by_x = [by_x[0]] + [dp_hop(by_x[d], 0, 0, d) for d in range(1, XS)]
-    by_y = call(sum_x_kernel, [shape((YS // QUAD, strip, hidden_width))] * QUAD, by_x)
-    by_y = [by_y[0]] + [dp_hop(by_y[d], 0, d, 0) for d in range(1, QUAD)]
-    one = (strip, hidden_width)
-    keep, send = call(sum_quad_kernel, [shape(one, F32), shape(one)], by_y)
-    (grad_down,) = call(sum_pair_kernel, [shape(one, F32)], [keep, dp_hop(send, 1, 0, 0)])
+    by_x = [strip0, dp_hop(strip1, 0, 0, 1), strip2, dp_hop(strip3, 0, 0, 3)]
+    by_y = call(sum_x_kernel, [shape((2, cols, hidden_width))] * PAIRS, by_x)
+    by_y = [by_y[0]] + [dp_hop(by_y[d], d, 0, 0) for d in range(1, PAIRS)]
+    one = (cols, hidden_width)
+    keep, send = call(sum_pairs_kernel, [shape(one, F32), shape(one)], by_y)
+    (grad_down,) = call(sum_last_kernel, [shape(one, F32)], [keep, dp_hop(send, 0, 1, 0)])
     return grad_tokens, grad_down.T[None]
 
 

time: 143 us -> 136 us (0.951); the launches traced: 141 us -> 135 us
  waiting for transfers between devices: 34.4 us -> 26 us
  starting transfers between devices: 86.7 us -> 89.7 us
    ppermute x16, waiting for transfers between devices: 11.5 us -> 5.17 us  [hop(): return lax.ppermute(x, 'expert', ring(step, swap))]
    ppermute x16, starting transfers between devices: 55.5 us -> 58.1 us  [hop(): return lax.ppermute(x, 'expert', ring(step, swap))]
    ppermute x7, waiting for transfers between devices: 22.8 us -> 20.8 us  [dp_hop(): return lax.ppermute(x, 'dp', shift(*step))]
    pallas_call x8 -> x9, Pallas kernels: 13.4 us -> 14.9 us  [call(): pl.pallas_call(lambda *refs: kernel(*refs[len(after):]), out_shape=outs,...]
    unnamed x16 -> x14, local copies, waits for them, and re-layouts: 3.28 us -> 1.93 us
  transfers between devices with their start and end apart: 24 -> 24, of which waited for: 11 -> 7; matrix products, arithmetic and copies ran while one was open for 0% -> 0% of each run, Pallas kernels for 5% -> 8%
where the time goes in v3:
time: 136 us; the launch traced here: 135 us
  starting transfers between devices  89.7 us (66%)
  waiting for transfers between devices  26 us (19%)
  Pallas kernels  16.7 us (12%)
  local copies, waits for them, and re-layouts  1.93 us (1%)
    ppermute x16, starting transfers between devices, hop(): return lax.ppermute(x, 'expert', ring(step, swap))  58.1 us
    ppermute x7, starting transfers between devices, dp_hop(): return lax.ppermute(x, 'dp', shift(*step))  27 us
    ppermute x7, waiting for transfers between devices, dp_hop(): return lax.ppermute(x, 'dp', shift(*step))  20.8 us
    pallas_call x9, Pallas kernels, call(): pl.pallas_call(lambda *refs: kernel(*refs[len(after):]), out_shape=outs,...  14.9 us
    ppermute x16, waiting for transfers between devices, hop(): return lax.ppermute(x, 'expert', ring(step, swap))  5.17 us
    all_to_all x1, starting transfers between devices, on_device(): lax.all_to_all(back, 'expert', split_axis=0, concat_axis=0, tiled=True)  4.57 us
  transfers between devices with their start and end apart: 24, of which 7 were waited for; matrix products, arithmetic and copies ran while one was open for 0% of the time, Pallas kernels for 8%

profile of v3, /device:TPU:6, one launch (start us, length us, event | category | flops | bytes accessed | tf_op | source)
XLA Modules:
  0.0 135.4 jit_solution(4585308268410448429)
XLA Ops:
  2.5 4.3 %collective-permute-start = (bf16[136,1024]{1,0:T(8,128)(2,1)}, bf16[136,1024]{1,0:T(8,128)(2,1)S(1)}, u32[]{:S(2)}, u32[]{:S(2)}) collective-permute-start(bf16[136,1024]{1,0:T(8,128)(2,1)} %get-tuple-element.25.refs_2_), channel_id=1, source_target_pairs={{0,2},{1,3},{2,4},{3,5},{4,6},{5,7},{6,8},{7,9},{8,10},{9,11},{10,... | collective-permute-start | bytes 835592 | tf_op jit(solution)/shard_map/ppermute | solution.py:245
  6.8 8.6 %collective-permute-start.3 = (bf16[128,1024]{1,0:T(8,128)(2,1)}, bf16[128,1024]{1,0:T(8,128)(2,1)S(1)}, u32[]{:S(2)}, u32[]{:S(2)}) collective-permute-start(bf16[128,1024]{1,0:T(8,128)(2,1)} %get-tuple-element.26.refs_7_), channel_id=1, source_target_pairs={{0,14},{1,15},{2,0},{3,1},{4,2},{5,3},{6,4},{7,5},{8,6},{9,7},{10,... | collective-permute-start | bytes 786440 | tf_op jit(solution)/shard_map/ppermute | solution.py:245
  17.3 5.1 %collective-permute-start.6 = (bf16[136,1024]{1,0:T(8,128)(2,1)}, bf16[136,1024]{1,0:T(8,128)(2,1)S(1)}, u32[]{:S(2)}, u32[]{:S(2)}) collective-permute-start(bf16[136,1024]{1,0:T(8,128)(2,1)} %get-tuple-element.25.refs_2_), channel_id=1, source_target_pairs={{0,14},{1,15},{2,0},{3,1},{4,2},{5,3},{6,4},{7,5},{8,6},{9,7},{10,... | collective-permute-start | bytes 835592 | tf_op jit(solution)/shard_map/ppermute | solution.py:245
  24.4 5.1 %collective-permute-start.4 = (bf16[128,1024]{1,0:T(8,128)(2,1)S(1)}, bf16[128,1024]{1,0:T(8,128)(2,1)S(1)}, u32[]{:S(2)}, u32[]{:S(2)}) collective-permute-start(bf16[128,1024]{1,0:T(8,128)(2,1)S(1)} %collective-permute-done.3.refs_9_), channel_id=1, source_target_pairs={{0,14},{1,15},{2,0},{3,1},{4,2},{5,3},{6,4},{7,5},{8,6},{9,7},{10,... | collective-permute-start | bytes 786440 | tf_op jit(solution)/shard_map/ppermute | solution.py:245
  31.5 5.1 %collective-permute-start.7 = (bf16[136,1024]{1,0:T(8,128)(2,1)S(1)}, bf16[136,1024]{1,0:T(8,128)(2,1)S(1)}, u32[]{:S(2)}, u32[]{:S(2)}) collective-permute-start(bf16[136,1024]{1,0:T(8,128)(2,1)S(1)} %collective-permute-done.6.refs_4_), channel_id=1, source_target_pairs={{0,14},{1,15},{2,0},{3,1},{4,2},{5,3},{6,4},{7,5},{8,6},{9,7},{10,... | collective-permute-start | bytes 835592 | tf_op jit(solution)/shard_map/ppermute | solution.py:245
  38.6 5.1 %collective-permute-start.5 = (bf16[128,1024]{1,0:T(8,128)(2,1)S(1)}, bf16[128,1024]{1,0:T(8,128)(2,1)S(1)}, u32[]{:S(2)}, u32[]{:S(2)}) collective-permute-start(bf16[128,1024]{1,0:T(8,128)(2,1)S(1)} %collective-permute-done.4.refs_11_), channel_id=1, source_target_pairs={{0,14},{1,15},{2,0},{3,1},{4,2},{5,3},{6,4},{7,5},{8,6},{9,7},{10,... | collective-permute-start | bytes 786440 | tf_op jit(solution)/shard_map/ppermute | solution.py:245
  45.7 5.1 %collective-permute-start.11 = (bf16[136,1024]{1,0:T(8,128)(2,1)S(1)}, bf16[136,1024]{1,0:T(8,128)(2,1)S(1)}, u32[]{:S(2)}, u32[]{:S(2)}) collective-permute-start(bf16[136,1024]{1,0:T(8,128)(2,1)S(1)} %collective-permute-done.7.refs_6_), channel_id=1, source_target_pairs={{0,14},{1,15},{2,0},{3,1},{4,2},{5,3},{6,4},{7,5},{8,6},{9,7},{10,... | collective-permute-start | bytes 835592 | tf_op jit(solution)/shard_map/ppermute | solution.py:245
  50.8 2.4 %collective-permute-start.14 = (bf16[128,1024]{1,0:T(8,128)(2,1)S(1)}, bf16[128,1024]{1,0:T(8,128)(2,1)S(1)}, u32[]{:S(2)}, u32[]{:S(2)}) collective-permute-start(bf16[128,1024]{1,0:T(8,128)(2,1)S(1)} %collective-permute-done.5.refs_1_.refs_5_), channel_id=1, source_target_pairs={{0,14},{1,15},{2,0},{3,1},{4,2},{5,3},{6,4},{7,5},{8,6},{9,7},{10,... | collective-permute-start | bytes 786440 | tf_op jit(solution)/shard_map/ppermute | solution.py:245
  57.8 3.7 %collective-permute-start.12 = (bf16[136,1024]{1,0:T(8,128)(2,1)S(1)}, bf16[136,1024]{1,0:T(8,128)(2,1)S(1)}, u32[]{:S(2)}, u32[]{:S(2)}) collective-permute-start(bf16[136,1024]{1,0:T(8,128)(2,1)S(1)} %collective-permute-done.2.refs_0_.refs_1_), channel_id=1, source_target_pairs={{0,2},{1,3},{2,4},{3,5},{4,6},{5,7},{6,8},{7,9},{8,10},{9,11},{10,... | collective-permute-start | bytes 835592 | tf_op jit(solution)/shard_map/ppermute | solution.py:245
  61.6 5.4 %shard_map.97 = (bf16[480,704]{1,0:T(8,128)(2,1)S(1)}, bf16[10,48,1024]{2,1,0:T(8,128)(2,1)S(1)}, f32[8,128]{1,0:T(8,128)S(1)}) custom-call(bf16[2,5,48,1024]{3,2,1,0:T(8,128)(2,1)S(1)} %get-tuple-element.27.refs_0_.refs_4_, bf16[2,5,48,1024]{3,2,1,0:T(8,128)(2,1)S(1)} %collective-permute-done.10.refs_1_.refs_5_, bf16[704,1024]{1,0:T(8,128)(2,1)S(1)} %bitcast.15, ...), custom_call_target="tpu_custom_call" | custom-call | tf_op jit(solution)/shard_map/pallas_call | solution.py:30
  67.1 3.2 %collective-permute-done.12.refs_3_ = bf16[136,1024]{1,0:T(8,128)(2,1)S(1)} collective-permute-done((bf16[136,1024]{1,0:T(8,128)(2,1)S(1)}, bf16[136,1024]{1,0:T(8,128)(2,1)S(1)}, u32[]{:S(2)}, u32[]{:S(2)}) %collective-permute-start.12) | collective-permute-done | bytes 278560 | tf_op jit(solution)/shard_map/ppermute | solution.py:245
  74.6 2.5 %shard_map.101 = (f32[288,704]{1,0:T(8,128)S(1)}, f32[288,704]{1,0:T(8,128)S(1)}, bf16[32,32,704]{2,1,0:T(8,128)(2,1)S(1)}, bf16[8,32,704]{2,1,0:T(8,128)(2,1)S(1)}) custom-call(bf16[2,3,48,1024]{3,2,1,0:T(8,128)(2,1)S(1)} %get-tuple-element.30.refs_0_, bf16[2,3,48,1024]{3,2,1,0:T(8,128)(2,1)S(1)} %collective-permute-done.15.refs_1_, ...), custom_call_target="tpu_custom_call" | custom-call | flops 1937768448 | bytes 10129408 | tf_op jit(solution)/shard_map/pallas_call | solution.py:30
  77.1 3.3 %collective-permute-start.17 = (bf16[8,32,704]{2,1,0:T(8,128)(2,1)S(1)}, bf16[8,32,704]{2,1,0:T(8,128)(2,1)S(1)}, u32[]{:S(2)}, u32[]{:S(2)}) collective-permute-start(bf16[8,32,704]{2,1,0:T(8,128)(2,1)S(1)} %get-tuple-element.40), channel_id=1, source_target_pairs={{0,32},{16,48},{32,0},{48,16},{64,96},{80,112},{96,64},{112,80},{1... | collective-permute-start | bytes 1081352 | tf_op jit(solution)/shard_map/ppermute | solution.py:248
  80.4 3.7 %shard_map.102 = (bf16[16,48,1024]{2,1,0:T(8,128)(2,1)}, bf16[8,32,704]{2,1,0:T(8,128)(2,1)S(1)}, bf16[8,32,704]{2,1,0:T(8,128)(2,1)S(1)}, bf16[8,32,704]{2,1,0:T(8,128)(2,1)S(1)}) custom-call(bf16[2,3,48,1024]{3,2,1,0:T(8,128)(2,1)S(1)} %get-tuple-element.30.refs_0_, bf16[2,3,48,1024]{3,2,1,0:T(8,128)(2,1)S(1)} %collective-permute-done.15.refs_1_, ...), custom_call_target="tpu_custom_call" | custom-call | flops 1245708288 | bytes 12206080 | tf_op jit(solution)/shard_map/pallas_call | solution.py:30
  84.1 4.6 %all-to-all-start = ((bf16[16,48,1024]{2,1,0:T(8,128)(2,1)}), bf16[16,48,1024]{2,1,0:T(8,128)(2,1)S(1)}, u32[]{:S(2)}, u32[]{:S(2)}) async-start(bf16[16,48,1024]{2,1,0:T(8,128)(2,1)} %get-tuple-element.37), calls=%async_computation | async-start | bytes 3145728 | tf_op jit(solution)/shard_map/all_to_all | solution.py:318
  88.6 4.0 %collective-permute-start.16 = (bf16[8,32,704]{2,1,0:T(8,128)(2,1)S(1)}, bf16[8,32,704]{2,1,0:T(8,128)(2,1)S(1)}, u32[]{:S(2)}, u32[]{:S(2)}) collective-permute-start(bf16[8,32,704]{2,1,0:T(8,128)(2,1)S(1)} %get-tuple-element.39), channel_id=1, source_target_pairs={{0,16},{16,32},{32,48},{48,0},{64,80},{80,96},{96,112},{112,64},{1... | collective-permute-start | bytes 1081352 | tf_op jit(solution)/shard_map/ppermute | solution.py:248
  94.6 7.4 %collective-permute-done.16.refs_1_ = bf16[8,32,704]{2,1,0:T(8,128)(2,1)S(1)} collective-permute-done((bf16[8,32,704]{2,1,0:T(8,128)(2,1)S(1)}, bf16[8,32,704]{2,1,0:T(8,128)(2,1)S(1)}, u32[]{:S(2)}, u32[]{:S(2)}) %collective-permute-start.16) | collective-permute-done | bytes 360480 | tf_op jit(solution)/shard_map/ppermute | solution.py:248
  102.0 4.9 %collective-permute-done.18.refs_3_ = bf16[8,32,704]{2,1,0:T(8,128)(2,1)S(1)} collective-permute-done((bf16[8,32,704]{2,1,0:T(8,128)(2,1)S(1)}, bf16[8,32,704]{2,1,0:T(8,128)(2,1)S(1)}, u32[]{:S(2)}, u32[]{:S(2)}) %collective-permute-start.18) | collective-permute-done | bytes 360480 | tf_op jit(solution)/shard_map/ppermute | solution.py:248
  107.1 4.5 %collective-permute-start.19 = (bf16[2,32,704]{2,1,0:T(8,128)(2,1)S(1)}, bf16[2,32,704]{2,1,0:T(8,128)(2,1)S(1)}, u32[]{:S(2)}, u32[]{:S(2)}) collective-permute-start(bf16[2,32,704]{2,1,0:T(8,128)(2,1)S(1)} %get-tuple-element.43), channel_id=1, source_target_pairs={{0,128},{16,144},{32,160},{48,176},{64,192},{80,208},{96,224},{112... | collective-permute-start | bytes 270344 | tf_op jit(solution)/shard_map/ppermute | solution.py:248
  111.6 5.9 %collective-permute-start.20 = (bf16[2,32,704]{2,1,0:T(8,128)(2,1)S(1)}, bf16[2,32,704]{2,1,0:T(8,128)(2,1)S(1)}, u32[]{:S(2)}, u32[]{:S(2)}) collective-permute-start(bf16[2,32,704]{2,1,0:T(8,128)(2,1)S(1)} %get-tuple-element.44), channel_id=1, source_target_pairs={{0,256},{16,272},{32,288},{48,304},{64,320},{80,336},{96,352},{112... | collective-permute-start | bytes 270344 | tf_op jit(solution)/shard_map/ppermute | solution.py:248
  117.6 5.3 %collective-permute-start.21 = (bf16[2,32,704]{2,1,0:T(8,128)(2,1)S(1)}, bf16[2,32,704]{2,1,0:T(8,128)(2,1)S(1)}, u32[]{:S(2)}, u32[]{:S(2)}) collective-permute-start(bf16[2,32,704]{2,1,0:T(8,128)(2,1)S(1)} %get-tuple-element.45), channel_id=1, source_target_pairs={{0,384},{16,400},{32,416},{48,432},{64,448},{80,464},{96,480},{112... | collective-permute-start | bytes 270344 | tf_op jit(solution)/shard_map/ppermute | solution.py:248
  123.2 4.3 %collective-permute-done.21.refs_3_ = bf16[2,32,704]{2,1,0:T(8,128)(2,1)S(1)} collective-permute-done((bf16[2,32,704]{2,1,0:T(8,128)(2,1)S(1)}, bf16[2,32,704]{2,1,0:T(8,128)(2,1)S(1)}, u32[]{:S(2)}, u32[]{:S(2)}) %collective-permute-start.21) | collective-permute-done | bytes 90144 | tf_op jit(solution)/shard_map/ppermute | solution.py:248
  127.5 2.1 %collective-permute-start.22 = (bf16[32,704]{1,0:T(8,128)(2,1)S(1)}, bf16[32,704]{1,0:T(8,128)(2,1)S(1)}, u32[]{:S(2)}, u32[]{:S(2)}) collective-permute-start(bf16[32,704]{1,0:T(8,128)(2,1)S(1)} %get-tuple-element.47), channel_id=1, source_target_pairs={{0,64},{16,80},{32,96},{48,112},{64,0},{80,16},{96,32},{112,48},{1... | collective-permute-start | bytes 135176 | tf_op jit(solution)/shard_map/ppermute | solution.py:248
  129.6 3.9 %collective-permute-done.22.refs_1_ = bf16[32,704]{1,0:T(8,128)(2,1)S(1)} collective-permute-done((bf16[32,704]{1,0:T(8,128)(2,1)S(1)}, bf16[32,704]{1,0:T(8,128)(2,1)S(1)}, u32[]{:S(2)}, u32[]{:S(2)}) %collective-permute-start.22) | collective-permute-done | bytes 45088 | tf_op jit(solution)/shard_map/ppermute | solution.py:248
  (51 shorter events, 24.8 us)
Async XLA Ops:
  2.5 20.0 %collective-permute-start = (bf16[136,1024]{1,0:T(8,128)(2,1)}, bf16[136,1024]{1,0:T(8,128)(2,1)S(1)}, u32[]{:S(2)}, u32[]{:S(2)}) collective-permute-start(bf16[136,1024]{1,0:T(8,128)(2,1)} %get-tuple-element.25.refs_2_), channel_id=1, source_target_pairs={{0,2},{1,3},{2,4},{3,5},{4,6},{5,7},{6,8},{7,9},{8,10},{9,11},{10,... | collective-permute-start | bytes 835592 | tf_op jit(solution)/shard_map/ppermute | solution.py:245
  6.8 17.6 %collective-permute-start.3 = (bf16[128,1024]{1,0:T(8,128)(2,1)}, bf16[128,1024]{1,0:T(8,128)(2,1)S(1)}, u32[]{:S(2)}, u32[]{:S(2)}) collective-permute-start(bf16[128,1024]{1,0:T(8,128)(2,1)} %get-tuple-element.26.refs_7_), channel_id=1, source_target_pairs={{0,14},{1,15},{2,0},{3,1},{4,2},{5,3},{6,4},{7,5},{8,6},{9,7},{10,... | collective-permute-start | bytes 786440 | tf_op jit(solution)/shard_map/ppermute | solution.py:245
  15.4 14.2 %collective-permute-start.8 = (bf16[128,1024]{1,0:T(8,128)(2,1)}, bf16[128,1024]{1,0:T(8,128)(2,1)S(1)}, u32[]{:S(2)}, u32[]{:S(2)}) collective-permute-start(bf16[128,1024]{1,0:T(8,128)(2,1)} %get-tuple-element.26.refs_7_), channel_id=1, source_target_pairs={{0,2},{1,3},{2,4},{3,5},{4,6},{5,7},{6,8},{7,9},{8,10},{9,11},{10,... | collective-permute-start | bytes 786440 | tf_op jit(solution)/shard_map/ppermute | solution.py:245
  17.3 14.2 %collective-permute-start.6 = (bf16[136,1024]{1,0:T(8,128)(2,1)}, bf16[136,1024]{1,0:T(8,128)(2,1)S(1)}, u32[]{:S(2)}, u32[]{:S(2)}) collective-permute-start(bf16[136,1024]{1,0:T(8,128)(2,1)} %get-tuple-element.25.refs_2_), channel_id=1, source_target_pairs={{0,14},{1,15},{2,0},{3,1},{4,2},{5,3},{6,4},{7,5},{8,6},{9,7},{10,... | collective-permute-start | bytes 835592 | tf_op jit(solution)/shard_map/ppermute | solution.py:245
  22.5 14.2 %collective-permute-start.1 = (bf16[136,1024]{1,0:T(8,128)(2,1)S(1)}, bf16[136,1024]{1,0:T(8,128)(2,1)S(1)}, u32[]{:S(2)}, u32[]{:S(2)}) collective-permute-start(bf16[136,1024]{1,0:T(8,128)(2,1)S(1)} %collective-permute-done.refs_3_), channel_id=1, source_target_pairs={{0,2},{1,3},{2,4},{3,5},{4,6},{5,7},{6,8},{7,9},{8,10},{9,11},{10,... | collective-permute-start | bytes 835592 | tf_op jit(solution)/shard_map/ppermute | solution.py:245
  24.4 14.2 %collective-permute-start.4 = (bf16[128,1024]{1,0:T(8,128)(2,1)S(1)}, bf16[128,1024]{1,0:T(8,128)(2,1)S(1)}, u32[]{:S(2)}, u32[]{:S(2)}) collective-permute-start(bf16[128,1024]{1,0:T(8,128)(2,1)S(1)} %collective-permute-done.3.refs_9_), channel_id=1, source_target_pairs={{0,14},{1,15},{2,0},{3,1},{4,2},{5,3},{6,4},{7,5},{8,6},{9,7},{10,... | collective-permute-start | bytes 786440 | tf_op jit(solution)/shard_map/ppermute | solution.py:245
  29.6 14.2 %collective-permute-start.9 = (bf16[128,1024]{1,0:T(8,128)(2,1)S(1)}, bf16[128,1024]{1,0:T(8,128)(2,1)S(1)}, u32[]{:S(2)}, u32[]{:S(2)}) collective-permute-start(bf16[128,1024]{1,0:T(8,128)(2,1)S(1)} %collective-permute-done.8.refs_8_), channel_id=1, source_target_pairs={{0,2},{1,3},{2,4},{3,5},{4,6},{5,7},{6,8},{7,9},{8,10},{9,11},{10,... | collective-permute-start | bytes 786440 | tf_op jit(solution)/shard_map/ppermute | solution.py:245
  31.5 14.2 %collective-permute-start.7 = (bf16[136,1024]{1,0:T(8,128)(2,1)S(1)}, bf16[136,1024]{1,0:T(8,128)(2,1)S(1)}, u32[]{:S(2)}, u32[]{:S(2)}) collective-permute-start(bf16[136,1024]{1,0:T(8,128)(2,1)S(1)} %collective-permute-done.6.refs_4_), channel_id=1, source_target_pairs={{0,14},{1,15},{2,0},{3,1},{4,2},{5,3},{6,4},{7,5},{8,6},{9,7},{10,... | collective-permute-start | bytes 835592 | tf_op jit(solution)/shard_map/ppermute | solution.py:245
  36.7 16.5 %collective-permute-start.2 = (bf16[136,1024]{1,0:T(8,128)(2,1)S(1)}, bf16[136,1024]{1,0:T(8,128)(2,1)S(1)}, u32[]{:S(2)}, u32[]{:S(2)}) collective-permute-start(bf16[136,1024]{1,0:T(8,128)(2,1)S(1)} %collective-permute-done.1.refs_5_), channel_id=1, source_target_pairs={{0,2},{1,3},{2,4},{3,5},{4,6},{5,7},{6,8},{7,9},{8,10},{9,11},{10,... | collective-permute-start | bytes 835592 | tf_op jit(solution)/shard_map/ppermute | solution.py:245
  38.6 12.2 %collective-permute-start.5 = (bf16[128,1024]{1,0:T(8,128)(2,1)S(1)}, bf16[128,1024]{1,0:T(8,128)(2,1)S(1)}, u32[]{:S(2)}, u32[]{:S(2)}) collective-permute-start(bf16[128,1024]{1,0:T(8,128)(2,1)S(1)} %collective-permute-done.4.refs_11_), channel_id=1, source_target_pairs={{0,14},{1,15},{2,0},{3,1},{4,2},{5,3},{6,4},{7,5},{8,6},{9,7},{10,... | collective-permute-start | bytes 786440 | tf_op jit(solution)/shard_map/ppermute | solution.py:245
  43.7 14.0 %collective-permute-start.13 = (bf16[128,1024]{1,0:T(8,128)(2,1)S(1)}, bf16[128,1024]{1,0:T(8,128)(2,1)S(1)}, u32[]{:S(2)}, u32[]{:S(2)}) collective-permute-start(bf16[128,1024]{1,0:T(8,128)(2,1)S(1)} %collective-permute-done.9.refs_10_), channel_id=1, source_target_pairs={{0,2},{1,3},{2,4},{3,5},{4,6},{5,7},{6,8},{7,9},{8,10},{9,11},{10,... | collective-permute-start | bytes 786440 | tf_op jit(solution)/shard_map/ppermute | solution.py:245
  45.7 15.9 %collective-permute-start.11 = (bf16[136,1024]{1,0:T(8,128)(2,1)S(1)}, bf16[136,1024]{1,0:T(8,128)(2,1)S(1)}, u32[]{:S(2)}, u32[]{:S(2)}) collective-permute-start(bf16[136,1024]{1,0:T(8,128)(2,1)S(1)} %collective-permute-done.7.refs_6_), channel_id=1, source_target_pairs={{0,14},{1,15},{2,0},{3,1},{4,2},{5,3},{6,4},{7,5},{8,6},{9,7},{10,... | collective-permute-start | bytes 835592 | tf_op jit(solution)/shard_map/ppermute | solution.py:245
  50.8 16.2 %collective-permute-start.14 = (bf16[128,1024]{1,0:T(8,128)(2,1)S(1)}, bf16[128,1024]{1,0:T(8,128)(2,1)S(1)}, u32[]{:S(2)}, u32[]{:S(2)}) collective-permute-start(bf16[128,1024]{1,0:T(8,128)(2,1)S(1)} %collective-permute-done.5.refs_1_.refs_5_), channel_id=1, source_target_pairs={{0,14},{1,15},{2,0},{3,1},{4,2},{5,3},{6,4},{7,5},{8,6},{9,7},{10,... | collective-permute-start | bytes 786440 | tf_op jit(solution)/shard_map/ppermute | solution.py:245
  55.8 5.8 %collective-permute-start.10 = (bf16[2,5,48,1024]{3,2,1,0:T(8,128)(2,1)S(1)}, bf16[2,5,48,1024]{3,2,1,0:T(8,128)(2,1)S(1)}, u32[]{:S(2)}, u32[]{:S(2)}) collective-permute-start(bf16[2,5,48,1024]{3,2,1,0:T(8,128)(2,1)S(1)} %get-tuple-element.28), channel_id=1, source_target_pairs={{0,1},{1,0},{2,3},{3,2},{4,5},{5,4},{6,7},{7,6},{8,9},{9,8},{10,11... | collective-permute-start | bytes 2949128 | tf_op jit(solution)/shard_map/ppermute | solution.py:245
  57.8 12.4 %collective-permute-start.12 = (bf16[136,1024]{1,0:T(8,128)(2,1)S(1)}, bf16[136,1024]{1,0:T(8,128)(2,1)S(1)}, u32[]{:S(2)}, u32[]{:S(2)}) collective-permute-start(bf16[136,1024]{1,0:T(8,128)(2,1)S(1)} %collective-permute-done.2.refs_0_.refs_1_), channel_id=1, source_target_pairs={{0,2},{1,3},{2,4},{3,5},{4,6},{5,7},{6,8},{7,9},{8,10},{9,11},{10,... | collective-permute-start | bytes 835592 | tf_op jit(solution)/shard_map/ppermute | solution.py:245
  70.7 3.9 %collective-permute-start.15 = (bf16[2,3,48,1024]{3,2,1,0:T(8,128)(2,1)S(1)}, bf16[2,3,48,1024]{3,2,1,0:T(8,128)(2,1)S(1)}, u32[]{:S(2)}, u32[]{:S(2)}) collective-permute-start(bf16[2,3,48,1024]{3,2,1,0:T(8,128)(2,1)S(1)} %get-tuple-element.31), channel_id=1, source_target_pairs={{0,1},{1,0},{2,3},{3,2},{4,5},{5,4},{6,7},{7,6},{8,9},{9,8},{10,11... | collective-permute-start | bytes 1769480 | tf_op jit(solution)/shard_map/ppermute | solution.py:245
  77.1 17.5 %collective-permute-start.17 = (bf16[8,32,704]{2,1,0:T(8,128)(2,1)S(1)}, bf16[8,32,704]{2,1,0:T(8,128)(2,1)S(1)}, u32[]{:S(2)}, u32[]{:S(2)}) collective-permute-start(bf16[8,32,704]{2,1,0:T(8,128)(2,1)S(1)} %get-tuple-element.40), channel_id=1, source_target_pairs={{0,32},{16,48},{32,0},{48,16},{64,96},{80,112},{96,64},{112,80},{1... | collective-permute-start | bytes 1081352 | tf_op jit(solution)/shard_map/ppermute | solution.py:248
  84.1 50.1 %all-to-all-start = ((bf16[16,48,1024]{2,1,0:T(8,128)(2,1)}), bf16[16,48,1024]{2,1,0:T(8,128)(2,1)S(1)}, u32[]{:S(2)}, u32[]{:S(2)}) async-start(bf16[16,48,1024]{2,1,0:T(8,128)(2,1)} %get-tuple-element.37), calls=%async_computation | async-start | bytes 3145728 | tf_op jit(solution)/shard_map/all_to_all | solution.py:318
  88.6 13.3 %collective-permute-start.16 = (bf16[8,32,704]{2,1,0:T(8,128)(2,1)S(1)}, bf16[8,32,704]{2,1,0:T(8,128)(2,1)S(1)}, u32[]{:S(2)}, u32[]{:S(2)}) collective-permute-start(bf16[8,32,704]{2,1,0:T(8,128)(2,1)S(1)} %get-tuple-element.39), channel_id=1, source_target_pairs={{0,16},{16,32},{32,48},{48,0},{64,80},{80,96},{96,112},{112,64},{1... | collective-permute-start | bytes 1081352 | tf_op jit(solution)/shard_map/ppermute | solution.py:248
  92.6 14.3 %collective-permute-start.18 = (bf16[8,32,704]{2,1,0:T(8,128)(2,1)S(1)}, bf16[8,32,704]{2,1,0:T(8,128)(2,1)S(1)}, u32[]{:S(2)}, u32[]{:S(2)}) collective-permute-start(bf16[8,32,704]{2,1,0:T(8,128)(2,1)S(1)} %get-tuple-element.41), channel_id=1, source_target_pairs={{0,48},{16,0},{32,16},{48,32},{64,112},{80,64},{96,80},{112,96},{1... | collective-permute-start | bytes 1081352 | tf_op jit(solution)/shard_map/ppermute | solution.py:248
  107.1 15.7 %collective-permute-start.19 = (bf16[2,32,704]{2,1,0:T(8,128)(2,1)S(1)}, bf16[2,32,704]{2,1,0:T(8,128)(2,1)S(1)}, u32[]{:S(2)}, u32[]{:S(2)}) collective-permute-start(bf16[2,32,704]{2,1,0:T(8,128)(2,1)S(1)} %get-tuple-element.43), channel_id=1, source_target_pairs={{0,128},{16,144},{32,160},{48,176},{64,192},{80,208},{96,224},{112... | collective-permute-start | bytes 270344 | tf_op jit(solution)/shard_map/ppermute | solution.py:248
  111.6 11.6 %collective-permute-start.20 = (bf16[2,32,704]{2,1,0:T(8,128)(2,1)S(1)}, bf16[2,32,704]{2,1,0:T(8,128)(2,1)S(1)}, u32[]{:S(2)}, u32[]{:S(2)}) collective-permute-start(bf16[2,32,704]{2,1,0:T(8,128)(2,1)S(1)} %get-tuple-element.44), channel_id=1, source_target_pairs={{0,256},{16,272},{32,288},{48,304},{64,320},{80,336},{96,352},{112... | collective-permute-start | bytes 270344 | tf_op jit(solution)/shard_map/ppermute | solution.py:248
  117.6 9.9 %collective-permute-start.21 = (bf16[2,32,704]{2,1,0:T(8,128)(2,1)S(1)}, bf16[2,32,704]{2,1,0:T(8,128)(2,1)S(1)}, u32[]{:S(2)}, u32[]{:S(2)}) collective-permute-start(bf16[2,32,704]{2,1,0:T(8,128)(2,1)S(1)} %get-tuple-element.45), channel_id=1, source_target_pairs={{0,384},{16,400},{32,416},{48,432},{64,448},{80,464},{96,480},{112... | collective-permute-start | bytes 270344 | tf_op jit(solution)/shard_map/ppermute | solution.py:248
  127.5 6.0 %collective-permute-start.22 = (bf16[32,704]{1,0:T(8,128)(2,1)S(1)}, bf16[32,704]{1,0:T(8,128)(2,1)S(1)}, u32[]{:S(2)}, u32[]{:S(2)}) collective-permute-start(bf16[32,704]{1,0:T(8,128)(2,1)S(1)} %get-tuple-element.47), channel_id=1, source_target_pairs={{0,64},{16,80},{32,96},{48,112},{64,0},{80,16},{96,32},{112,48},{1... | collective-permute-start | bytes 135176 | tf_op jit(solution)/shard_map/ppermute | solution.py:248
  (7 other events, 92.5 us)

commit v4 on v3

--- a/solution.py
+++ b/solution.py
@@ -13,7 +13,7 @@
 CAP = 48
 META = 8
 CHIPS = 8
-XS, YS, PAIRS = 4, 8, 4
+XS, YS, QUAD = 4, 8, 4
 MIB = 1024 * 1024
 NT = (((1,), (1,)), ((), ()))
 TN = (((0,), (0,)), ((), ()))
@@ -94,22 +94,28 @@
     return x, s
 
 
-def select_kernel(n, *refs):
-    toks, grads, (own, sib) = refs[:n], refs[n : 2 * n], refs[2 * n :]
-    me, other = neighbours()
+def select_kernel(n, which, *refs):
+    toks, grads, outs = refs[:n], refs[n : 2 * n], refs[2 * n :]
+    experts = neighbours()
     for d in range(n):
-        x, s = pick(toks[d], grads[d], [me, other])
-        for i, out in enumerate((own, sib)):
+        x, s = pick(toks[d], grads[d], [experts[i] for i in which])
+        for i, out in enumerate(outs):
             out[0, d] = x[i * CAP : (i + 1) * CAP]
             out[1, d] = s[i * CAP : (i + 1) * CAP]
 
 
-def joined(own, got, part):
-    return jnp.concatenate([r[part].reshape(-1, r.shape[-1]) for r in (own, got)], 0)
-
-
-def forward(own, got, w_gate, w_up):
-    x = joined(own, got, 0)
+def own_kernel(n, *refs):
+    blocks, weights, (own, *outs) = refs[: 2 * n], refs[2 * n : 2 * n + 3], refs[2 * n + 3 :]
+    select_kernel(n, [0], *blocks, own)
+    early_kernel(own, *weights, *outs)
+
+
+def joined(groups, part):
+    return jnp.concatenate([g[part].reshape(-1, g.shape[-1]) for g in groups], 0)
+
+
+def forward(groups, w_gate, w_up):
+    x = joined(groups, 0)
     return dot(x, w_gate[...], NT), dot(x, w_up[...], NT)
 
 
@@ -117,25 +123,25 @@
     return (gate * jax.nn.sigmoid(gate) * up).astype(BF16)
 
 
-def backward(own, got, gate, up, w_gate, w_up, w_down):
-    down = dot(joined(own, got, 1), w_down[...], NT)
+def backward(groups, gate, up, w_gate, w_up, w_down):
+    down = dot(joined(groups, 1), w_down[...], NT)
     sig = jax.nn.sigmoid(gate)
     grad_gate = (down * up * sig * (1.0 + gate * (1.0 - sig))).astype(BF16)
     grad_up = (down * (gate * sig)).astype(BF16)
     return (dot(grad_gate, w_gate[...]) + dot(grad_up, w_up[...])).astype(BF16)
 
 
-def first_kernel(own, got, w_gate, w_up, w_down, hidden, back, done):
+def early_kernel(group, w_gate, w_up, w_down, hidden, back, done):
     done[...] = jnp.zeros_like(done)
-    gate, up = forward(own, got, w_gate, w_up)
+    gate, up = forward([group], w_gate, w_up)
     hidden[...] = hidden_rows(gate, up)
-    back[...] = backward(own, got, gate, up, w_gate, w_up, w_down).reshape(back.shape)
-
-
-def weight_kernel(own, got, w_gate, w_up, own_early, got_early, hidden_early, gate, up, total, strip):
-    gate[...], up[...] = forward(own, got, w_gate, w_up)
-    s = jnp.concatenate([joined(own_early, got_early, 1), joined(own, got, 1)], 0)
-    h = jnp.concatenate([hidden_early[...], hidden_rows(gate[...], up[...])], 0)
+    back[...] = backward([group], gate, up, w_gate, w_up, w_down).reshape(back.shape)
+
+
+def weight_kernel(own, got, w_gate, w_up, own_a, got_a, hidden_a, hidden_x, gate, up, total, strip):
+    gate[...], up[...] = forward([own, got], w_gate, w_up)
+    s = joined([own_a, got_a, own, got], 1)
+    h = jnp.concatenate([hidden_a[...], hidden_x[...], hidden_rows(gate[...], up[...])], 0)
     parts, width = total.shape[0], s.shape[1]
     for i in range(4):
         cols = slice(i * width // 4, (i + 1) * width // 4)
@@ -151,13 +157,13 @@
 
 
 def last_kernel(blocks, early, *refs):
-    own, got, gate, up, w_gate, w_up, w_down, back_early, total = refs[:9]
-    back, *strips = refs[9:]
+    own, got, gate, up, w_gate, w_up, w_down, back_a, back_x, total = refs[:10]
+    back, *strips = refs[10:]
     me, other = neighbours()
-    late = backward(own, got, gate[...], up[...], w_gate, w_up, w_down)
+    late = backward([own, got], gate[...], up[...], w_gate, w_up, w_down)
     for i, d in enumerate(early):
-        back[around(me, -d)] = back_early[i]
-        back[around(other, -d)] = back_early[len(early) + i]
+        back[around(me, -d)] = back_a[i]
+        back[around(other, -d)] = back_x[i]
     for i, d in enumerate(blocks):
         back[around(me, -d)] = late[i * CAP : (i + 1) * CAP]
         j = len(blocks) + i
@@ -189,18 +195,18 @@
 
 def sum_x_kernel(*refs):
     parts, outs = refs[:XS], refs[XS:]
-    pair = lax.div(dp_place()[0], 2)
+    place = lax.rem(dp_place()[0], QUAD)
     for step, out in enumerate(outs):
-        at = lax.rem(pair + step, PAIRS)
-        for i in range(2):
-            out[i] = sum(r[2 * at + i].astype(F32) for r in parts).astype(BF16)
-
-
-def sum_pairs_kernel(*refs):
+        at = lax.rem(place + step, QUAD)
+        for quad in range(YS // QUAD):
+            out[quad] = sum(r[quad * QUAD + at].astype(F32) for r in parts).astype(BF16)
+
+
+def sum_quad_kernel(*refs):
     *parts, keep, send = refs
-    mine = lax.rem(dp_place()[0], 2)
-    keep[...] = sum(r[mine].astype(F32) for r in parts)
-    send[...] = sum(r[1 - mine].astype(F32) for r in parts).astype(BF16)
+    quad = lax.div(dp_place()[0], QUAD)
+    keep[...] = sum(r[quad].astype(F32) for r in parts)
+    send[...] = sum(r[1 - quad].astype(F32) for r in parts).astype(BF16)
 
 
 def sum_last_kernel(keep, got, out):
@@ -223,14 +229,14 @@
     ]
 
 
-def shift(pairs, inside, dx):
+def shift(quads, places, dx):
     return [
         (
-            (2 * p + i) * XS + x,
-            (2 * ((p + pairs) % PAIRS) + (i + inside) % 2) * XS + (x + dx) % XS,
+            (q * QUAD + r) * XS + x,
+            ((q + quads) % (YS // QUAD) * QUAD + (r + places) % QUAD) * XS + (x + dx) % XS,
         )
-        for p in range(PAIRS)
-        for i in range(2)
+        for q in range(YS // QUAD)
+        for r in range(QUAD)
         for x in range(XS)
     ]
 
@@ -268,34 +274,49 @@
     toks[4] = hop(toks[3], 1)
     grads[4] = hop(grads[-3], -1)
 
-    toks[-3] = hold(toks[-3], 10**10)
-
-    grads[3] = hold(grads[3], 10**10)
-
-    def select(blocks, after=()):
-        group = shape((2, len(blocks), CAP, width))
-        own, sib = call(
-            functools.partial(select_kernel, len(blocks)),
-            [group, group],
-            [toks[d] for d in blocks] + [grads[d] for d in blocks],
-            flops=8 * len(blocks) * CAP * ROWS * width,
+    def blocks(which):
+        return [toks[d] for d in which] + [grads[d] for d in which]
+
+    def select(which, experts, after):
+        return call(
+            functools.partial(select_kernel, len(which), experts),
+            [shape((2, len(which), CAP, width))] * len(experts),
+            blocks(which),
+            flops=4 * len(experts) * len(which) * CAP * ROWS * width,
             after=after,
             free=True,
         )
-        return own, hop(sib, 0, 1)
 
     early, late = [0, 1, -1, 2, -2], [3, -3, 4]
-    own_a, got_a = select(early, [toks[3], grads[-3]])
-    rows = 2 * len(early) * CAP
-    hidden_a, back_a, done = call(
-        first_kernel,
-        [shape((rows, hidden_width)), shape((2 * len(early), CAP, width)), shape((8, 128), F32)],
-        [own_a, got_a, *weights],
+    rows = len(early) * CAP
+    group = shape((2, len(early), CAP, width))
+    results = [
+        shape((rows, hidden_width)),
+        shape((len(early), CAP, width)),
+        shape((8, 128), F32),
+    ]
+    own_a, hidden_a, back_a, done = call(
+        functools.partial(own_kernel, len(early)),
+        [group, *results],
+        [*blocks(early), *weights],
         flops=10 * rows * width * hidden_width,
         limit=32,
+        after=[toks[3], grads[-3]],
         free=True,
     )
-    own_b, got_b = select(late, [done])
+    (sib_a,) = select(early, [1], [done, toks[4], grads[4]])
+    got_a = hop(sib_a, 0, 1)
+    hidden_x, back_x, _ = call(
+        early_kernel,
+        results,
+        [got_a, *weights],
+        flops=10 * rows * width * hidden_width,
+        limit=32,
+    )
+    toks[-3] = hold(toks[-3], 10**10)
+    grads[3] = hold(grads[3], 10**10)
+    own_b, sib_b = select(late, [0, 1], [done])
+    got_b = hop(sib_b, 0, 1)
     rows = 2 * len(late) * CAP
     cols = width // (XS * YS)
     strip = shape((YS, cols, hidden_width))
@@ -303,7 +324,7 @@
     gate, up, total, strip2 = call(
         weight_kernel,
         [wide, wide, shape((XS * YS, cols, hidden_width)), strip],
-        [own_b, got_b, *weights[:2], own_a, got_a, hidden_a],
+        [own_b, got_b, *weights[:2], own_a, got_a, hidden_a, hidden_x],
         flops=4 * rows * width * hidden_width + 4 * CHIPS * CAP * width * hidden_width,
         limit=24,
     )
@@ -311,7 +332,7 @@
     back, strip0, strip1, strip3 = call(
         functools.partial(last_kernel, late, early),
         [shape((2 * CHIPS, CAP, width))] + [strip] * 3,
-        [own_b, got_b, gate, up, *weights, back_a, total],
+        [own_b, got_b, gate, up, *weights, back_a, back_x, total],
         flops=6 * rows * width * hidden_width,
         limit=32,
     )
@@ -324,11 +345,11 @@
     )
 
     by_x = [strip0, dp_hop(strip1, 0, 0, 1), strip2, dp_hop(strip3, 0, 0, 3)]
-    by_y = call(sum_x_kernel, [shape((2, cols, hidden_width))] * PAIRS, by_x)
-    by_y = [by_y[0]] + [dp_hop(by_y[d], d, 0, 0) for d in range(1, PAIRS)]
+    by_y = call(sum_x_kernel, [shape((YS // QUAD, cols, hidden_width))] * QUAD, by_x)
+    by_y = [by_y[0]] + [dp_hop(by_y[d], 0, d, 0) for d in range(1, QUAD)]
     one = (cols, hidden_width)
-    keep, send = call(sum_pairs_kernel, [shape(one, F32), shape(one)], by_y)
-    (grad_down,) = call(sum_last_kernel, [shape(one, F32)], [keep, dp_hop(send, 0, 1, 0)])
+    keep, send = call(sum_quad_kernel, [shape(one, F32), shape(one)], by_y)
+    (grad_down,) = call(sum_last_kernel, [shape(one, F32)], [keep, dp_hop(send, 1, 0, 0)])
     return grad_tokens, grad_down.T[None]
 
 

time: 136 us -> 132 us (0.971)
  waiting for transfers between devices: 26 us -> 21.5 us
  local copies, waits for them, and re-layouts: 1.93 us -> 0.04 us
    ppermute x16, waiting for transfers between devices: 5.17 us -> 2.93 us  [hop(): return lax.ppermute(x, 'expert', ring(step, swap))]
    ppermute x7, waiting for transfers between devices: 20.8 us -> 18.6 us  [dp_hop(): return lax.ppermute(x, 'dp', shift(*step))]
    unnamed x14, local copies, waits for them, and re-layouts: 1.93 us -> 0.04 us
    pallas_call x9 -> x10, Pallas kernels: 14.9 us -> 15.7 us  [call(): pl.pallas_call(lambda *refs: kernel(*refs[len(after):]), out_shape=outs,...]
  transfers between devices with their start and end apart: 24 -> 24, of which waited for: 7 -> 6; matrix products, arithmetic and copies ran while one was open for 0% -> 0% of each run, Pallas kernels for 8% -> 9%
where the time goes in v4:
time: 132 us; the launch traced here: 131 us
  starting transfers between devices  90.4 us (68%)
  waiting for transfers between devices  21.5 us (16%)
  Pallas kernels  17.5 us (13%)
    ppermute x16, starting transfers between devices, hop(): return lax.ppermute(x, 'expert', ring(step, swap))  58.6 us
    ppermute x7, starting transfers between devices, dp_hop(): return lax.ppermute(x, 'dp', shift(*step))  27.3 us
    ppermute x7, waiting for transfers between devices, dp_hop(): return lax.ppermute(x, 'dp', shift(*step))  18.6 us
    pallas_call x10, Pallas kernels, call(): pl.pallas_call(lambda *refs: kernel(*refs[len(after):]), out_shape=outs,...  15.7 us
    all_to_all x1, starting transfers between devices, on_device(): lax.all_to_all(back, 'expert', split_axis=0, concat_axis=0, tiled=True)  4.57 us
    ppermute x16, waiting for transfers between devices, hop(): return lax.ppermute(x, 'expert', ring(step, swap))  2.93 us
  transfers between devices with their start and end apart: 24, of which 6 were waited for; matrix products, arithmetic and copies ran while one was open for 0% of the time, Pallas kernels for 9%

profile of v4, /device:TPU:6, one launch (start us, length us, event | category | flops | bytes accessed | tf_op | source)
XLA Modules:
  0.0 130.7 jit_solution(12388247397878829945)
XLA Ops:
  2.5 4.3 %collective-permute-start = (bf16[136,1024]{1,0:T(8,128)(2,1)}, bf16[136,1024]{1,0:T(8,128)(2,1)S(1)}, u32[]{:S(2)}, u32[]{:S(2)}) collective-permute-start(bf16[136,1024]{1,0:T(8,128)(2,1)} %get-tuple-element.26.refs_2_.refs_3_), channel_id=1, source_target_pairs={{0,2},{1,3},{2,4},{3,5},{4,6},{5,7},{6,8},{7,9},{8,10},{9,11},{10,... | collective-permute-start | bytes 835592 | tf_op jit(solution)/shard_map/ppermute | solution.py:251
  6.9 8.9 %collective-permute-start.3 = (bf16[128,1024]{1,0:T(8,128)(2,1)}, bf16[128,1024]{1,0:T(8,128)(2,1)S(1)}, u32[]{:S(2)}, u32[]{:S(2)}) collective-permute-start(bf16[128,1024]{1,0:T(8,128)(2,1)} %get-tuple-element.27.refs_7_.refs_8_), channel_id=1, source_target_pairs={{0,14},{1,15},{2,0},{3,1},{4,2},{5,3},{6,4},{7,5},{8,6},{9,7},{10,... | collective-permute-start | bytes 786440 | tf_op jit(solution)/shard_map/ppermute | solution.py:251
  17.6 5.1 %collective-permute-start.6 = (bf16[136,1024]{1,0:T(8,128)(2,1)}, bf16[136,1024]{1,0:T(8,128)(2,1)S(1)}, u32[]{:S(2)}, u32[]{:S(2)}) collective-permute-start(bf16[136,1024]{1,0:T(8,128)(2,1)} %get-tuple-element.26.refs_2_.refs_3_), channel_id=1, source_target_pairs={{0,14},{1,15},{2,0},{3,1},{4,2},{5,3},{6,4},{7,5},{8,6},{9,7},{10,... | collective-permute-start | bytes 835592 | tf_op jit(solution)/shard_map/ppermute | solution.py:251
  24.7 5.1 %collective-permute-start.4 = (bf16[128,1024]{1,0:T(8,128)(2,1)S(1)}, bf16[128,1024]{1,0:T(8,128)(2,1)S(1)}, u32[]{:S(2)}, u32[]{:S(2)}) collective-permute-start(bf16[128,1024]{1,0:T(8,128)(2,1)S(1)} %collective-permute-done.3.refs_9_.refs_10_), channel_id=1, source_target_pairs={{0,14},{1,15},{2,0},{3,1},{4,2},{5,3},{6,4},{7,5},{8,6},{9,7},{10,... | collective-permute-start | bytes 786440 | tf_op jit(solution)/shard_map/ppermute | solution.py:251
  31.8 5.1 %collective-permute-start.7 = (bf16[136,1024]{1,0:T(8,128)(2,1)S(1)}, bf16[136,1024]{1,0:T(8,128)(2,1)S(1)}, u32[]{:S(2)}, u32[]{:S(2)}) collective-permute-start(bf16[136,1024]{1,0:T(8,128)(2,1)S(1)} %collective-permute-done.6.refs_4_.refs_5_), channel_id=1, source_target_pairs={{0,14},{1,15},{2,0},{3,1},{4,2},{5,3},{6,4},{7,5},{8,6},{9,7},{10,... | collective-permute-start | bytes 835592 | tf_op jit(solution)/shard_map/ppermute | solution.py:251
  38.9 5.1 %collective-permute-start.5 = (bf16[128,1024]{1,0:T(8,128)(2,1)S(1)}, bf16[128,1024]{1,0:T(8,128)(2,1)S(1)}, u32[]{:S(2)}, u32[]{:S(2)}) collective-permute-start(bf16[128,1024]{1,0:T(8,128)(2,1)S(1)} %collective-permute-done.4.refs_11_.refs_12_), channel_id=1, source_target_pairs={{0,14},{1,15},{2,0},{3,1},{4,2},{5,3},{6,4},{7,5},{8,6},{9,7},{10,... | collective-permute-start | bytes 786440 | tf_op jit(solution)/shard_map/ppermute | solution.py:251
  46.0 5.1 %collective-permute-start.10 = (bf16[136,1024]{1,0:T(8,128)(2,1)S(1)}, bf16[136,1024]{1,0:T(8,128)(2,1)S(1)}, u32[]{:S(2)}, u32[]{:S(2)}) collective-permute-start(bf16[136,1024]{1,0:T(8,128)(2,1)S(1)} %collective-permute-done.7.refs_6_.refs_7_), channel_id=1, source_target_pairs={{0,14},{1,15},{2,0},{3,1},{4,2},{5,3},{6,4},{7,5},{8,6},{9,7},{10,... | collective-permute-start | bytes 835592 | tf_op jit(solution)/shard_map/ppermute | solution.py:251
  53.5 3.5 %collective-permute-start.11 = (bf16[136,1024]{1,0:T(8,128)(2,1)S(1)}, bf16[136,1024]{1,0:T(8,128)(2,1)S(1)}, u32[]{:S(2)}, u32[]{:S(2)}) collective-permute-start(bf16[136,1024]{1,0:T(8,128)(2,1)S(1)} %collective-permute-done.2.refs_0_.refs_1_), channel_id=1, source_target_pairs={{0,2},{1,3},{2,4},{3,5},{4,6},{5,7},{6,8},{7,9},{8,10},{9,11},{10,... | collective-permute-start | bytes 835592 | tf_op jit(solution)/shard_map/ppermute | solution.py:251
  57.1 3.2 %shard_map.96 = (bf16[2,5,48,1024]{3,2,1,0:T(8,128)(2,1)S(1)}, bf16[240,704]{1,0:T(8,128)(2,1)S(1)}, bf16[5,48,1024]{2,1,0:T(8,128)(2,1)S(1)}, f32[8,128]{1,0:T(8,128)S(1)}) custom-call(bf16[136,1024]{1,0:T(8,128)(2,1)S(1)} %collective-permute-done.2.refs_0_.refs_1_, bf16[128,1024]{1,0:T(8,128)(2,1)S(1)} %collective-permute-done.5.refs_1_.refs_5_, ...), custom_call_target="tpu_custom_call" | custom-call | tf_op jit(solution)/shard_map/pallas_call | solution.py:30
  60.3 2.9 %collective-permute-done.11.refs_3_.refs_1_ = bf16[136,1024]{1,0:T(8,128)(2,1)S(1)} collective-permute-done((bf16[136,1024]{1,0:T(8,128)(2,1)S(1)}, bf16[136,1024]{1,0:T(8,128)(2,1)S(1)}, u32[]{:S(2)}, u32[]{:S(2)}) %collective-permute-start.11) | collective-permute-done | bytes 278560 | tf_op jit(solution)/shard_map/ppermute | solution.py:251
  66.1 2.4 %collective-permute-start.14 = (bf16[2,3,48,1024]{3,2,1,0:T(8,128)(2,1)S(1)}, bf16[2,3,48,1024]{3,2,1,0:T(8,128)(2,1)S(1)}, u32[]{:S(2)}, u32[]{:S(2)}) collective-permute-start(bf16[2,3,48,1024]{3,2,1,0:T(8,128)(2,1)S(1)} %get-tuple-element.30), channel_id=1, source_target_pairs={{0,1},{1,0},{2,3},{3,2},{4,5},{5,4},{6,7},{7,6},{8,9},{9,8},{10,11... | collective-permute-start | bytes 1769480 | tf_op jit(solution)/shard_map/ppermute | solution.py:251
  68.5 3.2 %shard_map.101 = (bf16[240,704]{1,0:T(8,128)(2,1)S(1)}, bf16[5,48,1024]{2,1,0:T(8,128)(2,1)S(1)}, f32[8,128]{1,0:T(8,128)}) custom-call(bf16[2,5,48,1024]{3,2,1,0:T(8,128)(2,1)S(1)} %collective-permute-done.15.refs_0_.refs_5_, bf16[704,1024]{1,0:T(8,128)(2,1)S(1)} %bitcast.16, bf16[704,1024]{1,0:T(8,128)(2,1)S(1)} %bitcast.20, bf16[704,1024]{1,0:T(8,128)(2,1)S(1)} %bitcast.24), custom_call_target="tpu_custom_call" | custom-call | flops 1730150400 | bytes 6141952 | tf_op jit(solution)/shard_map/pallas_call | solution.py:30
  71.8 2.5 %shard_map.102 = (f32[288,704]{1,0:T(8,128)S(1)}, f32[288,704]{1,0:T(8,128)S(1)}, bf16[32,32,704]{2,1,0:T(8,128)(2,1)S(1)}, bf16[8,32,704]{2,1,0:T(8,128)(2,1)S(1)}) custom-call(bf16[2,3,48,1024]{3,2,1,0:T(8,128)(2,1)S(1)} %get-tuple-element.29.refs_0_, bf16[2,3,48,1024]{3,2,1,0:T(8,128)(2,1)S(1)} %collective-permute-done.14.refs_1_, ...), custom_call_target="tpu_custom_call" | custom-call | flops 1937768448 | bytes 10129408 | tf_op jit(solution)/shard_map/pallas_call | solution.py:30
  74.2 3.3 %collective-permute-start.17 = (bf16[8,32,704]{2,1,0:T(8,128)(2,1)S(1)}, bf16[8,32,704]{2,1,0:T(8,128)(2,1)S(1)}, u32[]{:S(2)}, u32[]{:S(2)}) collective-permute-start(bf16[8,32,704]{2,1,0:T(8,128)(2,1)S(1)} %get-tuple-element.42), channel_id=1, source_target_pairs={{0,32},{16,48},{32,0},{48,16},{64,96},{80,112},{96,64},{112,80},{1... | collective-permute-start | bytes 1081352 | tf_op jit(solution)/shard_map/ppermute | solution.py:254
  77.6 3.7 %shard_map.103 = (bf16[16,48,1024]{2,1,0:T(8,128)(2,1)}, bf16[8,32,704]{2,1,0:T(8,128)(2,1)S(1)}, bf16[8,32,704]{2,1,0:T(8,128)(2,1)S(1)}, bf16[8,32,704]{2,1,0:T(8,128)(2,1)S(1)}) custom-call(bf16[2,3,48,1024]{3,2,1,0:T(8,128)(2,1)S(1)} %get-tuple-element.29.refs_0_, bf16[2,3,48,1024]{3,2,1,0:T(8,128)(2,1)S(1)} %collective-permute-done.14.refs_1_, ...), custom_call_target="tpu_custom_call" | custom-call | flops 1245708288 | bytes 12206080 | tf_op jit(solution)/shard_map/pallas_call | solution.py:30
  81.2 4.6 %all-to-all-start = ((bf16[16,48,1024]{2,1,0:T(8,128)(2,1)}), bf16[16,48,1024]{2,1,0:T(8,128)(2,1)S(1)}, u32[]{:S(2)}, u32[]{:S(2)}) async-start(bf16[16,48,1024]{2,1,0:T(8,128)(2,1)} %get-tuple-element.39), calls=%async_computation | async-start | bytes 3145728 | tf_op jit(solution)/shard_map/all_to_all | solution.py:339
  85.8 4.0 %collective-permute-start.16 = (bf16[8,32,704]{2,1,0:T(8,128)(2,1)S(1)}, bf16[8,32,704]{2,1,0:T(8,128)(2,1)S(1)}, u32[]{:S(2)}, u32[]{:S(2)}) collective-permute-start(bf16[8,32,704]{2,1,0:T(8,128)(2,1)S(1)} %get-tuple-element.41), channel_id=1, source_target_pairs={{0,16},{16,32},{32,48},{48,0},{64,80},{80,96},{96,112},{112,64},{1... | collective-permute-start | bytes 1081352 | tf_op jit(solution)/shard_map/ppermute | solution.py:254
  91.8 7.4 %collective-permute-done.16.refs_1_ = bf16[8,32,704]{2,1,0:T(8,128)(2,1)S(1)} collective-permute-done((bf16[8,32,704]{2,1,0:T(8,128)(2,1)S(1)}, bf16[8,32,704]{2,1,0:T(8,128)(2,1)S(1)}, u32[]{:S(2)}, u32[]{:S(2)}) %collective-permute-start.16) | collective-permute-done | bytes 360480 | tf_op jit(solution)/shard_map/ppermute | solution.py:254
  99.2 4.9 %collective-permute-done.18.refs_3_ = bf16[8,32,704]{2,1,0:T(8,128)(2,1)S(1)} collective-permute-done((bf16[8,32,704]{2,1,0:T(8,128)(2,1)S(1)}, bf16[8,32,704]{2,1,0:T(8,128)(2,1)S(1)}, u32[]{:S(2)}, u32[]{:S(2)}) %collective-permute-start.18) | collective-permute-done | bytes 360480 | tf_op jit(solution)/shard_map/ppermute | solution.py:254
  104.3 3.5 %collective-permute-start.19 = (bf16[2,32,704]{2,1,0:T(8,128)(2,1)S(1)}, bf16[2,32,704]{2,1,0:T(8,128)(2,1)S(1)}, u32[]{:S(2)}, u32[]{:S(2)}) collective-permute-start(bf16[2,32,704]{2,1,0:T(8,128)(2,1)S(1)} %get-tuple-element.45), channel_id=1, source_target_pairs={{0,64},{16,80},{32,96},{48,112},{64,128},{80,144},{96,160},{112,17... | collective-permute-start | bytes 270344 | tf_op jit(solution)/shard_map/ppermute | solution.py:254
  107.8 4.5 %collective-permute-start.20 = (bf16[2,32,704]{2,1,0:T(8,128)(2,1)S(1)}, bf16[2,32,704]{2,1,0:T(8,128)(2,1)S(1)}, u32[]{:S(2)}, u32[]{:S(2)}) collective-permute-start(bf16[2,32,704]{2,1,0:T(8,128)(2,1)S(1)} %get-tuple-element.46), channel_id=1, source_target_pairs={{0,128},{16,144},{32,160},{48,176},{64,192},{80,208},{96,224},{112... | collective-permute-start | bytes 270344 | tf_op jit(solution)/shard_map/ppermute | solution.py:254
  112.3 3.3 %collective-permute-start.21 = (bf16[2,32,704]{2,1,0:T(8,128)(2,1)S(1)}, bf16[2,32,704]{2,1,0:T(8,128)(2,1)S(1)}, u32[]{:S(2)}, u32[]{:S(2)}) collective-permute-start(bf16[2,32,704]{2,1,0:T(8,128)(2,1)S(1)} %get-tuple-element.47), channel_id=1, source_target_pairs={{0,192},{16,208},{32,224},{48,240},{64,0},{80,16},{96,32},{112,48}... | collective-permute-start | bytes 270344 | tf_op jit(solution)/shard_map/ppermute | solution.py:254
  118.9 6.8 %collective-permute-start.22 = (bf16[32,704]{1,0:T(8,128)(2,1)S(1)}, bf16[32,704]{1,0:T(8,128)(2,1)S(1)}, u32[]{:S(2)}, u32[]{:S(2)}) collective-permute-start(bf16[32,704]{1,0:T(8,128)(2,1)S(1)} %get-tuple-element.49), channel_id=1, source_target_pairs={{0,256},{16,272},{32,288},{48,304},{64,320},{80,336},{96,352},{112... | collective-permute-start | bytes 135176 | tf_op jit(solution)/shard_map/ppermute | solution.py:254
  125.7 3.0 %collective-permute-done.22.refs_1_ = bf16[32,704]{1,0:T(8,128)(2,1)S(1)} collective-permute-done((bf16[32,704]{1,0:T(8,128)(2,1)S(1)}, bf16[32,704]{1,0:T(8,128)(2,1)S(1)}, u32[]{:S(2)}, u32[]{:S(2)}) %collective-permute-start.22) | collective-permute-done | bytes 45088 | tf_op jit(solution)/shard_map/ppermute | solution.py:254
  (52 shorter events, 24.1 us)
Async XLA Ops:
  2.5 20.3 %collective-permute-start = (bf16[136,1024]{1,0:T(8,128)(2,1)}, bf16[136,1024]{1,0:T(8,128)(2,1)S(1)}, u32[]{:S(2)}, u32[]{:S(2)}) collective-permute-start(bf16[136,1024]{1,0:T(8,128)(2,1)} %get-tuple-element.26.refs_2_.refs_3_), channel_id=1, source_target_pairs={{0,2},{1,3},{2,4},{3,5},{4,6},{5,7},{6,8},{7,9},{8,10},{9,11},{10,... | collective-permute-start | bytes 835592 | tf_op jit(solution)/shard_map/ppermute | solution.py:251
  6.9 17.9 %collective-permute-start.3 = (bf16[128,1024]{1,0:T(8,128)(2,1)}, bf16[128,1024]{1,0:T(8,128)(2,1)S(1)}, u32[]{:S(2)}, u32[]{:S(2)}) collective-permute-start(bf16[128,1024]{1,0:T(8,128)(2,1)} %get-tuple-element.27.refs_7_.refs_8_), channel_id=1, source_target_pairs={{0,14},{1,15},{2,0},{3,1},{4,2},{5,3},{6,4},{7,5},{8,6},{9,7},{10,... | collective-permute-start | bytes 786440 | tf_op jit(solution)/shard_map/ppermute | solution.py:251
  15.7 14.2 %collective-permute-start.8 = (bf16[128,1024]{1,0:T(8,128)(2,1)}, bf16[128,1024]{1,0:T(8,128)(2,1)S(1)}, u32[]{:S(2)}, u32[]{:S(2)}) collective-permute-start(bf16[128,1024]{1,0:T(8,128)(2,1)} %get-tuple-element.27.refs_7_.refs_8_), channel_id=1, source_target_pairs={{0,2},{1,3},{2,4},{3,5},{4,6},{5,7},{6,8},{7,9},{8,10},{9,11},{10,... | collective-permute-start | bytes 786440 | tf_op jit(solution)/shard_map/ppermute | solution.py:251
  17.6 14.2 %collective-permute-start.6 = (bf16[136,1024]{1,0:T(8,128)(2,1)}, bf16[136,1024]{1,0:T(8,128)(2,1)S(1)}, u32[]{:S(2)}, u32[]{:S(2)}) collective-permute-start(bf16[136,1024]{1,0:T(8,128)(2,1)} %get-tuple-element.26.refs_2_.refs_3_), channel_id=1, source_target_pairs={{0,14},{1,15},{2,0},{3,1},{4,2},{5,3},{6,4},{7,5},{8,6},{9,7},{10,... | collective-permute-start | bytes 835592 | tf_op jit(solution)/shard_map/ppermute | solution.py:251
  22.8 14.2 %collective-permute-start.1 = (bf16[136,1024]{1,0:T(8,128)(2,1)S(1)}, bf16[136,1024]{1,0:T(8,128)(2,1)S(1)}, u32[]{:S(2)}, u32[]{:S(2)}) collective-permute-start(bf16[136,1024]{1,0:T(8,128)(2,1)S(1)} %collective-permute-done.refs_3_.refs_4_), channel_id=1, source_target_pairs={{0,2},{1,3},{2,4},{3,5},{4,6},{5,7},{6,8},{7,9},{8,10},{9,11},{10,... | collective-permute-start | bytes 835592 | tf_op jit(solution)/shard_map/ppermute | solution.py:251
  24.7 14.2 %collective-permute-start.4 = (bf16[128,1024]{1,0:T(8,128)(2,1)S(1)}, bf16[128,1024]{1,0:T(8,128)(2,1)S(1)}, u32[]{:S(2)}, u32[]{:S(2)}) collective-permute-start(bf16[128,1024]{1,0:T(8,128)(2,1)S(1)} %collective-permute-done.3.refs_9_.refs_10_), channel_id=1, source_target_pairs={{0,14},{1,15},{2,0},{3,1},{4,2},{5,3},{6,4},{7,5},{8,6},{9,7},{10,... | collective-permute-start | bytes 786440 | tf_op jit(solution)/shard_map/ppermute | solution.py:251
  29.9 14.2 %collective-permute-start.9 = (bf16[128,1024]{1,0:T(8,128)(2,1)S(1)}, bf16[128,1024]{1,0:T(8,128)(2,1)S(1)}, u32[]{:S(2)}, u32[]{:S(2)}) collective-permute-start(bf16[128,1024]{1,0:T(8,128)(2,1)S(1)} %collective-permute-done.8.refs_8_.refs_9_), channel_id=1, source_target_pairs={{0,2},{1,3},{2,4},{3,5},{4,6},{5,7},{6,8},{7,9},{8,10},{9,11},{10,... | collective-permute-start | bytes 786440 | tf_op jit(solution)/shard_map/ppermute | solution.py:251
  31.8 14.2 %collective-permute-start.7 = (bf16[136,1024]{1,0:T(8,128)(2,1)S(1)}, bf16[136,1024]{1,0:T(8,128)(2,1)S(1)}, u32[]{:S(2)}, u32[]{:S(2)}) collective-permute-start(bf16[136,1024]{1,0:T(8,128)(2,1)S(1)} %collective-permute-done.6.refs_4_.refs_5_), channel_id=1, source_target_pairs={{0,14},{1,15},{2,0},{3,1},{4,2},{5,3},{6,4},{7,5},{8,6},{9,7},{10,... | collective-permute-start | bytes 835592 | tf_op jit(solution)/shard_map/ppermute | solution.py:251
  37.0 16.5 %collective-permute-start.2 = (bf16[136,1024]{1,0:T(8,128)(2,1)S(1)}, bf16[136,1024]{1,0:T(8,128)(2,1)S(1)}, u32[]{:S(2)}, u32[]{:S(2)}) collective-permute-start(bf16[136,1024]{1,0:T(8,128)(2,1)S(1)} %collective-permute-done.1.refs_5_.refs_6_), channel_id=1, source_target_pairs={{0,2},{1,3},{2,4},{3,5},{4,6},{5,7},{6,8},{7,9},{8,10},{9,11},{10,... | collective-permute-start | bytes 835592 | tf_op jit(solution)/shard_map/ppermute | solution.py:251
  38.9 12.2 %collective-permute-start.5 = (bf16[128,1024]{1,0:T(8,128)(2,1)S(1)}, bf16[128,1024]{1,0:T(8,128)(2,1)S(1)}, u32[]{:S(2)}, u32[]{:S(2)}) collective-permute-start(bf16[128,1024]{1,0:T(8,128)(2,1)S(1)} %collective-permute-done.4.refs_11_.refs_12_), channel_id=1, source_target_pairs={{0,14},{1,15},{2,0},{3,1},{4,2},{5,3},{6,4},{7,5},{8,6},{9,7},{10,... | collective-permute-start | bytes 786440 | tf_op jit(solution)/shard_map/ppermute | solution.py:251
  44.1 13.0 %collective-permute-start.12 = (bf16[128,1024]{1,0:T(8,128)(2,1)S(1)}, bf16[128,1024]{1,0:T(8,128)(2,1)S(1)}, u32[]{:S(2)}, u32[]{:S(2)}) collective-permute-start(bf16[128,1024]{1,0:T(8,128)(2,1)S(1)} %collective-permute-done.9.refs_10_.refs_11_), channel_id=1, source_target_pairs={{0,2},{1,3},{2,4},{3,5},{4,6},{5,7},{6,8},{7,9},{8,10},{9,11},{10,... | collective-permute-start | bytes 786440 | tf_op jit(solution)/shard_map/ppermute | solution.py:251
  46.0 19.6 %collective-permute-start.10 = (bf16[136,1024]{1,0:T(8,128)(2,1)S(1)}, bf16[136,1024]{1,0:T(8,128)(2,1)S(1)}, u32[]{:S(2)}, u32[]{:S(2)}) collective-permute-start(bf16[136,1024]{1,0:T(8,128)(2,1)S(1)} %collective-permute-done.7.refs_6_.refs_7_), channel_id=1, source_target_pairs={{0,14},{1,15},{2,0},{3,1},{4,2},{5,3},{6,4},{7,5},{8,6},{9,7},{10,... | collective-permute-start | bytes 835592 | tf_op jit(solution)/shard_map/ppermute | solution.py:251
  51.2 9.1 %collective-permute-start.13 = (bf16[128,1024]{1,0:T(8,128)(2,1)S(1)}, bf16[128,1024]{1,0:T(8,128)(2,1)S(1)}, u32[]{:S(2)}, u32[]{:S(2)}) collective-permute-start(bf16[128,1024]{1,0:T(8,128)(2,1)S(1)} %collective-permute-done.5.refs_1_.refs_5_), channel_id=1, source_target_pairs={{0,14},{1,15},{2,0},{3,1},{4,2},{5,3},{6,4},{7,5},{8,6},{9,7},{10,... | collective-permute-start | bytes 786440 | tf_op jit(solution)/shard_map/ppermute | solution.py:251
  53.5 9.7 %collective-permute-start.11 = (bf16[136,1024]{1,0:T(8,128)(2,1)S(1)}, bf16[136,1024]{1,0:T(8,128)(2,1)S(1)}, u32[]{:S(2)}, u32[]{:S(2)}) collective-permute-start(bf16[136,1024]{1,0:T(8,128)(2,1)S(1)} %collective-permute-done.2.refs_0_.refs_1_), channel_id=1, source_target_pairs={{0,2},{1,3},{2,4},{3,5},{4,6},{5,7},{6,8},{7,9},{8,10},{9,11},{10,... | collective-permute-start | bytes 835592 | tf_op jit(solution)/shard_map/ppermute | solution.py:251
  63.7 4.8 %collective-permute-start.15 = (bf16[2,5,48,1024]{3,2,1,0:T(8,128)(2,1)S(1)}, bf16[2,5,48,1024]{3,2,1,0:T(8,128)(2,1)S(1)}, u32[]{:S(2)}, u32[]{:S(2)}) collective-permute-start(bf16[2,5,48,1024]{3,2,1,0:T(8,128)(2,1)S(1)} %shard_map.100), channel_id=1, source_target_pairs={{0,1},{1,0},{2,3},{3,2},{4,5},{5,4},{6,7},{7,6},{8,9},{9,8},{10,11... | collective-permute-start | bytes 2949128 | tf_op jit(solution)/shard_map/ppermute | solution.py:251
  66.1 5.7 %collective-permute-start.14 = (bf16[2,3,48,1024]{3,2,1,0:T(8,128)(2,1)S(1)}, bf16[2,3,48,1024]{3,2,1,0:T(8,128)(2,1)S(1)}, u32[]{:S(2)}, u32[]{:S(2)}) collective-permute-start(bf16[2,3,48,1024]{3,2,1,0:T(8,128)(2,1)S(1)} %get-tuple-element.30), channel_id=1, source_target_pairs={{0,1},{1,0},{2,3},{3,2},{4,5},{5,4},{6,7},{7,6},{8,9},{9,8},{10,11... | collective-permute-start | bytes 1769480 | tf_op jit(solution)/shard_map/ppermute | solution.py:251
  74.2 17.5 %collective-permute-start.17 = (bf16[8,32,704]{2,1,0:T(8,128)(2,1)S(1)}, bf16[8,32,704]{2,1,0:T(8,128)(2,1)S(1)}, u32[]{:S(2)}, u32[]{:S(2)}) collective-permute-start(bf16[8,32,704]{2,1,0:T(8,128)(2,1)S(1)} %get-tuple-element.42), channel_id=1, source_target_pairs={{0,32},{16,48},{32,0},{48,16},{64,96},{80,112},{96,64},{112,80},{1... | collective-permute-start | bytes 1081352 | tf_op jit(solution)/shard_map/ppermute | solution.py:254
  81.2 48.2 %all-to-all-start = ((bf16[16,48,1024]{2,1,0:T(8,128)(2,1)}), bf16[16,48,1024]{2,1,0:T(8,128)(2,1)S(1)}, u32[]{:S(2)}, u32[]{:S(2)}) async-start(bf16[16,48,1024]{2,1,0:T(8,128)(2,1)} %get-tuple-element.39), calls=%async_computation | async-start | bytes 3145728 | tf_op jit(solution)/shard_map/all_to_all | solution.py:339
  85.8 13.3 %collective-permute-start.16 = (bf16[8,32,704]{2,1,0:T(8,128)(2,1)S(1)}, bf16[8,32,704]{2,1,0:T(8,128)(2,1)S(1)}, u32[]{:S(2)}, u32[]{:S(2)}) collective-permute-start(bf16[8,32,704]{2,1,0:T(8,128)(2,1)S(1)} %get-tuple-element.41), channel_id=1, source_target_pairs={{0,16},{16,32},{32,48},{48,0},{64,80},{80,96},{96,112},{112,64},{1... | collective-permute-start | bytes 1081352 | tf_op jit(solution)/shard_map/ppermute | solution.py:254
  89.8 14.3 %collective-permute-start.18 = (bf16[8,32,704]{2,1,0:T(8,128)(2,1)S(1)}, bf16[8,32,704]{2,1,0:T(8,128)(2,1)S(1)}, u32[]{:S(2)}, u32[]{:S(2)}) collective-permute-start(bf16[8,32,704]{2,1,0:T(8,128)(2,1)S(1)} %get-tuple-element.43), channel_id=1, source_target_pairs={{0,48},{16,0},{32,16},{48,32},{64,112},{80,64},{96,80},{112,96},{1... | collective-permute-start | bytes 1081352 | tf_op jit(solution)/shard_map/ppermute | solution.py:254
  104.3 11.3 %collective-permute-start.19 = (bf16[2,32,704]{2,1,0:T(8,128)(2,1)S(1)}, bf16[2,32,704]{2,1,0:T(8,128)(2,1)S(1)}, u32[]{:S(2)}, u32[]{:S(2)}) collective-permute-start(bf16[2,32,704]{2,1,0:T(8,128)(2,1)S(1)} %get-tuple-element.45), channel_id=1, source_target_pairs={{0,64},{16,80},{32,96},{48,112},{64,128},{80,144},{96,160},{112,17... | collective-permute-start | bytes 270344 | tf_op jit(solution)/shard_map/ppermute | solution.py:254
  107.8 9.5 %collective-permute-start.20 = (bf16[2,32,704]{2,1,0:T(8,128)(2,1)S(1)}, bf16[2,32,704]{2,1,0:T(8,128)(2,1)S(1)}, u32[]{:S(2)}, u32[]{:S(2)}) collective-permute-start(bf16[2,32,704]{2,1,0:T(8,128)(2,1)S(1)} %get-tuple-element.46), channel_id=1, source_target_pairs={{0,128},{16,144},{32,160},{48,176},{64,192},{80,208},{96,224},{112... | collective-permute-start | bytes 270344 | tf_op jit(solution)/shard_map/ppermute | solution.py:254
  112.3 6.5 %collective-permute-start.21 = (bf16[2,32,704]{2,1,0:T(8,128)(2,1)S(1)}, bf16[2,32,704]{2,1,0:T(8,128)(2,1)S(1)}, u32[]{:S(2)}, u32[]{:S(2)}) collective-permute-start(bf16[2,32,704]{2,1,0:T(8,128)(2,1)S(1)} %get-tuple-element.47), channel_id=1, source_target_pairs={{0,192},{16,208},{32,224},{48,240},{64,0},{80,16},{96,32},{112,48}... | collective-permute-start | bytes 270344 | tf_op jit(solution)/shard_map/ppermute | solution.py:254
  118.9 9.9 %collective-permute-start.22 = (bf16[32,704]{1,0:T(8,128)(2,1)S(1)}, bf16[32,704]{1,0:T(8,128)(2,1)S(1)}, u32[]{:S(2)}, u32[]{:S(2)}) collective-permute-start(bf16[32,704]{1,0:T(8,128)(2,1)S(1)} %get-tuple-element.49), channel_id=1, source_target_pairs={{0,256},{16,272},{32,288},{48,304},{64,320},{80,336},{96,352},{112... | collective-permute-start | bytes 135176 | tf_op jit(solution)/shard_map/ppermute | solution.py:254
  (7 other events, 326.5 us)

commit v5 on v4

--- a/solution.py
+++ b/solution.py
@@ -151,7 +151,7 @@
 
 
 def take_strip(total, step, out):
-    at = lax.rem(dp_place()[1] + step, XS)
+    at = lax.bitwise_xor(dp_place()[1], step)
     for y in range(YS):
         out[y] = total[y * XS + at]
 
@@ -213,7 +213,8 @@
     out[...] = keep[...] + got[...].astype(F32)
 
 
-def combine_kernel(ids, slots, came, out):
+def combine_kernel(ids, slots, came, out, done):
+    done[...] = jnp.zeros_like(done)
     spread = jnp.zeros((came.shape[0], ROWS), F32)
     row = lax.broadcasted_iota(jnp.int32, spread.shape, 0)
     for k in range(ids.shape[0]):
@@ -229,12 +230,13 @@
     ]
 
 
-def shift(quads, places, dx):
+def along_x(bits):
+    return [(y * XS + x, y * XS + (x ^ bits)) for y in range(YS) for x in range(XS)]
+
+
+def along_y(quads, places):
     return [
-        (
-            (q * QUAD + r) * XS + x,
-            ((q + quads) % (YS // QUAD) * QUAD + (r + places) % QUAD) * XS + (x + dx) % XS,
-        )
+        ((q * QUAD + r) * XS + x, ((q + quads) % (YS // QUAD) * QUAD + (r + places) % QUAD) * XS + x)
         for q in range(YS // QUAD)
         for r in range(QUAD)
         for x in range(XS)
@@ -250,8 +252,8 @@
     def hop(x, step, swap=0):
         return lax.ppermute(x, "expert", ring(step, swap))
 
-    def dp_hop(x, *step):
-        return lax.ppermute(x, "dp", shift(*step))
+    def dp_hop(x, pairs):
+        return lax.ppermute(x, "dp", pairs)
 
     toks, grads = {}, {}
     toks[0], grads[0] = pl.pallas_call(
@@ -328,7 +330,7 @@
         flops=4 * rows * width * hidden_width + 4 * CHIPS * CAP * width * hidden_width,
         limit=24,
     )
-    strip2 = hold(dp_hop(strip2, 0, 0, 2))
+    strip2 = hold(dp_hop(strip2, along_x(2)))
     back, strip0, strip1, strip3 = call(
         functools.partial(last_kernel, late, early),
         [shape((2 * CHIPS, CAP, width))] + [strip] * 3,
@@ -337,19 +339,24 @@
         limit=32,
     )
     came = lax.all_to_all(back, "expert", split_axis=0, concat_axis=0, tiled=True)
-    (grad_tokens,) = call(
+    grad_tokens, combined = call(
         combine_kernel,
-        [shape((ROWS, width))],
+        [shape((ROWS, width)), shape((8, 128), F32)],
         [ids, slots, came.reshape(2 * CHIPS * CAP, width)],
         flops=2 * 2 * CHIPS * CAP * width * ROWS,
     )
 
-    by_x = [strip0, dp_hop(strip1, 0, 0, 1), strip2, dp_hop(strip3, 0, 0, 3)]
+    by_x = [strip0, dp_hop(strip1, along_x(1)), strip2, dp_hop(strip3, along_x(3))]
     by_y = call(sum_x_kernel, [shape((YS // QUAD, cols, hidden_width))] * QUAD, by_x)
-    by_y = [by_y[0]] + [dp_hop(by_y[d], 0, d, 0) for d in range(1, QUAD)]
+    by_y = [by_y[0]] + [dp_hop(by_y[d], along_y(0, d)) for d in range(1, QUAD)]
     one = (cols, hidden_width)
     keep, send = call(sum_quad_kernel, [shape(one, F32), shape(one)], by_y)
-    (grad_down,) = call(sum_last_kernel, [shape(one, F32)], [keep, dp_hop(send, 1, 0, 0)])
+    (grad_down,) = call(
+        sum_last_kernel,
+        [shape(one, F32)],
+        [keep, dp_hop(send, along_y(1, 0))],
+        after=[combined],
+    )
     return grad_tokens, grad_down.T[None]
 
 

time: 132 us -> 131 us (level)
  the two profiles are of different devices: /device:TPU:6 before, /device:TPU:56 now
where the time goes in v5:
time: 131 us; the launch traced here: 130 us
  starting transfers between devices  86.6 us (66%)
  waiting for transfers between devices  24.8 us (19%)
  Pallas kernels  17.4 us (13%)
    ppermute x16, starting transfers between devices, hop(): return lax.ppermute(x, 'expert', ring(step, swap))  58.6 us
    ppermute x7, starting transfers between devices, dp_hop(): return lax.ppermute(x, 'dp', pairs)  23.5 us
    ppermute x7, waiting for transfers between devices, dp_hop(): return lax.ppermute(x, 'dp', pairs)  19.8 us
    pallas_call x10, Pallas kernels, call(): pl.pallas_call(lambda *refs: kernel(*refs[len(after):]), out_shape=outs,...  15.6 us
    all_to_all x1, starting transfers between devices, on_device(): lax.all_to_all(back, 'expert', split_axis=0, concat_axis=0, tiled=True)  4.57 us
    ppermute x16, waiting for transfers between devices, hop(): return lax.ppermute(x, 'expert', ring(step, swap))  2.94 us
  transfers between devices with their start and end apart: 24, of which 7 were waited for; matrix products, arithmetic and copies ran while one was open for 0% of the time, Pallas kernels for 10%

profile of v5, /device:TPU:56, one launch (start us, length us, event | category | flops | bytes accessed | tf_op | source)
XLA Modules:
  0.0 130.0 jit_solution(11380781209317924352)
XLA Ops:
  2.5 4.3 %collective-permute-start = (bf16[136,1024]{1,0:T(8,128)(2,1)}, bf16[136,1024]{1,0:T(8,128)(2,1)S(1)}, u32[]{:S(2)}, u32[]{:S(2)}) collective-permute-start(bf16[136,1024]{1,0:T(8,128)(2,1)} %get-tuple-element.28.refs_2_.refs_3_), channel_id=1, source_target_pairs={{0,2},{1,3},{2,4},{3,5},{4,6},{5,7},{6,8},{7,9},{8,10},{9,11},{10,... | collective-permute-start | bytes 835592 | tf_op jit(solution)/shard_map/ppermute | solution.py:253
  6.9 8.9 %collective-permute-start.3 = (bf16[128,1024]{1,0:T(8,128)(2,1)}, bf16[128,1024]{1,0:T(8,128)(2,1)S(1)}, u32[]{:S(2)}, u32[]{:S(2)}) collective-permute-start(bf16[128,1024]{1,0:T(8,128)(2,1)} %get-tuple-element.29.refs_7_.refs_8_), channel_id=1, source_target_pairs={{0,14},{1,15},{2,0},{3,1},{4,2},{5,3},{6,4},{7,5},{8,6},{9,7},{10,... | collective-permute-start | bytes 786440 | tf_op jit(solution)/shard_map/ppermute | solution.py:253
  17.6 5.1 %collective-permute-start.6 = (bf16[136,1024]{1,0:T(8,128)(2,1)}, bf16[136,1024]{1,0:T(8,128)(2,1)S(1)}, u32[]{:S(2)}, u32[]{:S(2)}) collective-permute-start(bf16[136,1024]{1,0:T(8,128)(2,1)} %get-tuple-element.28.refs_2_.refs_3_), channel_id=1, source_target_pairs={{0,14},{1,15},{2,0},{3,1},{4,2},{5,3},{6,4},{7,5},{8,6},{9,7},{10,... | collective-permute-start | bytes 835592 | tf_op jit(solution)/shard_map/ppermute | solution.py:253
  24.7 5.1 %collective-permute-start.4 = (bf16[128,1024]{1,0:T(8,128)(2,1)S(1)}, bf16[128,1024]{1,0:T(8,128)(2,1)S(1)}, u32[]{:S(2)}, u32[]{:S(2)}) collective-permute-start(bf16[128,1024]{1,0:T(8,128)(2,1)S(1)} %collective-permute-done.3.refs_9_.refs_10_), channel_id=1, source_target_pairs={{0,14},{1,15},{2,0},{3,1},{4,2},{5,3},{6,4},{7,5},{8,6},{9,7},{10,... | collective-permute-start | bytes 786440 | tf_op jit(solution)/shard_map/ppermute | solution.py:253
  31.8 5.1 %collective-permute-start.7 = (bf16[136,1024]{1,0:T(8,128)(2,1)S(1)}, bf16[136,1024]{1,0:T(8,128)(2,1)S(1)}, u32[]{:S(2)}, u32[]{:S(2)}) collective-permute-start(bf16[136,1024]{1,0:T(8,128)(2,1)S(1)} %collective-permute-done.6.refs_4_.refs_5_), channel_id=1, source_target_pairs={{0,14},{1,15},{2,0},{3,1},{4,2},{5,3},{6,4},{7,5},{8,6},{9,7},{10,... | collective-permute-start | bytes 835592 | tf_op jit(solution)/shard_map/ppermute | solution.py:253
  38.9 5.1 %collective-permute-start.5 = (bf16[128,1024]{1,0:T(8,128)(2,1)S(1)}, bf16[128,1024]{1,0:T(8,128)(2,1)S(1)}, u32[]{:S(2)}, u32[]{:S(2)}) collective-permute-start(bf16[128,1024]{1,0:T(8,128)(2,1)S(1)} %collective-permute-done.4.refs_11_.refs_12_), channel_id=1, source_target_pairs={{0,14},{1,15},{2,0},{3,1},{4,2},{5,3},{6,4},{7,5},{8,6},{9,7},{10,... | collective-permute-start | bytes 786440 | tf_op jit(solution)/shard_map/ppermute | solution.py:253
  46.0 5.1 %collective-permute-start.10 = (bf16[136,1024]{1,0:T(8,128)(2,1)S(1)}, bf16[136,1024]{1,0:T(8,128)(2,1)S(1)}, u32[]{:S(2)}, u32[]{:S(2)}) collective-permute-start(bf16[136,1024]{1,0:T(8,128)(2,1)S(1)} %collective-permute-done.7.refs_6_.refs_7_), channel_id=1, source_target_pairs={{0,14},{1,15},{2,0},{3,1},{4,2},{5,3},{6,4},{7,5},{8,6},{9,7},{10,... | collective-permute-start | bytes 835592 | tf_op jit(solution)/shard_map/ppermute | solution.py:253
  53.5 3.5 %collective-permute-start.11 = (bf16[136,1024]{1,0:T(8,128)(2,1)S(1)}, bf16[136,1024]{1,0:T(8,128)(2,1)S(1)}, u32[]{:S(2)}, u32[]{:S(2)}) collective-permute-start(bf16[136,1024]{1,0:T(8,128)(2,1)S(1)} %collective-permute-done.2.refs_0_.refs_1_), channel_id=1, source_target_pairs={{0,2},{1,3},{2,4},{3,5},{4,6},{5,7},{6,8},{7,9},{8,10},{9,11},{10,... | collective-permute-start | bytes 835592 | tf_op jit(solution)/shard_map/ppermute | solution.py:253
  57.1 3.2 %shard_map.96 = (bf16[2,5,48,1024]{3,2,1,0:T(8,128)(2,1)S(1)}, bf16[240,704]{1,0:T(8,128)(2,1)S(1)}, bf16[5,48,1024]{2,1,0:T(8,128)(2,1)S(1)}, f32[8,128]{1,0:T(8,128)S(1)}) custom-call(bf16[136,1024]{1,0:T(8,128)(2,1)S(1)} %collective-permute-done.2.refs_0_.refs_1_, bf16[128,1024]{1,0:T(8,128)(2,1)S(1)} %collective-permute-done.5.refs_1_.refs_5_, ...), custom_call_target="tpu_custom_call" | custom-call | tf_op jit(solution)/shard_map/pallas_call | solution.py:30
  60.3 2.9 %collective-permute-done.11.refs_3_.refs_1_ = bf16[136,1024]{1,0:T(8,128)(2,1)S(1)} collective-permute-done((bf16[136,1024]{1,0:T(8,128)(2,1)S(1)}, bf16[136,1024]{1,0:T(8,128)(2,1)S(1)}, u32[]{:S(2)}, u32[]{:S(2)}) %collective-permute-start.11) | collective-permute-done | bytes 278560 | tf_op jit(solution)/shard_map/ppermute | solution.py:253
  66.1 2.4 %collective-permute-start.14 = (bf16[2,3,48,1024]{3,2,1,0:T(8,128)(2,1)S(1)}, bf16[2,3,48,1024]{3,2,1,0:T(8,128)(2,1)S(1)}, u32[]{:S(2)}, u32[]{:S(2)}) collective-permute-start(bf16[2,3,48,1024]{3,2,1,0:T(8,128)(2,1)S(1)} %get-tuple-element.32), channel_id=1, source_target_pairs={{0,1},{1,0},{2,3},{3,2},{4,5},{5,4},{6,7},{7,6},{8,9},{9,8},{10,11... | collective-permute-start | bytes 1769480 | tf_op jit(solution)/shard_map/ppermute | solution.py:253
  68.5 3.2 %shard_map.101 = (bf16[240,704]{1,0:T(8,128)(2,1)S(1)}, bf16[5,48,1024]{2,1,0:T(8,128)(2,1)S(1)}, f32[8,128]{1,0:T(8,128)}) custom-call(bf16[2,5,48,1024]{3,2,1,0:T(8,128)(2,1)S(1)} %collective-permute-done.15.refs_0_.refs_5_, bf16[704,1024]{1,0:T(8,128)(2,1)S(1)} %bitcast.16, bf16[704,1024]{1,0:T(8,128)(2,1)S(1)} %bitcast.20, bf16[704,1024]{1,0:T(8,128)(2,1)S(1)} %bitcast.24), custom_call_target="tpu_custom_call" | custom-call | flops 1730150400 | bytes 6141952 | tf_op jit(solution)/shard_map/pallas_call | solution.py:30
  74.1 4.9 %collective-permute-start.17 = (bf16[8,32,704]{2,1,0:T(8,128)(2,1)S(1)}, bf16[8,32,704]{2,1,0:T(8,128)(2,1)S(1)}, u32[]{:S(2)}, u32[]{:S(2)}) collective-permute-start(bf16[8,32,704]{2,1,0:T(8,128)(2,1)S(1)} %get-tuple-element.46), channel_id=1, source_target_pairs={{0,32},{16,48},{32,0},{48,16},{64,96},{80,112},{96,64},{112,80},{1... | collective-permute-start | bytes 1081352 | tf_op jit(solution)/shard_map/ppermute | solution.py:256
  79.1 3.7 %shard_map.103 = (bf16[16,48,1024]{2,1,0:T(8,128)(2,1)}, bf16[8,32,704]{2,1,0:T(8,128)(2,1)S(1)}, bf16[8,32,704]{2,1,0:T(8,128)(2,1)S(1)}, bf16[8,32,704]{2,1,0:T(8,128)(2,1)S(1)}) custom-call(bf16[2,3,48,1024]{3,2,1,0:T(8,128)(2,1)S(1)} %get-tuple-element.31.refs_0_, bf16[2,3,48,1024]{3,2,1,0:T(8,128)(2,1)S(1)} %collective-permute-done.14.refs_1_, ...), custom_call_target="tpu_custom_call" | custom-call | flops 1245708288 | bytes 12206080 | tf_op jit(solution)/shard_map/pallas_call | solution.py:30
  82.8 4.6 %all-to-all-start = ((bf16[16,48,1024]{2,1,0:T(8,128)(2,1)}), bf16[16,48,1024]{2,1,0:T(8,128)(2,1)S(1)}, u32[]{:S(2)}, u32[]{:S(2)}) async-start(bf16[16,48,1024]{2,1,0:T(8,128)(2,1)} %get-tuple-element.41), calls=%async_computation | async-start | bytes 3145728 | tf_op jit(solution)/shard_map/all_to_all | solution.py:341
  87.4 2.5 %collective-permute-start.16 = (bf16[8,32,704]{2,1,0:T(8,128)(2,1)S(1)}, bf16[8,32,704]{2,1,0:T(8,128)(2,1)S(1)}, u32[]{:S(2)}, u32[]{:S(2)}) collective-permute-start(bf16[8,32,704]{2,1,0:T(8,128)(2,1)S(1)} %get-tuple-element.45), channel_id=1, source_target_pairs={{0,16},{16,0},{32,48},{48,32},{64,80},{80,64},{96,112},{112,96},{1... | collective-permute-start | bytes 1081352 | tf_op jit(solution)/shard_map/ppermute | solution.py:256
  89.9 2.5 %collective-permute-start.18 = (bf16[8,32,704]{2,1,0:T(8,128)(2,1)S(1)}, bf16[8,32,704]{2,1,0:T(8,128)(2,1)S(1)}, u32[]{:S(2)}, u32[]{:S(2)}) collective-permute-start(bf16[8,32,704]{2,1,0:T(8,128)(2,1)S(1)} %get-tuple-element.47), channel_id=1, source_target_pairs={{0,48},{16,32},{32,16},{48,0},{64,112},{80,96},{96,80},{112,64},{1... | collective-permute-start | bytes 1081352 | tf_op jit(solution)/shard_map/ppermute | solution.py:256
  92.4 8.3 %collective-permute-done.16.refs_1_ = bf16[8,32,704]{2,1,0:T(8,128)(2,1)S(1)} collective-permute-done((bf16[8,32,704]{2,1,0:T(8,128)(2,1)S(1)}, bf16[8,32,704]{2,1,0:T(8,128)(2,1)S(1)}, u32[]{:S(2)}, u32[]{:S(2)}) %collective-permute-start.16) | collective-permute-done | bytes 360480 | tf_op jit(solution)/shard_map/ppermute | solution.py:256
  100.7 3.4 %collective-permute-done.18.refs_3_ = bf16[8,32,704]{2,1,0:T(8,128)(2,1)S(1)} collective-permute-done((bf16[8,32,704]{2,1,0:T(8,128)(2,1)S(1)}, bf16[8,32,704]{2,1,0:T(8,128)(2,1)S(1)}, u32[]{:S(2)}, u32[]{:S(2)}) %collective-permute-start.18) | collective-permute-done | bytes 360480 | tf_op jit(solution)/shard_map/ppermute | solution.py:256
  104.3 4.8 %collective-permute-start.19 = (bf16[2,32,704]{2,1,0:T(8,128)(2,1)S(1)}, bf16[2,32,704]{2,1,0:T(8,128)(2,1)S(1)}, u32[]{:S(2)}, u32[]{:S(2)}) collective-permute-start(bf16[2,32,704]{2,1,0:T(8,128)(2,1)S(1)} %get-tuple-element.49), channel_id=1, source_target_pairs={{0,64},{16,80},{32,96},{48,112},{64,128},{80,144},{96,160},{112,17... | collective-permute-start | bytes 270344 | tf_op jit(solution)/shard_map/ppermute | solution.py:256
  111.1 3.1 %collective-permute-start.21 = (bf16[2,32,704]{2,1,0:T(8,128)(2,1)S(1)}, bf16[2,32,704]{2,1,0:T(8,128)(2,1)S(1)}, u32[]{:S(2)}, u32[]{:S(2)}) collective-permute-start(bf16[2,32,704]{2,1,0:T(8,128)(2,1)S(1)} %get-tuple-element.51), channel_id=1, source_target_pairs={{0,192},{16,208},{32,224},{48,240},{64,0},{80,16},{96,32},{112,48}... | collective-permute-start | bytes 270344 | tf_op jit(solution)/shard_map/ppermute | solution.py:256
  114.3 3.6 %collective-permute-done.20.refs_2_ = bf16[2,32,704]{2,1,0:T(8,128)(2,1)S(1)} collective-permute-done((bf16[2,32,704]{2,1,0:T(8,128)(2,1)S(1)}, bf16[2,32,704]{2,1,0:T(8,128)(2,1)S(1)}, u32[]{:S(2)}, u32[]{:S(2)}) %collective-permute-start.20) | collective-permute-done | bytes 90144 | tf_op jit(solution)/shard_map/ppermute | solution.py:256
  119.5 3.7 %collective-permute-start.22 = (bf16[32,704]{1,0:T(8,128)(2,1)S(1)}, bf16[32,704]{1,0:T(8,128)(2,1)S(1)}, u32[]{:S(2)}, u32[]{:S(2)}) collective-permute-start(bf16[32,704]{1,0:T(8,128)(2,1)S(1)} %get-tuple-element.53), channel_id=1, source_target_pairs={{0,256},{16,272},{32,288},{48,304},{64,320},{80,336},{96,352},{112... | collective-permute-start | bytes 135176 | tf_op jit(solution)/shard_map/ppermute | solution.py:256
  126.5 2.9 %collective-permute-done.22.refs_2_ = bf16[32,704]{1,0:T(8,128)(2,1)S(1)} collective-permute-done((bf16[32,704]{1,0:T(8,128)(2,1)S(1)}, bf16[32,704]{1,0:T(8,128)(2,1)S(1)}, u32[]{:S(2)}, u32[]{:S(2)}) %collective-permute-start.22) | collective-permute-done | bytes 45088 | tf_op jit(solution)/shard_map/ppermute | solution.py:256
  (52 shorter events, 26.9 us)
Async XLA Ops:
  2.5 20.3 %collective-permute-start = (bf16[136,1024]{1,0:T(8,128)(2,1)}, bf16[136,1024]{1,0:T(8,128)(2,1)S(1)}, u32[]{:S(2)}, u32[]{:S(2)}) collective-permute-start(bf16[136,1024]{1,0:T(8,128)(2,1)} %get-tuple-element.28.refs_2_.refs_3_), channel_id=1, source_target_pairs={{0,2},{1,3},{2,4},{3,5},{4,6},{5,7},{6,8},{7,9},{8,10},{9,11},{10,... | collective-permute-start | bytes 835592 | tf_op jit(solution)/shard_map/ppermute | solution.py:253
  6.9 17.9 %collective-permute-start.3 = (bf16[128,1024]{1,0:T(8,128)(2,1)}, bf16[128,1024]{1,0:T(8,128)(2,1)S(1)}, u32[]{:S(2)}, u32[]{:S(2)}) collective-permute-start(bf16[128,1024]{1,0:T(8,128)(2,1)} %get-tuple-element.29.refs_7_.refs_8_), channel_id=1, source_target_pairs={{0,14},{1,15},{2,0},{3,1},{4,2},{5,3},{6,4},{7,5},{8,6},{9,7},{10,... | collective-permute-start | bytes 786440 | tf_op jit(solution)/shard_map/ppermute | solution.py:253
  15.7 14.2 %collective-permute-start.8 = (bf16[128,1024]{1,0:T(8,128)(2,1)}, bf16[128,1024]{1,0:T(8,128)(2,1)S(1)}, u32[]{:S(2)}, u32[]{:S(2)}) collective-permute-start(bf16[128,1024]{1,0:T(8,128)(2,1)} %get-tuple-element.29.refs_7_.refs_8_), channel_id=1, source_target_pairs={{0,2},{1,3},{2,4},{3,5},{4,6},{5,7},{6,8},{7,9},{8,10},{9,11},{10,... | collective-permute-start | bytes 786440 | tf_op jit(solution)/shard_map/ppermute | solution.py:253
  17.6 14.2 %collective-permute-start.6 = (bf16[136,1024]{1,0:T(8,128)(2,1)}, bf16[136,1024]{1,0:T(8,128)(2,1)S(1)}, u32[]{:S(2)}, u32[]{:S(2)}) collective-permute-start(bf16[136,1024]{1,0:T(8,128)(2,1)} %get-tuple-element.28.refs_2_.refs_3_), channel_id=1, source_target_pairs={{0,14},{1,15},{2,0},{3,1},{4,2},{5,3},{6,4},{7,5},{8,6},{9,7},{10,... | collective-permute-start | bytes 835592 | tf_op jit(solution)/shard_map/ppermute | solution.py:253
  22.8 14.2 %collective-permute-start.1 = (bf16[136,1024]{1,0:T(8,128)(2,1)S(1)}, bf16[136,1024]{1,0:T(8,128)(2,1)S(1)}, u32[]{:S(2)}, u32[]{:S(2)}) collective-permute-start(bf16[136,1024]{1,0:T(8,128)(2,1)S(1)} %collective-permute-done.refs_3_.refs_4_), channel_id=1, source_target_pairs={{0,2},{1,3},{2,4},{3,5},{4,6},{5,7},{6,8},{7,9},{8,10},{9,11},{10,... | collective-permute-start | bytes 835592 | tf_op jit(solution)/shard_map/ppermute | solution.py:253
  24.7 14.2 %collective-permute-start.4 = (bf16[128,1024]{1,0:T(8,128)(2,1)S(1)}, bf16[128,1024]{1,0:T(8,128)(2,1)S(1)}, u32[]{:S(2)}, u32[]{:S(2)}) collective-permute-start(bf16[128,1024]{1,0:T(8,128)(2,1)S(1)} %collective-permute-done.3.refs_9_.refs_10_), channel_id=1, source_target_pairs={{0,14},{1,15},{2,0},{3,1},{4,2},{5,3},{6,4},{7,5},{8,6},{9,7},{10,... | collective-permute-start | bytes 786440 | tf_op jit(solution)/shard_map/ppermute | solution.py:253
  29.9 14.2 %collective-permute-start.9 = (bf16[128,1024]{1,0:T(8,128)(2,1)S(1)}, bf16[128,1024]{1,0:T(8,128)(2,1)S(1)}, u32[]{:S(2)}, u32[]{:S(2)}) collective-permute-start(bf16[128,1024]{1,0:T(8,128)(2,1)S(1)} %collective-permute-done.8.refs_8_.refs_9_), channel_id=1, source_target_pairs={{0,2},{1,3},{2,4},{3,5},{4,6},{5,7},{6,8},{7,9},{8,10},{9,11},{10,... | collective-permute-start | bytes 786440 | tf_op jit(solution)/shard_map/ppermute | solution.py:253
  31.8 14.2 %collective-permute-start.7 = (bf16[136,1024]{1,0:T(8,128)(2,1)S(1)}, bf16[136,1024]{1,0:T(8,128)(2,1)S(1)}, u32[]{:S(2)}, u32[]{:S(2)}) collective-permute-start(bf16[136,1024]{1,0:T(8,128)(2,1)S(1)} %collective-permute-done.6.refs_4_.refs_5_), channel_id=1, source_target_pairs={{0,14},{1,15},{2,0},{3,1},{4,2},{5,3},{6,4},{7,5},{8,6},{9,7},{10,... | collective-permute-start | bytes 835592 | tf_op jit(solution)/shard_map/ppermute | solution.py:253
  37.0 16.5 %collective-permute-start.2 = (bf16[136,1024]{1,0:T(8,128)(2,1)S(1)}, bf16[136,1024]{1,0:T(8,128)(2,1)S(1)}, u32[]{:S(2)}, u32[]{:S(2)}) collective-permute-start(bf16[136,1024]{1,0:T(8,128)(2,1)S(1)} %collective-permute-done.1.refs_5_.refs_6_), channel_id=1, source_target_pairs={{0,2},{1,3},{2,4},{3,5},{4,6},{5,7},{6,8},{7,9},{8,10},{9,11},{10,... | collective-permute-start | bytes 835592 | tf_op jit(solution)/shard_map/ppermute | solution.py:253
  38.9 12.2 %collective-permute-start.5 = (bf16[128,1024]{1,0:T(8,128)(2,1)S(1)}, bf16[128,1024]{1,0:T(8,128)(2,1)S(1)}, u32[]{:S(2)}, u32[]{:S(2)}) collective-permute-start(bf16[128,1024]{1,0:T(8,128)(2,1)S(1)} %collective-permute-done.4.refs_11_.refs_12_), channel_id=1, source_target_pairs={{0,14},{1,15},{2,0},{3,1},{4,2},{5,3},{6,4},{7,5},{8,6},{9,7},{10,... | collective-permute-start | bytes 786440 | tf_op jit(solution)/shard_map/ppermute | solution.py:253
  44.1 13.0 %collective-permute-start.12 = (bf16[128,1024]{1,0:T(8,128)(2,1)S(1)}, bf16[128,1024]{1,0:T(8,128)(2,1)S(1)}, u32[]{:S(2)}, u32[]{:S(2)}) collective-permute-start(bf16[128,1024]{1,0:T(8,128)(2,1)S(1)} %collective-permute-done.9.refs_10_.refs_11_), channel_id=1, source_target_pairs={{0,2},{1,3},{2,4},{3,5},{4,6},{5,7},{6,8},{7,9},{8,10},{9,11},{10,... | collective-permute-start | bytes 786440 | tf_op jit(solution)/shard_map/ppermute | solution.py:253
  46.0 19.6 %collective-permute-start.10 = (bf16[136,1024]{1,0:T(8,128)(2,1)S(1)}, bf16[136,1024]{1,0:T(8,128)(2,1)S(1)}, u32[]{:S(2)}, u32[]{:S(2)}) collective-permute-start(bf16[136,1024]{1,0:T(8,128)(2,1)S(1)} %collective-permute-done.7.refs_6_.refs_7_), channel_id=1, source_target_pairs={{0,14},{1,15},{2,0},{3,1},{4,2},{5,3},{6,4},{7,5},{8,6},{9,7},{10,... | collective-permute-start | bytes 835592 | tf_op jit(solution)/shard_map/ppermute | solution.py:253
  51.2 9.1 %collective-permute-start.13 = (bf16[128,1024]{1,0:T(8,128)(2,1)S(1)}, bf16[128,1024]{1,0:T(8,128)(2,1)S(1)}, u32[]{:S(2)}, u32[]{:S(2)}) collective-permute-start(bf16[128,1024]{1,0:T(8,128)(2,1)S(1)} %collective-permute-done.5.refs_1_.refs_5_), channel_id=1, source_target_pairs={{0,14},{1,15},{2,0},{3,1},{4,2},{5,3},{6,4},{7,5},{8,6},{9,7},{10,... | collective-permute-start | bytes 786440 | tf_op jit(solution)/shard_map/ppermute | solution.py:253
  53.5 9.7 %collective-permute-start.11 = (bf16[136,1024]{1,0:T(8,128)(2,1)S(1)}, bf16[136,1024]{1,0:T(8,128)(2,1)S(1)}, u32[]{:S(2)}, u32[]{:S(2)}) collective-permute-start(bf16[136,1024]{1,0:T(8,128)(2,1)S(1)} %collective-permute-done.2.refs_0_.refs_1_), channel_id=1, source_target_pairs={{0,2},{1,3},{2,4},{3,5},{4,6},{5,7},{6,8},{7,9},{8,10},{9,11},{10,... | collective-permute-start | bytes 835592 | tf_op jit(solution)/shard_map/ppermute | solution.py:253
  63.7 4.8 %collective-permute-start.15 = (bf16[2,5,48,1024]{3,2,1,0:T(8,128)(2,1)S(1)}, bf16[2,5,48,1024]{3,2,1,0:T(8,128)(2,1)S(1)}, u32[]{:S(2)}, u32[]{:S(2)}) collective-permute-start(bf16[2,5,48,1024]{3,2,1,0:T(8,128)(2,1)S(1)} %shard_map.100), channel_id=1, source_target_pairs={{0,1},{1,0},{2,3},{3,2},{4,5},{5,4},{6,7},{7,6},{8,9},{9,8},{10,11... | collective-permute-start | bytes 2949128 | tf_op jit(solution)/shard_map/ppermute | solution.py:253
  66.1 5.7 %collective-permute-start.14 = (bf16[2,3,48,1024]{3,2,1,0:T(8,128)(2,1)S(1)}, bf16[2,3,48,1024]{3,2,1,0:T(8,128)(2,1)S(1)}, u32[]{:S(2)}, u32[]{:S(2)}) collective-permute-start(bf16[2,3,48,1024]{3,2,1,0:T(8,128)(2,1)S(1)} %get-tuple-element.32), channel_id=1, source_target_pairs={{0,1},{1,0},{2,3},{3,2},{4,5},{5,4},{6,7},{7,6},{8,9},{9,8},{10,11... | collective-permute-start | bytes 1769480 | tf_op jit(solution)/shard_map/ppermute | solution.py:253
  74.1 18.2 %collective-permute-start.17 = (bf16[8,32,704]{2,1,0:T(8,128)(2,1)S(1)}, bf16[8,32,704]{2,1,0:T(8,128)(2,1)S(1)}, u32[]{:S(2)}, u32[]{:S(2)}) collective-permute-start(bf16[8,32,704]{2,1,0:T(8,128)(2,1)S(1)} %get-tuple-element.46), channel_id=1, source_target_pairs={{0,32},{16,48},{32,0},{48,16},{64,96},{80,112},{96,64},{112,80},{1... | collective-permute-start | bytes 1081352 | tf_op jit(solution)/shard_map/ppermute | solution.py:256
  82.8 42.4 %all-to-all-start = ((bf16[16,48,1024]{2,1,0:T(8,128)(2,1)}), bf16[16,48,1024]{2,1,0:T(8,128)(2,1)S(1)}, u32[]{:S(2)}, u32[]{:S(2)}) async-start(bf16[16,48,1024]{2,1,0:T(8,128)(2,1)} %get-tuple-element.41), calls=%async_computation | async-start | bytes 3145728 | tf_op jit(solution)/shard_map/all_to_all | solution.py:341
  87.4 13.3 %collective-permute-start.16 = (bf16[8,32,704]{2,1,0:T(8,128)(2,1)S(1)}, bf16[8,32,704]{2,1,0:T(8,128)(2,1)S(1)}, u32[]{:S(2)}, u32[]{:S(2)}) collective-permute-start(bf16[8,32,704]{2,1,0:T(8,128)(2,1)S(1)} %get-tuple-element.45), channel_id=1, source_target_pairs={{0,16},{16,0},{32,48},{48,32},{64,80},{80,64},{96,112},{112,96},{1... | collective-permute-start | bytes 1081352 | tf_op jit(solution)/shard_map/ppermute | solution.py:256
  89.9 14.3 %collective-permute-start.18 = (bf16[8,32,704]{2,1,0:T(8,128)(2,1)S(1)}, bf16[8,32,704]{2,1,0:T(8,128)(2,1)S(1)}, u32[]{:S(2)}, u32[]{:S(2)}) collective-permute-start(bf16[8,32,704]{2,1,0:T(8,128)(2,1)S(1)} %get-tuple-element.47), channel_id=1, source_target_pairs={{0,48},{16,32},{32,16},{48,0},{64,112},{80,96},{96,80},{112,64},{1... | collective-permute-start | bytes 1081352 | tf_op jit(solution)/shard_map/ppermute | solution.py:256
  104.3 9.9 %collective-permute-start.19 = (bf16[2,32,704]{2,1,0:T(8,128)(2,1)S(1)}, bf16[2,32,704]{2,1,0:T(8,128)(2,1)S(1)}, u32[]{:S(2)}, u32[]{:S(2)}) collective-permute-start(bf16[2,32,704]{2,1,0:T(8,128)(2,1)S(1)} %get-tuple-element.49), channel_id=1, source_target_pairs={{0,64},{16,80},{32,96},{48,112},{64,128},{80,144},{96,160},{112,17... | collective-permute-start | bytes 270344 | tf_op jit(solution)/shard_map/ppermute | solution.py:256
  109.2 8.6 %collective-permute-start.20 = (bf16[2,32,704]{2,1,0:T(8,128)(2,1)S(1)}, bf16[2,32,704]{2,1,0:T(8,128)(2,1)S(1)}, u32[]{:S(2)}, u32[]{:S(2)}) collective-permute-start(bf16[2,32,704]{2,1,0:T(8,128)(2,1)S(1)} %get-tuple-element.50), channel_id=1, source_target_pairs={{0,128},{16,144},{32,160},{48,176},{64,192},{80,208},{96,224},{112... | collective-permute-start | bytes 270344 | tf_op jit(solution)/shard_map/ppermute | solution.py:256
  111.1 8.3 %collective-permute-start.21 = (bf16[2,32,704]{2,1,0:T(8,128)(2,1)S(1)}, bf16[2,32,704]{2,1,0:T(8,128)(2,1)S(1)}, u32[]{:S(2)}, u32[]{:S(2)}) collective-permute-start(bf16[2,32,704]{2,1,0:T(8,128)(2,1)S(1)} %get-tuple-element.51), channel_id=1, source_target_pairs={{0,192},{16,208},{32,224},{48,240},{64,0},{80,16},{96,32},{112,48}... | collective-permute-start | bytes 270344 | tf_op jit(solution)/shard_map/ppermute | solution.py:256
  119.5 9.9 %collective-permute-start.22 = (bf16[32,704]{1,0:T(8,128)(2,1)S(1)}, bf16[32,704]{1,0:T(8,128)(2,1)S(1)}, u32[]{:S(2)}, u32[]{:S(2)}) collective-permute-start(bf16[32,704]{1,0:T(8,128)(2,1)S(1)} %get-tuple-element.53), channel_id=1, source_target_pairs={{0,256},{16,272},{32,288},{48,304},{64,320},{80,336},{96,352},{112... | collective-permute-start | bytes 135176 | tf_op jit(solution)/shard_map/ppermute | solution.py:256
  (7 other events, 316.9 us)
